TPU v7x, 32 devices: a whole 2x2x4 slice. The times are simulated.
32 devices in a mesh: seq: 16 (over z, x, core), head: 2 (over y).
Axes of the slice: x: 2, y: 2, z: 4, core: 2. Of those that a mesh axis runs over, the one named last changes fastest.
Arguments:
- queries: bfloat16 [4096, 3072], P(('seq', 'head')), may hold values from -6 to 6
- keys: bfloat16 [4096, 3072], P('seq', 'head'), may hold values from -6 to 6
- values: bfloat16 [4096, 3072], P('seq', 'head'), may hold values from -6 to 6
- window: int32 [16, 27], P('seq'), may hold values from -1 to 15, as said below
- out_weight: bfloat16 [3072, 6144], P('seq', 'head'), may hold values from -0.109375 to 0.109375
Outputs:
- projected: bfloat16 [4096, 6144], P('seq', 'head')
Inputs may be any that keep to these rules, and one draw needn't show every extreme that they name: Tile g lies at (g // 16, g // 4 % 4, g % 4) in a grid of 1 x 4 x 4 tiles. Entry k of window[g] is either -1 or the tile that lies (k // 9 - 1, k // 3 % 3 - 1, k % 3 - 1) steps away from g along time, height and width; it is -1 where that tile is outside the grid. Entry 13 is g itself.
All inputs are finite; a program needn't handle non-finite values.
Results may differ from a plain program's by a relative error of at most 0.0075.
Values may be sent and summed in bfloat16 or wider, within the bound.
No kernel may reach another device: no remote copies, remote signals or barrier semaphores. Data moves between devices by JAX's collectives and lax.ppermute only.
A program may use at most 64 MiB of HBM per device.

v0:
```python
import jax
import jax.numpy as jnp
from jax import lax
from jax.sharding import PartitionSpec as P

HEAD_DIM = 128
GH = 4
GW = 4


def passed_along(array, axis, by):
    count = lax.axis_size(axis)
    pairs = [(i, i + by) for i in range(count) if 0 <= i + by < count]
    return lax.ppermute(array, axis, pairs)


def attend_block(softmax_state, queries, kv_block, live_keys):
    run_max, run_sum, run_acc = softmax_state
    factor = queries.shape[-1] ** (-0.5)
    scores = (
        jnp.einsum("qhd,khd->qhk", queries, kv_block[0], preferred_element_type=jnp.float32)
        * factor
    )
    scores = jnp.where(live_keys[None, None, :], scores, -1e30)
    new_max = jnp.maximum(run_max, jnp.max(scores, axis=-1))
    rescale = jnp.exp(run_max - new_max)
    weights = jnp.where(live_keys[None, None, :], jnp.exp(scores - new_max[:, :, None]), 0.0)
    run_sum = run_sum * rescale + jnp.sum(weights, axis=-1)
    run_acc = run_acc * rescale[:, :, None] + jnp.einsum(
        "qhk,khd->qhd",
        weights.astype(jnp.bfloat16),
        kv_block[1],
        preferred_element_type=jnp.float32,
    )
    return (new_max, run_sum, run_acc)


def local(queries, keys, values, window, out_weight):
    tok_rows = queries.shape[0]
    head_width = HEAD_DIM
    heads_all = queries.shape[1] // head_width
    local_q = lax.all_to_all(
        queries.reshape(tok_rows, heads_all, head_width),
        "head",
        split_axis=1,
        concat_axis=0,
        tiled=True,
    )
    tile_rows = local_q.shape[0]
    heads_dev = local_q.shape[1]
    live_tiles = window[0] >= 0
    kv_pair = jnp.stack(
        [
            keys.reshape(tile_rows, heads_dev, head_width),
            values.reshape(tile_rows, heads_dev, head_width),
        ]
    )
    softmax_state = (
        jnp.full((tile_rows, heads_dev), -1e30, jnp.float32),
        jnp.zeros((tile_rows, heads_dev), jnp.float32),
        jnp.zeros((tile_rows, heads_dev, head_width), jnp.float32),
    )
    seq_span = lax.axis_size("seq")
    plane_size = GH * GW

    def tile_mask(first_slot, tile_count):
        return jnp.repeat(live_tiles[first_slot : first_slot + tile_count], tile_rows)

    from_left = passed_along(kv_pair, "seq", 1)
    from_right = passed_along(kv_pair, "seq", -1)
    kv_line = jnp.concatenate([from_left, kv_pair, from_right], axis=1)
    above = passed_along(kv_line, "seq", GW)
    below = passed_along(kv_line, "seq", -GW)
    kv_plane = jnp.concatenate([above, kv_line, below], axis=1)
    line_rows = 3 * tile_rows
    for row_index in (1, 0, 2):
        softmax_state = attend_block(
            softmax_state,
            local_q,
            kv_plane[:, row_index * line_rows : (row_index + 1) * line_rows],
            tile_mask(9 + 3 * row_index, 3),
        )
    if plane_size < seq_span:
        for depth_step in (-1, 1):
            kv_depth = passed_along(kv_plane, "seq", -depth_step * plane_size)
            for row_index in range(3):
                softmax_state = attend_block(
                    softmax_state,
                    local_q,
                    kv_depth[:, row_index * line_rows : (row_index + 1) * line_rows],
                    tile_mask(9 * (depth_step + 1) + 3 * row_index, 3),
                )
    run_max, run_sum, run_acc = softmax_state
    finished = (run_acc / run_sum[:, :, None]).astype(jnp.bfloat16)
    finished = finished.reshape(tile_rows, heads_dev * head_width)
    all_heads = lax.all_gather(finished, "head", axis=1, tiled=True)
    projected = jnp.dot(
        all_heads,
        lax.all_gather(out_weight, "seq", axis=0, tiled=True),
        preferred_element_type=jnp.float32,
    )
    return projected.astype(jnp.bfloat16)


def solution(mesh):
    in_specs = (
        P(("seq", "head"), None),
        P("seq", "head"),
        P("seq", "head"),
        P("seq", None),
        P("seq", "head"),
    )
    out_specs = P("seq", "head")
    return jax.shard_map(local, mesh=mesh, in_specs=in_specs, out_specs=out_specs, check_vma=False)
```

profile of v0, /device:TPU:0, one launch (start us, length us, event | category | flops | bytes accessed | tf_op | source)
XLA Modules:
  0.0 324.8 jit_solution(1052470034834472436)
XLA Ops:
  6.5 0.0 copy-start
  6.5 1.5 copy.24
  8.0 0.4 copy.26
  8.4 0.0 copy-start.1
  8.4 1.4 copy.23
  9.8 0.4 copy.25
  10.2 0.1 pad_maximum_fusion.1
  10.4 1.3 collective-permute-start.1
  11.7 3.1 collective-permute-start
  14.8 0.9 collective-permute-done.1
  15.7 2.1 collective-permute-done
  17.7 2.6 pad_maximum_fusion
  20.3 25.3 %collective-permute-start.2 = (bf16[2,768,12,128]{3,1,2,0:T(8,128)(2,1)}, bf16[2,768,12,128]{3,1,2,0:T(8,128)(2,1)}, u32[]{:S(2)}, u32[]{:S(2)}) collective-permute-start(bf16[2,768,12,128]{3,1,2,0:T(8,128)(2,1)} %pad_maximum_fusion), channel_id=1, source_target_pairs={{0,8},{2,10},{4,12},{6,14},{8,16},{10,18},{12,20},{14,22},{16,24},... | collective-permute-start | bytes 14155784 | tf_op jit(solution)/shard_map/ppermute | solution.py:14
  45.6 1.3 collective-permute-start.3
  46.9 0.0 copy-done
  46.9 1.2 copy.27
  48.0 3.5 %all-to-all-start = ((bf16[128,24,128]{0,2,1:T(8,128)(2,1)}), bf16[128,24,128]{0,2,1:T(8,128)(2,1)S(1)}, u32[]{:S(2)}, u32[]{:S(2)}) async-start(bf16[128,24,128]{0,2,1:T(8,128)(2,1)} %bitcast.4), calls=%async_computation | async-start | bytes 1572864 | tf_op jit(solution)/shard_map/all_to_all | solution.py:42
  51.6 0.2 all-gather.3.cloned.1.call-start
  51.8 0.0 copy-done.1
  51.8 0.1 slice_bitcast_fusion.14
  51.9 0.1 broadcast_in_dim.81
  52.0 0.1 broadcast_in_dim.85
  52.1 0.1 broadcast_in_dim.74
  52.2 7.4 %all-to-all-done = bf16[128,24,128]{0,2,1:T(8,128)(2,1)S(1)} async-done(((bf16[128,24,128]{0,2,1:T(8,128)(2,1)}), bf16[128,24,128]{0,2,1:T(8,128)(2,1)S(1)}, u32[]{:S(2)}, u32[]{:S(2)}) %all-to-all-start) | async-done | bytes 786464 | tf_op jit(solution)/shard_map/all_to_all | solution.py:42
  59.5 0.4 copy.29
  59.9 6.8 %bitcast_reduce_fusion.2 = (f32[256,12]{0,1:T(8,128)S(1)}, f32[12,768,256]{2,1,0:T(8,128)}) fusion(pred[768]{0:T(1024)(128)(4,1)S(1)} %broadcast_in_dim.75, bf16[256,12,128]{2,0,1:T(8,128)(2,1)S(1)} %bitcast.105, bf16[2,768,12,128]{3,1,2,0:T(8,128)(2,1)} %pad_maximum_fusion), kind=kOutput, calls=%fused_computation.9 | convolution fusion | flops 611054592 | bytes 12595968 | tf_op jit(solution)/shard_map/qhd,khd->qhk/dot_general | solution.py:21
  66.7 66.6 %collective-permute-done.2 = bf16[2,768,12,128]{3,1,2,0:T(8,128)(2,1)} collective-permute-done((bf16[2,768,12,128]{3,1,2,0:T(8,128)(2,1)}, bf16[2,768,12,128]{3,1,2,0:T(8,128)(2,1)}, u32[]{:S(2)}, u32[]{:S(2)}) %collective-permute-start.2) | collective-permute-done | bytes 4718624 | tf_op jit(solution)/shard_map/ppermute | solution.py:14
  133.3 3.1 bitcast_reduce_fusion.1
  136.4 3.9 %collective-permute-done.3 = bf16[2,768,12,128]{3,1,2,0:T(8,128)(2,1)} collective-permute-done((bf16[2,768,12,128]{3,1,2,0:T(8,128)(2,1)}, bf16[2,768,12,128]{3,1,2,0:T(8,128)(2,1)}, u32[]{:S(2)}, u32[]{:S(2)}) %collective-permute-start.3) | collective-permute-done | bytes 4718624 | tf_op jit(solution)/shard_map/ppermute | solution.py:14
  140.2 3.1 bitcast_reduce_fusion
  143.3 7.1 %fusion.16 = f32[12,128,256]{2,1,0:T(8,128)S(1)} fusion(f32[12,768,256]{2,1,0:T(8,128)} %get-tuple-element.20, f32[256,12]{0,1:T(8,128)S(1)} %get-tuple-element.11, pred[768]{0:T(1024)(128)(4,1)S(1)} %broadcast_in_dim.75, bf16[2,768,12,128]{3,1,2,0:T(8,128)(2,1)} %pad_maximum_fusion), kind=kOutput, calls=%fused_computation.24 | convolution fusion | flops 615776256 | bytes 13387776 | tf_op jit(solution)/shard_map/qhk,khd->qhd/dot_general | solution.py:29
  150.4 2.7 fusion.10
  153.1 7.4 %fusion.6 = (f32[256,12]{0,1:T(8,128)S(1)}, f32[256,12]{0,1:T(8,128)S(1)}) fusion(f32[12,768,256]{2,1,0:T(8,128)} %get-tuple-element.20, f32[256,12]{0,1:T(8,128)S(1)} %get-tuple-element.11, pred[768]{0:T(1024)(128)(4,1)S(1)} %broadcast_in_dim.75, f32[256,12]{0,1:T(8,128)S(1)} %get-tuple-element.9, f32[12,768,256]{2,1,0:T(8,128)S(1)} %get-tuple-element.18, ...), kind=kLoop, calls=%fused_computation.15 | loop fusion | flops 23586816 | bytes 18925056 | tf_op jit(solution)/shard_map/reduce_sum | solution.py:28
  160.5 4.3 %fusion.14 = f32[12,128,256]{2,1,0:T(8,128)S(1)} fusion(f32[12,768,256]{2,1,0:T(8,128)S(1)} %get-tuple-element.18, f32[256,12]{0,1:T(8,128)S(1)} %get-tuple-element.9, pred[768]{0:T(1024)(128)(4,1)S(1)} %broadcast_in_dim.82, bf16[2,768,12,128]{3,1,2,0:T(8,128)(2,1)} %collective-permute-done.2), kind=kOutput, calls=%fused_computation.23 | convolution fusion | flops 615776256 | bytes 13387776 | tf_op jit(solution)/shard_map/qhk,khd->qhd/dot_general | solution.py:29
  164.9 5.4 %fusion.28 = bf16[256,12,128]{0,2,1:T(8,128)(2,1)} fusion(f32[12,128,256]{2,1,0:T(8,128)S(1)} %fusion.14, f32[12,128,256]{2,1,0:T(8,128)S(1)} %fusion.16, f32[256,12]{0,1:T(8,128)S(1)} %get-tuple-element.5, f32[256,12]{0,1:T(8,128)S(1)} %get-tuple-element.7, f32[256,12]{0,1:T(8,128)S(1)} %get-tuple-element.6, f32[256,12]{0,1:T(8,128)S(1)} %get-tuple-element.10, ...), kind=kOutput, calls=%fused_computation.44 | convolution fusion | flops 618528768 | bytes 15812608 | tf_op jit(solution)/shard_map/qhk,khd->qhd/dot_general | solution.py:29
  170.3 0.0 all-gather.3.cloned.1.call-update
  170.3 0.0 all-gather.5.cloned.1.call-start
  170.4 0.7 all-gather.5.cloned.1.call-update
  171.1 36.0 %all-gather.3.cloned.1.call-done = bf16[256,3072]{0,1:T(8,128)(2,1)} async-done(((bf16[256,1536]{0,1:T(8,128)(2,1)}), bf16[256,3072]{0,1:T(8,128)(2,1)}) %all-gather.3.cloned.1.call-update) | async-done | bytes 1572880 | tf_op jit(solution)/shard_map/all_gather | solution.py:96
  207.1 100.6 %all-gather.5.cloned.1.call-done = bf16[3072,3072]{1,0:T(8,128)(2,1)} async-done(((bf16[192,3072]{1,0:T(8,128)(2,1)}), bf16[3072,3072]{1,0:T(8,128)(2,1)}) %all-gather.5.cloned.1.call-update) | async-done | bytes 18874384 | tf_op jit(solution)/shard_map/all_gather | solution.py:99
  307.6 10.3 %convolution_convert_fusion = bf16[256,3072]{1,0:T(8,128)(2,1)} fusion(bf16[256,3072]{0,1:T(8,128)(2,1)} %all-gather.3.cloned.1.call-done, bf16[3072,3072]{1,0:T(8,128)(2,1)} %all-gather.5.cloned.1.call-done), kind=kOutput, calls=%fused_computation.31 | convolution fusion | flops 4832624640 | bytes 22020096 | tf_op jit(solution)/shard_map/dot_general | solution.py:97
  (6 shorter events, 0.1 us)
Async XLA Ops:
  6.5 40.3 %copy-start = (bf16[128,3072]{1,0:T(8,128)(2,1)S(1)}, bf16[128,3072]{1,0:T(8,128)(2,1)}, u32[]{:S(2)}) copy-start(bf16[128,3072]{1,0:T(8,128)(2,1)} %param.5) | copy-start | bytes 2359300
  8.4 43.4 %copy-start.1 = (s32[1,27]{1,0:T(1,128)S(1)}, s32[1,27]{1,0:T(1,128)}, u32[]{:S(2)}) copy-start(s32[1,27]{1,0:T(1,128)} %param.8) | copy-start | bytes 328
  10.4 5.3 %collective-permute-start.1 = (bf16[2,256,12,128]{3,1,2,0:T(8,128)(2,1)S(1)}, bf16[2,256,12,128]{3,1,2,0:T(8,128)(2,1)S(1)}, u32[]{:S(2)}, u32[]{:S(2)}) collective-permute-start(bf16[2,256,12,128]{3,1,2,0:T(8,128)(2,1)S(1)} %pad_maximum_fusion.1), channel_id=1, source_target_pairs={{2,0},{4,2},{6,4},{8,6},{10,8},{12,10},{14,12},{16,14},{18,16},{20... | collective-permute-start | bytes 4718600 | tf_op jit(solution)/shard_map/ppermute | solution.py:14
  11.7 6.1 %collective-permute-start = (bf16[2,256,12,128]{3,1,2,0:T(8,128)(2,1)S(1)}, bf16[2,256,12,128]{3,1,2,0:T(8,128)(2,1)S(1)}, u32[]{:S(2)}, u32[]{:S(2)}) collective-permute-start(bf16[2,256,12,128]{3,1,2,0:T(8,128)(2,1)S(1)} %pad_maximum_fusion.1), channel_id=1, source_target_pairs={{0,2},{2,4},{4,6},{6,8},{8,10},{10,12},{12,14},{14,16},{16,18},{18... | collective-permute-start | bytes 4718600 | tf_op jit(solution)/shard_map/ppermute | solution.py:14
  20.3 113.0 %collective-permute-start.2 = (bf16[2,768,12,128]{3,1,2,0:T(8,128)(2,1)}, bf16[2,768,12,128]{3,1,2,0:T(8,128)(2,1)}, u32[]{:S(2)}, u32[]{:S(2)}) collective-permute-start(bf16[2,768,12,128]{3,1,2,0:T(8,128)(2,1)} %pad_maximum_fusion), channel_id=1, source_target_pairs={{0,8},{2,10},{4,12},{6,14},{8,16},{10,18},{12,20},{14,22},{16,24},... | collective-permute-start | bytes 14155784 | tf_op jit(solution)/shard_map/ppermute | solution.py:14
  45.6 94.7 %collective-permute-start.3 = (bf16[2,768,12,128]{3,1,2,0:T(8,128)(2,1)}, bf16[2,768,12,128]{3,1,2,0:T(8,128)(2,1)}, u32[]{:S(2)}, u32[]{:S(2)}) collective-permute-start(bf16[2,768,12,128]{3,1,2,0:T(8,128)(2,1)} %pad_maximum_fusion), channel_id=1, source_target_pairs={{8,0},{10,2},{12,4},{14,6},{16,8},{18,10},{20,12},{22,14},{24,16},... | collective-permute-start | bytes 14155784 | tf_op jit(solution)/shard_map/ppermute | solution.py:14
  48.0 11.5 %all-to-all-start = ((bf16[128,24,128]{0,2,1:T(8,128)(2,1)}), bf16[128,24,128]{0,2,1:T(8,128)(2,1)S(1)}, u32[]{:S(2)}, u32[]{:S(2)}) async-start(bf16[128,24,128]{0,2,1:T(8,128)(2,1)} %bitcast.4), calls=%async_computation | async-start | bytes 1572864 | tf_op jit(solution)/shard_map/all_to_all | solution.py:42
  51.6 155.5 %all-gather.3.cloned.1.call-start = ((), (), s32[]{:S(2)}) async-start(), calls=%async_computation.1 | async-start | bytes 2359296 | tf_op jit(solution)/shard_map/all_gather | solution.py:96
  170.3 137.3 %all-gather.5.cloned.1.call-start = ((), (), s32[]{:S(2)}) async-start(), calls=%async_computation.2 | async-start | bytes 20054016 | tf_op jit(solution)/shard_map/all_gather | solution.py:99
Sparse Core Ops, SparseCore 0:
  170.5 36.5 all-gather.2
  208.6 98.9 all-gather.4
where the time goes:
time: 325 us
  waiting for transfers between devices  218 us (67%)
  matrix products  40 us (12%)
  starting transfers between devices  34.8 us (11%)
  between operations  13.6 us (4%)
  other arithmetic  12.8 us (4%)
  local copies, waits for them, and re-layouts  5.53 us (2%)
    all_gather x1, waiting for transfers between devices, local(): lax.all_gather(out_weight, 'seq', axis=0, tiled=True)  101 us
    ppermute x4, waiting for transfers between devices, passed_along(): return lax.ppermute(array, axis, pairs)  73.4 us
    all_gather x1, waiting for transfers between devices, local(): all_heads = lax.all_gather(finished, 'head', axis=1, tiled=True)  36 us
    ppermute x4, starting transfers between devices, passed_along(): return lax.ppermute(array, axis, pairs)  31 us
    dot_general x3, matrix products, attend_block(): jnp.einsum('qhk,khd->qhd', weights.astype(jnp.bfloat16), kv_block[1], pre...  16.9 us
    dot_general x3, matrix products, attend_block(): jnp.einsum('qhd,khd->qhk', queries, kv_block[0], preferred_element_type=j...  12.9 us
    dot_general x1, matrix products, local(): jnp.dot(all_heads, lax.all_gather(out_weight, 'seq', axis=0, tiled=True),...  10.3 us
    reduce_sum x2, other arithmetic, attend_block(): run_sum = run_sum * rescale + jnp.sum(weights, axis=-1)  10.1 us
  transfers between devices with their start and end apart: 7, of which 7 were waited for; matrix products, arithmetic and copies ran while one was open for 4% of the time, Pallas kernels for 0%

commit v1 on v0

--- a/solution.py
+++ b/solution.py
@@ -1,11 +1,17 @@
+import functools
+
 import jax
 import jax.numpy as jnp
 from jax import lax
+from jax.experimental import pallas as pl
+from jax.experimental.pallas import tpu as pltpu
 from jax.sharding import PartitionSpec as P
 
 HEAD_DIM = 128
 GH = 4
 GW = 4
+LOG2E = 1.4426950408889634
+DEAD = -1e30
 
 
 def passed_along(array, axis, by):
@@ -35,7 +41,7 @@
     return (new_max, run_sum, run_acc)
 
 
-def local(queries, keys, values, window, out_weight):
+def local_general(queries, keys, values, window, out_weight):
     tok_rows = queries.shape[0]
     head_width = HEAD_DIM
     heads_all = queries.shape[1] // head_width
@@ -102,7 +108,156 @@
     return projected.astype(jnp.bfloat16)
 
 
+def attend_kernel(tile, win, q_ref, own_ref, up_ref, dn_ref, o_ref, vt_ref):
+    coef = q_ref.shape[1] ** -0.5 * LOG2E
+    refs = (up_ref, own_ref, dn_ref)
+    for r in range(3):
+        for c in range(GW):
+            vt_ref[r, :, c * tile : (c + 1) * tile] = refs[r][(2 * c + 1) * tile : (2 * c + 2) * tile, :].T
+    for c in range(GW):
+        q = q_ref[c * tile : (c + 1) * tile, :]
+        lo, hi = max(c - 1, 0), min(c + 2, GW)
+        top = total = acc = None
+        for r in (1, 0, 2):
+            scores, lives = [], []
+            new = top
+            for k in range(lo, hi):
+                keys = refs[r][2 * k * tile : (2 * k + 1) * tile, :]
+                s = lax.dot_general(keys, q, (((1,), (1,)), ((), ())), preferred_element_type=jnp.float32)
+                live = win[c, 9 + 3 * r + k - c + 1] >= 0
+                scores.append(s)
+                lives.append(live)
+                high = jnp.where(live, jnp.max(s, axis=0, keepdims=True), DEAD)
+                new = high if new is None else jnp.maximum(new, high)
+            weights, part = [], None
+            for s, live in zip(scores, lives):
+                w = jnp.exp2((s - jnp.where(live, new, -DEAD)) * coef)
+                w_sum = jnp.sum(w, axis=0, keepdims=True)
+                part = w_sum if part is None else part + w_sum
+                weights.append(w.astype(jnp.bfloat16))
+            pv = jnp.dot(
+                vt_ref[r, :, lo * tile : hi * tile],
+                jnp.concatenate(weights, axis=0),
+                preferred_element_type=jnp.float32,
+            )
+            if top is None:
+                total, acc = part, pv
+            else:
+                again = jnp.exp2((top - new) * coef)
+                total = total * again + part
+                acc = acc * again + pv
+            top = new
+        o_ref[c * tile : (c + 1) * tile, :] = (acc / total).astype(jnp.bfloat16).T
+
+
+def attend_line(win, q, own, up, dn):
+    rows, width = q.shape
+    tile = rows // GW
+    units = 3 * (3 * GW - 2)
+    return pl.pallas_call(
+        functools.partial(attend_kernel, tile),
+        out_shape=jax.ShapeDtypeStruct(q.shape, jnp.bfloat16),
+        in_specs=[pl.BlockSpec(memory_space=pltpu.SMEM)] + [pl.BlockSpec(memory_space=pltpu.VMEM)] * 4,
+        out_specs=pl.BlockSpec(memory_space=pltpu.VMEM),
+        scratch_shapes=[pltpu.VMEM((3, width, rows), jnp.bfloat16)],
+        compiler_params=pltpu.CompilerParams(vmem_limit_bytes=40 * 2**20),
+        cost_estimate=pl.CostEstimate(
+            flops=units * 4 * tile * tile * width,
+            bytes_accessed=16 * rows * width,
+            transcendentals=units * tile * tile,
+        ),
+    )(win, q, own, up, dn)
+
+
+def project_kernel(steps, width, place, *refs):
+    pieces, w_ref, o_ref = refs[:-2], refs[-2], refs[-1]
+    acc = None
+    for i in range(0, len(pieces), 2):
+        left = jnp.concatenate([pieces[i][...], pieces[i + 1][...]], axis=1)
+        right = jnp.concatenate(
+            [w_ref[pl.ds(pl.multiple_of(place[i + j], width), width), :] for j in (0, 1)], axis=0
+        )
+        d = jnp.dot(left, right, preferred_element_type=jnp.float32)
+        acc = d if acc is None else acc + d
+    o_ref[...] = acc.astype(jnp.bfloat16)
+
+
+def project(place, pieces, w):
+    rows, width = pieces[0].shape
+    step = rows // GW
+    return pl.pallas_call(
+        functools.partial(project_kernel, GW, width),
+        out_shape=jax.ShapeDtypeStruct((rows, w.shape[1]), jnp.bfloat16),
+        grid_spec=pltpu.PrefetchScalarGridSpec(
+            num_scalar_prefetch=1,
+            grid=(GW,),
+            in_specs=[pl.BlockSpec((step, width), lambda i, place: (i, 0))] * len(pieces)
+            + [pl.BlockSpec(w.shape, lambda i, place: (0, 0))],
+            out_specs=pl.BlockSpec((step, w.shape[1]), lambda i, place: (i, 0)),
+        ),
+        compiler_params=pltpu.CompilerParams(vmem_limit_bytes=40 * 2**20),
+        cost_estimate=pl.CostEstimate(
+            flops=2 * rows * w.shape[0] * w.shape[1],
+            bytes_accessed=2 * (rows * w.shape[0] + w.shape[0] * w.shape[1] + rows * w.shape[1]),
+            transcendentals=0,
+        ),
+    )(place, *pieces, w)
+
+
+def local_plane(queries, keys, values, window, out_weight):
+    span = lax.axis_size("seq")
+    lines = [[r + c for c in range(GW)] for r in range(0, span, GW)]
+    columns = [[r + c for r in range(0, span, GW)] for c in range(GW)]
+    down = [(i, i + GW) for i in range(span - GW)]
+    up = [(i + GW, i) for i in range(span - GW)]
+    own_width = keys.shape[1]
+    width = HEAD_DIM
+    steps = own_width // (GW * width)
+    part = GW * width
+    chunks = out_weight.shape[1] // (GW * 256)
+    cut = out_weight.shape[1] // chunks
+
+    def over_line(array, split, concat):
+        return lax.all_to_all(array, "seq", split, concat, axis_index_groups=lines, tiled=True)
+
+    def swap(array, by):
+        return lax.ppermute(array, "seq", [(i, i ^ by) for i in range(span)])
+
+    win = lax.all_gather(window, "seq", axis=0, tiled=True, axis_index_groups=lines)
+    w_own = [over_line(out_weight[:, n * cut : (n + 1) * cut], 1, 0) for n in range(chunks)]
+    w_all = [lax.all_gather(w, "seq", axis=0, tiled=True, axis_index_groups=columns) for w in w_own]
+
+    q = lax.all_to_all(queries, "head", 1, 0, tiled=True)
+    pieces, homes = [], []
+    for h in range(steps):
+        cols = slice(h * part, (h + 1) * part)
+        kv = over_line(jnp.concatenate([keys[:, cols], values[:, cols]], axis=0), 1, 0)
+        kv_up = lax.ppermute(kv, "seq", down)
+        kv_dn = lax.ppermute(kv, "seq", up)
+        mine = attend_line(win, over_line(q[:, cols], 1, 0), kv, kv_up, kv_dn)
+        held = [(mine, 0, 0), (lax.ppermute(mine, "head", [(0, 1), (1, 0)]), 1, 0)]
+        held += [(swap(a, 2), y, c + 2) for a, y, c in held]
+        held += [(swap(a, 1), y, c + 1) for a, y, c in held]
+        pieces += [a for a, _, _ in held]
+        homes += [(y, c, h) for _, y, c in held]
+
+    y_own = lax.axis_index("head")
+    c_own = lax.axis_index("seq") % GW
+    homes = jnp.asarray(homes, jnp.int32)
+    place = (homes[:, 0] ^ y_own) * own_width + homes[:, 2] * part + (homes[:, 1] ^ c_own) * width
+    outs = [over_line(project(place, pieces, w), 0, 1) for w in w_all]
+    return jnp.concatenate(outs, axis=1)
+
+
 def solution(mesh):
+    span, sides = mesh.shape["seq"], mesh.shape["head"]
+
+    def local(queries, keys, values, window, out_weight):
+        one_step = span == GH * GW and sides == 2
+        even = keys.shape[1] % (GW * HEAD_DIM) == 0 and out_weight.shape[1] % (GW * 256) == 0
+        which = local_plane if one_step and even else local_general
+        return which(queries, keys, values, window, out_weight)
+
     in_specs = (
         P(("seq", "head"), None),
         P("seq", "head"),

time: 325 us -> 255 us (0.78)
  waiting for transfers between devices: 218 us -> 77 us
  matrix products: 40 us -> 0 us
  starting transfers between devices: 34.8 us -> 65.2 us
  Pallas kernels: 0 us -> 30.4 us
  blocking collectives: 0 us -> 29.1 us
  local copies, waits for them, and re-layouts: 5.53 us -> 32.8 us
  other arithmetic: 12.8 us -> 3.95 us
    all_gather x2 -> x3, waiting for transfers between devices: 137 us -> 0.04 us  [local_plane(): lax.all_gather(w, 'seq', axis=0, tiled=True, axis_index_groups=columns)]
    ppermute x4 -> x27, waiting for transfers between devices: 73.4 us -> 32.5 us  [the longest x18 27.2 us: swap(): return lax.ppermute(array, 'seq', [(i, i ^ by) for i in range(span)])]
    dot_general x7 -> x0, matrix products: 40 us -> none  [the longest x3 16.9 us: attend_block(): jnp.einsum('qhk,khd->qhd', weights.astype(jnp.bfloat16), kv_block[1], pre...]
    all_to_all x1 -> x11, starting transfers between devices: 3.54 us -> 40 us  [the longest x10 36.5 us: over_line(): lax.all_to_all(array, 'seq', split, concat, axis_index_groups=lines, tile...]
    all_to_all x1 -> x11, waiting for transfers between devices: 7.36 us -> 43.8 us  [the longest x10 33.5 us: over_line(): lax.all_to_all(array, 'seq', split, concat, axis_index_groups=lines, tile...]
    pallas_call x0 -> x6, Pallas kernels: none -> 30.4 us  [the longest x3 17.1 us: attend_line(): pl.pallas_call(functools.partial(attend_kernel, tile), out_shape=jax.Shap...]
    all_to_all x0 -> x2, blocking collectives: none -> 22.2 us  [over_line(): lax.all_to_all(array, 'seq', split, concat, axis_index_groups=lines, tile...]
    unnamed x7 -> x61, local copies, waits for them, and re-layouts: 4.05 us -> 22 us
  transfers between devices with their start and end apart: 7 -> 41, of which waited for: 7 -> 16; matrix products, arithmetic and copies ran while one was open for 4% -> 5% of each run, Pallas kernels for 0% -> 12%
where the time goes in v1:
time: 255 us; the launch traced here: 252 us
  waiting for transfers between devices  77 us (30%)
  starting transfers between devices  65.2 us (26%)
  local copies, waits for them, and re-layouts  32.8 us (13%)
  Pallas kernels  30.4 us (12%)
  blocking collectives  29.1 us (11%)
  between operations  13.6 us (5%)
  other arithmetic  3.95 us (2%)
    all_to_all x10, starting transfers between devices, over_line(): lax.all_to_all(array, 'seq', split, concat, axis_index_groups=lines, tile...  36.5 us
    all_to_all x10, waiting for transfers between devices, over_line(): lax.all_to_all(array, 'seq', split, concat, axis_index_groups=lines, tile...  33.5 us
    ppermute x18, waiting for transfers between devices, swap(): return lax.ppermute(array, 'seq', [(i, i ^ by) for i in range(span)])  27.2 us
    all_to_all x2, blocking collectives, over_line(): lax.all_to_all(array, 'seq', split, concat, axis_index_groups=lines, tile...  22.2 us
    unnamed x61, local copies, waits for them, and re-layouts  22 us
    pallas_call x3, Pallas kernels, attend_line(): pl.pallas_call(functools.partial(attend_kernel, tile), out_shape=jax.Shap...  17.1 us
    pallas_call x3, Pallas kernels, project(): pl.pallas_call(functools.partial(project_kernel, GW, width), out_shape=ja...  13.2 us
    ppermute x3, starting transfers between devices, local_plane(): kv_up = lax.ppermute(kv, 'seq', down)  12.4 us
  transfers between devices with their start and end apart: 41, of which 16 were waited for; matrix products, arithmetic and copies ran while one was open for 5% of the time, Pallas kernels for 12%

profile of v1, /device:TPU:0, one launch (start us, length us, event | category | flops | bytes accessed | tf_op | source)
XLA Modules:
  0.0 252.1 jit_solution(14711926244076834365)
XLA Ops:
  6.5 1.3 fusion
  7.9 11.6 %all_to_all.247 = bf16[192,4,256]{2,0,1:T(8,128)(2,1)} all-to-all(bf16[192,4,256]{2,0,1:T(8,128)(2,1)S(1)} %bitcast.103), channel_id=1, replica_groups={{0,2,4,6},{8,10,12,14},{16,18,20,22},{24,26,28,30},{1,3,5,7},{9,11,13,1..., dimensions={1} | all-to-all | bytes 786432 | tf_op jit(solution)/shard_map/all_to_all | solution.py:221
  19.6 10.6 %all_to_all.248 = bf16[192,4,256]{2,0,1:T(8,128)(2,1)} all-to-all(bf16[192,4,256]{2,0,1:T(8,128)(2,1)S(1)} %bitcast.104), channel_id=1, replica_groups={{0,2,4,6},{8,10,12,14},{16,18,20,22},{24,26,28,30},{1,3,5,7},{9,11,13,1..., dimensions={1} | all-to-all | bytes 786432 | tf_op jit(solution)/shard_map/all_to_all | solution.py:221
  31.0 3.5 %all-to-all-start.11 = ((bf16[192,4,256]{2,0,1:T(8,128)(2,1)}), bf16[192,4,256]{2,0,1:T(8,128)(2,1)S(1)}, u32[]{:S(2)}, u32[]{:S(2)}) async-start(bf16[192,4,256]{2,0,1:T(8,128)(2,1)} %bitcast.70), calls=%async_computation.11 | async-start | bytes 786432 | tf_op jit(solution)/shard_map/all_to_all | solution.py:221
  35.6 6.3 %all-to-all-done.11 = bf16[192,4,256]{2,0,1:T(8,128)(2,1)S(1)} async-done(((bf16[192,4,256]{2,0,1:T(8,128)(2,1)}), bf16[192,4,256]{2,0,1:T(8,128)(2,1)S(1)}, u32[]{:S(2)}, u32[]{:S(2)}) %all-to-all-start.11) | async-done | bytes 393248 | tf_op jit(solution)/shard_map/all_to_all | solution.py:221
  41.9 3.5 %all-to-all-start.6 = ((bf16[512,4,128]{2,0,1:T(8,128)(2,1)}), bf16[512,4,128]{2,0,1:T(8,128)(2,1)S(1)}, u32[]{:S(2)}, u32[]{:S(2)}) async-start(bf16[512,4,128]{2,0,1:T(8,128)(2,1)} %copy_bitcast_fusion), calls=%async_computation.6 | async-start | bytes 1048576 | tf_op jit(solution)/shard_map/all_to_all | solution.py:221
  45.4 1.2 copy.48
  46.5 7.6 %all-to-all-done.6 = bf16[512,4,128]{2,0,1:T(8,128)(2,1)S(1)} async-done(((bf16[512,4,128]{2,0,1:T(8,128)(2,1)}), bf16[512,4,128]{2,0,1:T(8,128)(2,1)S(1)}, u32[]{:S(2)}, u32[]{:S(2)}) %all-to-all-start.6) | async-done | bytes 524320 | tf_op jit(solution)/shard_map/all_to_all | solution.py:221
  54.2 3.5 %all-to-all-start = ((bf16[128,2,1536]{0,2,1:T(8,128)(2,1)}), bf16[128,2,1536]{0,2,1:T(8,128)(2,1)S(1)}, u32[]{:S(2)}, u32[]{:S(2)}) async-start(bf16[128,2,1536]{0,2,1:T(8,128)(2,1)} %bitcast.3), calls=%async_computation | async-start | bytes 1572864 | tf_op jit(solution)/shard_map/all_to_all | solution.py:230
  58.6 10.2 %all-to-all-done = bf16[128,2,1536]{0,2,1:T(8,128)(2,1)S(1)} async-done(((bf16[128,2,1536]{0,2,1:T(8,128)(2,1)}), bf16[128,2,1536]{0,2,1:T(8,128)(2,1)S(1)}, u32[]{:S(2)}, u32[]{:S(2)}) %all-to-all-start) | async-done | bytes 786464 | tf_op jit(solution)/shard_map/all_to_all | solution.py:230
  68.9 3.5 %all-to-all-start.4 = ((bf16[512,4,128]{2,0,1:T(8,128)(2,1)}), bf16[512,4,128]{2,0,1:T(8,128)(2,1)S(1)}, u32[]{:S(2)}, u32[]{:S(2)}) async-start(bf16[512,4,128]{2,0,1:T(8,128)(2,1)} %copy_bitcast_fusion.1), calls=%async_computation.4 | async-start | bytes 1048576 | tf_op jit(solution)/shard_map/all_to_all | solution.py:221
  73.3 7.9 %all-to-all-done.4 = bf16[512,4,128]{2,0,1:T(8,128)(2,1)S(1)} async-done(((bf16[512,4,128]{2,0,1:T(8,128)(2,1)}), bf16[512,4,128]{2,0,1:T(8,128)(2,1)S(1)}, u32[]{:S(2)}, u32[]{:S(2)}) %all-to-all-start.4) | async-done | bytes 524320 | tf_op jit(solution)/shard_map/all_to_all | solution.py:221
  81.2 3.5 %all-to-all-start.2 = ((bf16[512,4,128]{2,0,1:T(8,128)(2,1)}), bf16[512,4,128]{2,0,1:T(8,128)(2,1)S(1)}, u32[]{:S(2)}, u32[]{:S(2)}) async-start(bf16[512,4,128]{2,0,1:T(8,128)(2,1)} %copy_bitcast_fusion.2), calls=%async_computation.2 | async-start | bytes 1048576 | tf_op jit(solution)/shard_map/all_to_all | solution.py:221
  84.7 3.7 %collective-permute-start.18 = (bf16[2048,128]{1,0:T(8,128)(2,1)S(1)}, bf16[2048,128]{1,0:T(8,128)(2,1)S(1)}, u32[]{:S(2)}, u32[]{:S(2)}) collective-permute-start(bf16[2048,128]{1,0:T(8,128)(2,1)S(1)} %bitcast.79), channel_id=1, source_target_pairs={{0,8},{2,10},{4,12},{6,14},{8,16},{10,18},{12,20},{14,22},{16,24},... | collective-permute-start | bytes 1572872 | tf_op jit(solution)/shard_map/ppermute | solution.py:235
  88.4 1.3 collective-permute-start.19
  89.7 1.2 copy.49
  90.9 1.2 fusion.3
  93.5 3.4 %all-to-all-start.5 = ((bf16[256,4,128]{0,2,1:T(8,128)(2,1)}), bf16[256,4,128]{0,2,1:T(8,128)(2,1)S(1)}, u32[]{:S(2)}, u32[]{:S(2)}) async-start(bf16[256,4,128]{0,2,1:T(8,128)(2,1)} %bitcast.18), calls=%async_computation.5 | async-start | bytes 524288 | tf_op jit(solution)/shard_map/all_to_all | solution.py:221
  96.9 1.3 collective-permute-start.10
  98.2 5.5 %collective-permute-start.9 = (bf16[2048,128]{1,0:T(8,128)(2,1)S(1)}, bf16[2048,128]{1,0:T(8,128)(2,1)}, u32[]{:S(2)}, u32[]{:S(2)}) collective-permute-start(bf16[2048,128]{1,0:T(8,128)(2,1)S(1)} %bitcast.83), channel_id=1, source_target_pairs={{0,8},{2,10},{4,12},{6,14},{8,16},{10,18},{12,20},{14,22},{16,24},... | collective-permute-start | bytes 1572872 | tf_op jit(solution)/shard_map/ppermute | solution.py:235
  103.7 3.2 %collective-permute-start = (bf16[2048,128]{1,0:T(8,128)(2,1)S(1)}, bf16[2048,128]{1,0:T(8,128)(2,1)S(1)}, u32[]{:S(2)}, u32[]{:S(2)}) collective-permute-start(bf16[2048,128]{1,0:T(8,128)(2,1)S(1)} %bitcast.76), channel_id=1, source_target_pairs={{0,8},{2,10},{4,12},{6,14},{8,16},{10,18},{12,20},{14,22},{16,24},... | collective-permute-start | bytes 1572872 | tf_op jit(solution)/shard_map/ppermute | solution.py:235
  106.9 1.3 collective-permute-start.1
  109.0 3.4 %all-to-all-start.3 = ((bf16[256,4,128]{0,2,1:T(8,128)(2,1)}), bf16[256,4,128]{0,2,1:T(8,128)(2,1)S(1)}, u32[]{:S(2)}, u32[]{:S(2)}) async-start(bf16[256,4,128]{0,2,1:T(8,128)(2,1)} %bitcast.12), calls=%async_computation.3 | async-start | bytes 524288 | tf_op jit(solution)/shard_map/all_to_all | solution.py:221
  114.0 4.4 %all-to-all-done.3 = bf16[256,4,128]{0,2,1:T(8,128)(2,1)S(1)} async-done(((bf16[256,4,128]{0,2,1:T(8,128)(2,1)}), bf16[256,4,128]{0,2,1:T(8,128)(2,1)S(1)}, u32[]{:S(2)}, u32[]{:S(2)}) %all-to-all-start.3) | async-done | bytes 262176 | tf_op jit(solution)/shard_map/all_to_all | solution.py:221
  118.4 4.0 %all-to-all-start.1 = ((bf16[256,4,128]{0,2,1:T(8,128)(2,1)}), bf16[256,4,128]{0,2,1:T(8,128)(2,1)}, u32[]{:S(2)}, u32[]{:S(2)}) async-start(bf16[256,4,128]{0,2,1:T(8,128)(2,1)} %bitcast.6), calls=%async_computation.1 | async-start | bytes 524288 | tf_op jit(solution)/shard_map/all_to_all | solution.py:221
  122.5 6.9 %all-gather = s32[4,1,27]{2,1,0:T(1,128)S(1)} all-gather(s32[1,1,27]{2,1,0:T(1,128)S(1)} %bitcast.107), channel_id=1, replica_groups={{0,2,4,6},{8,10,12,14},{16,18,20,22},{24,26,28,30},{1,3,5,7},{9,11,13,1..., dimensions={0}, use_global_device_ids=true | all-gather | bytes 540 | tf_op jit(solution)/shard_map/all_gather | solution.py:226
  129.6 5.7 %shard_map.66.refs_16_ = bf16[1024,128]{1,0:T(8,128)(2,1)S(1)} custom-call(s32[4,27]{1,0:T(4,128)S(1)} %bitcast.88, bf16[1024,128]{1,0:T(8,128)(2,1)S(1)} %bitcast.87, bf16[2048,128]{1,0:T(8,128)(2,1)S(1)} %bitcast.81, bf16[2048,128]{1,0:T(8,128)(2,1)S(1)} %collective-permute-done.18.up_ref, bf16[2048,128]{1,0:T(8,128)(2,1)} %collective-permute-done.19.dn_ref), custom_call_target="tpu_custom_call" | custom-call | flops 1006632960 | bytes 2097152 | tf_op jit(solution)/shard_map/pallas_call | solution.py:157
  135.8 1.1 copy.51
  137.0 5.8 %shard_map.65.refs_8_ = bf16[1024,128]{1,0:T(8,128)(2,1)S(1)} custom-call(s32[4,27]{1,0:T(4,128)S(1)} %bitcast.89, bf16[1024,128]{1,0:T(8,128)(2,1)S(1)} %bitcast.86, bf16[2048,128]{1,0:T(8,128)(2,1)S(1)} %bitcast.84, bf16[2048,128]{1,0:T(8,128)(2,1)} %collective-permute-done.9.up_ref, bf16[2048,128]{1,0:T(8,128)(2,1)} %collective-permute-done.10.dn_ref), custom_call_target="tpu_custom_call" | custom-call | flops 1006632960 | bytes 2097152 | tf_op jit(solution)/shard_map/pallas_call | solution.py:157
  142.8 1.8 collective-permute-start.11
  144.6 5.7 %shard_map.64.refs_0_ = bf16[1024,128]{1,0:T(8,128)(2,1)S(1)} custom-call(s32[4,27]{1,0:T(4,128)S(1)} %bitcast.90, bf16[1024,128]{1,0:T(8,128)(2,1)S(1)} %bitcast.85, bf16[2048,128]{1,0:T(8,128)(2,1)S(1)} %bitcast.78, bf16[2048,128]{1,0:T(8,128)(2,1)S(1)} %collective-permute-done.up_ref, bf16[2048,128]{1,0:T(8,128)(2,1)} %collective-permute-done.1.dn_ref), custom_call_target="tpu_custom_call" | custom-call | flops 1006632960 | bytes 2097152 | tf_op jit(solution)/shard_map/pallas_call | solution.py:157
  151.0 1.7 collective-permute-start.12
  153.0 5.3 %collective-permute-done.2.refs_1_ = bf16[1024,128]{1,0:T(8,128)(2,1)S(1)} collective-permute-done((bf16[1024,128]{1,0:T(8,128)(2,1)S(1)}, bf16[1024,128]{1,0:T(8,128)(2,1)S(1)}, u32[]{:S(2)}, u32[]{:S(2)}) %collective-permute-start.2) | collective-permute-done | bytes 262176 | tf_op jit(solution)/shard_map/ppermute | solution.py:238
  158.3 1.6 collective-permute-done.21.refs_18_
  159.9 5.6 %collective-permute-done.12.refs_10_ = bf16[1024,128]{1,0:T(8,128)(2,1)S(1)} collective-permute-done((bf16[1024,128]{1,0:T(8,128)(2,1)S(1)}, bf16[1024,128]{1,0:T(8,128)(2,1)S(1)}, u32[]{:S(2)}, u32[]{:S(2)}) %collective-permute-start.12) | collective-permute-done | bytes 262176 | tf_op jit(solution)/shard_map/ppermute | solution.py:224
  165.8 5.3 %collective-permute-done.3.refs_2_ = bf16[1024,128]{1,0:T(8,128)(2,1)S(1)} collective-permute-done((bf16[1024,128]{1,0:T(8,128)(2,1)S(1)}, bf16[1024,128]{1,0:T(8,128)(2,1)S(1)}, u32[]{:S(2)}, u32[]{:S(2)}) %collective-permute-start.3) | collective-permute-done | bytes 262176 | tf_op jit(solution)/shard_map/ppermute | solution.py:224
  171.5 1.7 collective-permute-start.4
  173.7 3.1 %collective-permute-done.22.refs_19_ = bf16[1024,128]{1,0:T(8,128)(2,1)S(1)} collective-permute-done((bf16[1024,128]{1,0:T(8,128)(2,1)S(1)}, bf16[1024,128]{1,0:T(8,128)(2,1)S(1)}, u32[]{:S(2)}, u32[]{:S(2)}) %collective-permute-start.22) | collective-permute-done | bytes 262176 | tf_op jit(solution)/shard_map/ppermute | solution.py:224
  176.7 5.7 %collective-permute-done.13.refs_11_ = bf16[1024,128]{1,0:T(8,128)(2,1)} collective-permute-done((bf16[1024,128]{1,0:T(8,128)(2,1)S(1)}, bf16[1024,128]{1,0:T(8,128)(2,1)}, u32[]{:S(2)}, u32[]{:S(2)}) %collective-permute-start.13) | collective-permute-done | bytes 262176 | tf_op jit(solution)/shard_map/ppermute | solution.py:224
  182.5 4.1 %collective-permute-done.4.refs_3_ = bf16[1024,128]{1,0:T(8,128)(2,1)} collective-permute-done((bf16[1024,128]{1,0:T(8,128)(2,1)S(1)}, bf16[1024,128]{1,0:T(8,128)(2,1)}, u32[]{:S(2)}, u32[]{:S(2)}) %collective-permute-start.4) | collective-permute-done | bytes 262176 | tf_op jit(solution)/shard_map/ppermute | solution.py:224
  191.2 1.1 collective-permute-done.8.refs_7_
  192.3 0.9 copy-done.1
  193.3 0.9 copy-done.5
  194.2 0.9 copy-done.9
  195.2 0.9 copy-done.13
  196.1 1.4 copy-done.19
  197.5 4.4 %shard_map.67 = bf16[1024,256]{1,0:T(8,128)(2,1)S(1)} custom-call(s32[24]{0:T(128)S(1)} %add_bitcast_fusion.place, bf16[1024,128]{1,0:T(8,128)(2,1)S(1)} %shard_map.64.refs_0_, bf16[1024,128]{1,0:T(8,128)(2,1)S(1)} %collective-permute-done.2.refs_1_, bf16[1024,128]{1,0:T(8,128)(2,1)S(1)} %collective-permute-done.3.refs_2_, ...), custom_call_target="tpu_custom_call" | custom-call | flops 1610612736 | bytes 8388608 | tf_op jit(solution)/shard_map/pallas_call | solution.py:188
  202.7 4.2 %all-to-all-start.8 = ((bf16[4,256,256]{2,1,0:T(8,128)(2,1)}), bf16[4,256,256]{2,1,0:T(8,128)(2,1)}, u32[]{:S(2)}, u32[]{:S(2)}) async-start(bf16[4,256,256]{2,1,0:T(8,128)(2,1)} %bitcast.75), calls=%async_computation.8 | async-start | bytes 1048576 | tf_op jit(solution)/shard_map/all_to_all | solution.py:221
  207.9 0.9 copy-done.6
  208.8 0.9 copy-done.10
  209.8 0.9 copy-done.14
  210.7 1.4 copy-done.20
  212.1 4.4 %shard_map.68 = bf16[1024,256]{1,0:T(8,128)(2,1)S(1)} custom-call(s32[24]{0:T(128)S(1)} %add_bitcast_fusion.place, bf16[1024,128]{1,0:T(8,128)(2,1)S(1)} %shard_map.64.refs_0_, bf16[1024,128]{1,0:T(8,128)(2,1)S(1)} %collective-permute-done.2.refs_1_, bf16[1024,128]{1,0:T(8,128)(2,1)S(1)} %collective-permute-done.3.refs_2_, ...), custom_call_target="tpu_custom_call" | custom-call | flops 1610612736 | bytes 8388608 | tf_op jit(solution)/shard_map/pallas_call | solution.py:188
  217.3 4.1 %all-to-all-start.10 = ((bf16[4,256,256]{2,1,0:T(8,128)(2,1)}), bf16[4,256,256]{2,1,0:T(8,128)(2,1)}, u32[]{:S(2)}, u32[]{:S(2)}) async-start(bf16[4,256,256]{2,1,0:T(8,128)(2,1)} %bitcast.73), calls=%async_computation.10 | async-start | bytes 1048576 | tf_op jit(solution)/shard_map/all_to_all | solution.py:221
  222.5 0.9 copy-done.7
  223.4 0.9 copy-done.11
  224.4 0.9 copy-done.15
  225.3 1.4 copy-done.21
  226.7 4.4 %shard_map.69 = bf16[1024,256]{1,0:T(8,128)(2,1)S(1)} custom-call(s32[24]{0:T(128)S(1)} %add_bitcast_fusion.place, bf16[1024,128]{1,0:T(8,128)(2,1)S(1)} %shard_map.64.refs_0_, bf16[1024,128]{1,0:T(8,128)(2,1)S(1)} %collective-permute-done.2.refs_1_, bf16[1024,128]{1,0:T(8,128)(2,1)S(1)} %collective-permute-done.3.refs_2_, ...), custom_call_target="tpu_custom_call" | custom-call | flops 1610612736 | bytes 8388608 | tf_op jit(solution)/shard_map/pallas_call | solution.py:188
  231.9 3.5 %all-to-all-start.12 = ((bf16[4,256,256]{2,1,0:T(8,128)(2,1)}), bf16[4,256,256]{2,1,0:T(8,128)(2,1)S(1)}, u32[]{:S(2)}, u32[]{:S(2)}) async-start(bf16[4,256,256]{2,1,0:T(8,128)(2,1)} %bitcast.74), calls=%async_computation.12 | async-start | bytes 1048576 | tf_op jit(solution)/shard_map/all_to_all | solution.py:221
  235.4 1.1 copy.71
  236.5 1.1 copy.72
  237.6 6.6 %all-to-all-done.12 = bf16[4,256,256]{2,1,0:T(8,128)(2,1)S(1)} async-done(((bf16[4,256,256]{2,1,0:T(8,128)(2,1)}), bf16[4,256,256]{2,1,0:T(8,128)(2,1)S(1)}, u32[]{:S(2)}, u32[]{:S(2)}) %all-to-all-start.12) | async-done | bytes 524320 | tf_op jit(solution)/shard_map/all_to_all | solution.py:221
  244.3 1.2 pad_maximum_fusion
  (112 shorter events, 19.5 us)
Async XLA Ops:
  6.5 185.8 %all-gather.5.cloned.1.call-start = ((), (), s32[]{:S(2)}) async-start(), calls=%async_computation.13 | async-start | bytes 1966080 | tf_op jit(solution)/shard_map/all_gather | solution.py:228
  19.5 187.4 %all-gather.7.cloned.1.call-start = ((), (), s32[]{:S(2)}) async-start(), calls=%async_computation.14 | async-start | bytes 1966080 | tf_op jit(solution)/shard_map/all_gather | solution.py:228
  19.6 14.9 %copy-start.24 = (bf16[256,1536]{1,0:T(8,128)(2,1)S(1)}, bf16[256,1536]{1,0:T(8,128)(2,1)}, u32[]{:S(2)}) copy-start(bf16[256,1536]{1,0:T(8,128)(2,1)} %param.7) | copy-start | bytes 2359300
  19.6 14.9 %copy-start.25 = (bf16[256,1536]{1,0:T(8,128)(2,1)S(1)}, bf16[256,1536]{1,0:T(8,128)(2,1)}, u32[]{:S(2)}) copy-start(bf16[256,1536]{1,0:T(8,128)(2,1)} %param.8) | copy-start | bytes 2359300
  31.0 10.9 %all-to-all-start.11 = ((bf16[192,4,256]{2,0,1:T(8,128)(2,1)}), bf16[192,4,256]{2,0,1:T(8,128)(2,1)S(1)}, u32[]{:S(2)}, u32[]{:S(2)}) async-start(bf16[192,4,256]{2,0,1:T(8,128)(2,1)} %bitcast.70), calls=%async_computation.11 | async-start | bytes 786432 | tf_op jit(solution)/shard_map/all_to_all | solution.py:221
  34.7 10.7 %copy-start.23 = (bf16[128,3072]{1,0:T(8,128)(2,1)S(1)}, bf16[128,3072]{1,0:T(8,128)(2,1)}, u32[]{:S(2)}) copy-start(bf16[128,3072]{1,0:T(8,128)(2,1)} %param.6) | copy-start | bytes 2359300
  41.9 12.3 %copy-start.22 = (bf16[192,4,256]{2,0,1:T(8,128)(2,1)}, bf16[192,4,256]{2,0,1:T(8,128)(2,1)S(1)}, u32[]{:S(2)}) copy-start(bf16[192,4,256]{2,0,1:T(8,128)(2,1)S(1)} %all-to-all-done.11) | copy-start | bytes 1179652
  41.9 12.3 %all-to-all-start.6 = ((bf16[512,4,128]{2,0,1:T(8,128)(2,1)}), bf16[512,4,128]{2,0,1:T(8,128)(2,1)S(1)}, u32[]{:S(2)}, u32[]{:S(2)}) async-start(bf16[512,4,128]{2,0,1:T(8,128)(2,1)} %copy_bitcast_fusion), calls=%async_computation.6 | async-start | bytes 1048576 | tf_op jit(solution)/shard_map/all_to_all | solution.py:221
  54.2 14.7 %all-to-all-start = ((bf16[128,2,1536]{0,2,1:T(8,128)(2,1)}), bf16[128,2,1536]{0,2,1:T(8,128)(2,1)S(1)}, u32[]{:S(2)}, u32[]{:S(2)}) async-start(bf16[128,2,1536]{0,2,1:T(8,128)(2,1)} %bitcast.3), calls=%async_computation | async-start | bytes 1572864 | tf_op jit(solution)/shard_map/all_to_all | solution.py:230
  68.9 12.3 %all-to-all-start.4 = ((bf16[512,4,128]{2,0,1:T(8,128)(2,1)}), bf16[512,4,128]{2,0,1:T(8,128)(2,1)S(1)}, u32[]{:S(2)}, u32[]{:S(2)}) async-start(bf16[512,4,128]{2,0,1:T(8,128)(2,1)} %copy_bitcast_fusion.1), calls=%async_computation.4 | async-start | bytes 1048576 | tf_op jit(solution)/shard_map/all_to_all | solution.py:221
  81.2 12.3 %all-to-all-start.2 = ((bf16[512,4,128]{2,0,1:T(8,128)(2,1)}), bf16[512,4,128]{2,0,1:T(8,128)(2,1)S(1)}, u32[]{:S(2)}, u32[]{:S(2)}) async-start(bf16[512,4,128]{2,0,1:T(8,128)(2,1)} %copy_bitcast_fusion.2), calls=%async_computation.2 | async-start | bytes 1048576 | tf_op jit(solution)/shard_map/all_to_all | solution.py:221
  84.7 22.2 %collective-permute-start.18 = (bf16[2048,128]{1,0:T(8,128)(2,1)S(1)}, bf16[2048,128]{1,0:T(8,128)(2,1)S(1)}, u32[]{:S(2)}, u32[]{:S(2)}) collective-permute-start(bf16[2048,128]{1,0:T(8,128)(2,1)S(1)} %bitcast.79), channel_id=1, source_target_pairs={{0,8},{2,10},{4,12},{6,14},{8,16},{10,18},{12,20},{14,22},{16,24},... | collective-permute-start | bytes 1572872 | tf_op jit(solution)/shard_map/ppermute | solution.py:235
  88.4 41.2 %collective-permute-start.19 = (bf16[2048,128]{1,0:T(8,128)(2,1)S(1)}, bf16[2048,128]{1,0:T(8,128)(2,1)}, u32[]{:S(2)}, u32[]{:S(2)}) collective-permute-start(bf16[2048,128]{1,0:T(8,128)(2,1)S(1)} %bitcast.80), channel_id=1, source_target_pairs={{8,0},{10,2},{12,4},{14,6},{16,8},{18,10},{20,12},{22,14},{24,16},... | collective-permute-start | bytes 1572872 | tf_op jit(solution)/shard_map/ppermute | solution.py:236
  92.9 29.6 %copy-start.26 = (s32[1,27]{1,0:T(1,128)S(1)}, s32[1,27]{1,0:T(1,128)}, u32[]{:S(2)}) copy-start(s32[1,27]{1,0:T(1,128)} %param.9) | copy-start | bytes 328
  93.5 15.6 %all-to-all-start.5 = ((bf16[256,4,128]{0,2,1:T(8,128)(2,1)}), bf16[256,4,128]{0,2,1:T(8,128)(2,1)S(1)}, u32[]{:S(2)}, u32[]{:S(2)}) async-start(bf16[256,4,128]{0,2,1:T(8,128)(2,1)} %bitcast.18), calls=%async_computation.5 | async-start | bytes 524288 | tf_op jit(solution)/shard_map/all_to_all | solution.py:221
  96.9 40.1 %collective-permute-start.10 = (bf16[2048,128]{1,0:T(8,128)(2,1)S(1)}, bf16[2048,128]{1,0:T(8,128)(2,1)}, u32[]{:S(2)}, u32[]{:S(2)}) collective-permute-start(bf16[2048,128]{1,0:T(8,128)(2,1)S(1)} %bitcast.82), channel_id=1, source_target_pairs={{8,0},{10,2},{12,4},{14,6},{16,8},{18,10},{20,12},{22,14},{24,16},... | collective-permute-start | bytes 1572872 | tf_op jit(solution)/shard_map/ppermute | solution.py:236
  98.2 38.8 %collective-permute-start.9 = (bf16[2048,128]{1,0:T(8,128)(2,1)S(1)}, bf16[2048,128]{1,0:T(8,128)(2,1)}, u32[]{:S(2)}, u32[]{:S(2)}) collective-permute-start(bf16[2048,128]{1,0:T(8,128)(2,1)S(1)} %bitcast.83), channel_id=1, source_target_pairs={{0,8},{2,10},{4,12},{6,14},{8,16},{10,18},{12,20},{14,22},{16,24},... | collective-permute-start | bytes 1572872 | tf_op jit(solution)/shard_map/ppermute | solution.py:235
  103.7 40.9 %collective-permute-start = (bf16[2048,128]{1,0:T(8,128)(2,1)S(1)}, bf16[2048,128]{1,0:T(8,128)(2,1)S(1)}, u32[]{:S(2)}, u32[]{:S(2)}) collective-permute-start(bf16[2048,128]{1,0:T(8,128)(2,1)S(1)} %bitcast.76), channel_id=1, source_target_pairs={{0,8},{2,10},{4,12},{6,14},{8,16},{10,18},{12,20},{14,22},{16,24},... | collective-permute-start | bytes 1572872 | tf_op jit(solution)/shard_map/ppermute | solution.py:235
  106.9 37.7 %collective-permute-start.1 = (bf16[2048,128]{1,0:T(8,128)(2,1)S(1)}, bf16[2048,128]{1,0:T(8,128)(2,1)}, u32[]{:S(2)}, u32[]{:S(2)}) collective-permute-start(bf16[2048,128]{1,0:T(8,128)(2,1)S(1)} %bitcast.77), channel_id=1, source_target_pairs={{8,0},{10,2},{12,4},{14,6},{16,8},{18,10},{20,12},{22,14},{24,16},... | collective-permute-start | bytes 1572872 | tf_op jit(solution)/shard_map/ppermute | solution.py:236
  109.0 9.4 %all-to-all-start.3 = ((bf16[256,4,128]{0,2,1:T(8,128)(2,1)}), bf16[256,4,128]{0,2,1:T(8,128)(2,1)S(1)}, u32[]{:S(2)}, u32[]{:S(2)}) async-start(bf16[256,4,128]{0,2,1:T(8,128)(2,1)} %bitcast.12), calls=%async_computation.3 | async-start | bytes 524288 | tf_op jit(solution)/shard_map/all_to_all | solution.py:221
  112.4 109.1 %all-gather.9.cloned.1.call-start = ((), (), s32[]{:S(2)}) async-start(), calls=%async_computation.15 | async-start | bytes 1966080 | tf_op jit(solution)/shard_map/all_gather | solution.py:228
  118.4 17.4 %all-to-all-start.1 = ((bf16[256,4,128]{0,2,1:T(8,128)(2,1)}), bf16[256,4,128]{0,2,1:T(8,128)(2,1)}, u32[]{:S(2)}, u32[]{:S(2)}) async-start(bf16[256,4,128]{0,2,1:T(8,128)(2,1)} %bitcast.6), calls=%async_computation.1 | async-start | bytes 524288 | tf_op jit(solution)/shard_map/all_to_all | solution.py:221
  135.3 17.4 %collective-permute-start.20 = (bf16[1024,128]{1,0:T(8,128)(2,1)S(1)}, bf16[1024,128]{1,0:T(8,128)(2,1)S(1)}, u32[]{:S(2)}, u32[]{:S(2)}) collective-permute-start(bf16[1024,128]{1,0:T(8,128)(2,1)S(1)} %shard_map.66.refs_16_), channel_id=1, source_target_pairs={{0,1},{1,0},{2,3},{3,2},{4,5},{5,4},{6,7},{7,6},{8,9},{9,8},{10,11... | collective-permute-start | bytes 786440 | tf_op jit(solution)/shard_map/ppermute | solution.py:238
  142.8 10.3 %collective-permute-start.11 = (bf16[1024,128]{1,0:T(8,128)(2,1)S(1)}, bf16[1024,128]{1,0:T(8,128)(2,1)S(1)}, u32[]{:S(2)}, u32[]{:S(2)}) collective-permute-start(bf16[1024,128]{1,0:T(8,128)(2,1)S(1)} %shard_map.65.refs_8_), channel_id=1, source_target_pairs={{0,1},{1,0},{2,3},{3,2},{4,5},{5,4},{6,7},{7,6},{8,9},{9,8},{10,11... | collective-permute-start | bytes 786440 | tf_op jit(solution)/shard_map/ppermute | solution.py:238
  144.6 45.9 %copy-start.27 = (s32[24,1]{0,1:T(1,128)S(1)}, s32[24,1]{0,1:T(1,128)}, u32[]{:S(2)}) copy-start(s32[24,1]{0,1:T(1,128)} %constant.31) | copy-start | bytes 292
  144.6 45.8 %copy-start.28 = (s32[24,1]{0,1:T(1,128)S(1)}, s32[24,1]{0,1:T(1,128)}, u32[]{:S(2)}) copy-start(s32[24,1]{0,1:T(1,128)} %constant.33) | copy-start | bytes 292
  144.6 45.8 %copy-start.29 = (s32[24,1]{0,1:T(1,128)S(1)}, s32[24,1]{0,1:T(1,128)}, u32[]{:S(2)}) copy-start(s32[24,1]{0,1:T(1,128)} %constant.34) | copy-start | bytes 292
  150.3 8.0 %collective-permute-start.2 = (bf16[1024,128]{1,0:T(8,128)(2,1)S(1)}, bf16[1024,128]{1,0:T(8,128)(2,1)S(1)}, u32[]{:S(2)}, u32[]{:S(2)}) collective-permute-start(bf16[1024,128]{1,0:T(8,128)(2,1)S(1)} %shard_map.64.refs_0_), channel_id=1, source_target_pairs={{0,1},{1,0},{2,3},{3,2},{4,5},{5,4},{6,7},{7,6},{8,9},{9,8},{10,11... | collective-permute-start | bytes 786440 | tf_op jit(solution)/shard_map/ppermute | solution.py:238
  150.6 9.2 %collective-permute-start.21 = (bf16[1024,128]{1,0:T(8,128)(2,1)S(1)}, bf16[1024,128]{1,0:T(8,128)(2,1)S(1)}, u32[]{:S(2)}, u32[]{:S(2)}) collective-permute-start(bf16[1024,128]{1,0:T(8,128)(2,1)S(1)} %shard_map.66.refs_16_), channel_id=1, source_target_pairs={{0,4},{2,6},{4,0},{6,2},{8,12},{10,14},{12,8},{14,10},{16,20},{18,... | collective-permute-start | bytes 786440 | tf_op jit(solution)/shard_map/ppermute | solution.py:224
  151.0 14.5 %collective-permute-start.12 = (bf16[1024,128]{1,0:T(8,128)(2,1)S(1)}, bf16[1024,128]{1,0:T(8,128)(2,1)S(1)}, u32[]{:S(2)}, u32[]{:S(2)}) collective-permute-start(bf16[1024,128]{1,0:T(8,128)(2,1)S(1)} %shard_map.65.refs_8_), channel_id=1, source_target_pairs={{0,4},{2,6},{4,0},{6,2},{8,12},{10,14},{12,8},{14,10},{16,20},{18,... | collective-permute-start | bytes 786440 | tf_op jit(solution)/shard_map/ppermute | solution.py:224
  152.7 18.4 %collective-permute-start.3 = (bf16[1024,128]{1,0:T(8,128)(2,1)S(1)}, bf16[1024,128]{1,0:T(8,128)(2,1)S(1)}, u32[]{:S(2)}, u32[]{:S(2)}) collective-permute-start(bf16[1024,128]{1,0:T(8,128)(2,1)S(1)} %shard_map.64.refs_0_), channel_id=1, source_target_pairs={{0,4},{2,6},{4,0},{6,2},{8,12},{10,14},{12,8},{14,10},{16,20},{18,... | collective-permute-start | bytes 786440 | tf_op jit(solution)/shard_map/ppermute | solution.py:224
  153.0 18.4 %collective-permute-start.23 = (bf16[1024,128]{1,0:T(8,128)(2,1)S(1)}, bf16[1024,128]{1,0:T(8,128)(2,1)S(1)}, u32[]{:S(2)}, u32[]{:S(2)}) collective-permute-start(bf16[1024,128]{1,0:T(8,128)(2,1)S(1)} %shard_map.66.refs_16_), channel_id=1, source_target_pairs={{0,2},{2,0},{4,6},{6,4},{8,10},{10,8},{12,14},{14,12},{16,18},{18,... | collective-permute-start | bytes 786440 | tf_op jit(solution)/shard_map/ppermute | solution.py:224
  158.3 14.8 %collective-permute-start.14 = (bf16[1024,128]{1,0:T(8,128)(2,1)S(1)}, bf16[1024,128]{1,0:T(8,128)(2,1)S(1)}, u32[]{:S(2)}, u32[]{:S(2)}) collective-permute-start(bf16[1024,128]{1,0:T(8,128)(2,1)S(1)} %shard_map.65.refs_8_), channel_id=1, source_target_pairs={{0,2},{2,0},{4,6},{6,4},{8,10},{10,8},{12,14},{14,12},{16,18},{18,... | collective-permute-start | bytes 786440 | tf_op jit(solution)/shard_map/ppermute | solution.py:224
  159.9 13.3 %collective-permute-start.5 = (bf16[1024,128]{1,0:T(8,128)(2,1)S(1)}, bf16[1024,128]{1,0:T(8,128)(2,1)S(1)}, u32[]{:S(2)}, u32[]{:S(2)}) collective-permute-start(bf16[1024,128]{1,0:T(8,128)(2,1)S(1)} %shard_map.64.refs_0_), channel_id=1, source_target_pairs={{0,2},{2,0},{4,6},{6,4},{8,10},{10,8},{12,14},{14,12},{16,18},{18,... | collective-permute-start | bytes 786440 | tf_op jit(solution)/shard_map/ppermute | solution.py:224
  165.5 11.2 %collective-permute-start.22 = (bf16[1024,128]{1,0:T(8,128)(2,1)S(1)}, bf16[1024,128]{1,0:T(8,128)(2,1)S(1)}, u32[]{:S(2)}, u32[]{:S(2)}) collective-permute-start(bf16[1024,128]{1,0:T(8,128)(2,1)S(1)} %collective-permute-done.20.refs_17_), channel_id=1, source_target_pairs={{0,4},{2,6},{4,0},{6,2},{8,12},{10,14},{12,8},{14,10},{16,20},{18,... | collective-permute-start | bytes 786440 | tf_op jit(solution)/shard_map/ppermute | solution.py:224
  171.1 11.3 %collective-permute-start.13 = (bf16[1024,128]{1,0:T(8,128)(2,1)S(1)}, bf16[1024,128]{1,0:T(8,128)(2,1)}, u32[]{:S(2)}, u32[]{:S(2)}) collective-permute-start(bf16[1024,128]{1,0:T(8,128)(2,1)S(1)} %collective-permute-done.11.refs_9_), channel_id=1, source_target_pairs={{0,4},{2,6},{4,0},{6,2},{8,12},{10,14},{12,8},{14,10},{16,20},{18,... | collective-permute-start | bytes 786440 | tf_op jit(solution)/shard_map/ppermute | solution.py:224
  171.5 15.1 %collective-permute-start.4 = (bf16[1024,128]{1,0:T(8,128)(2,1)S(1)}, bf16[1024,128]{1,0:T(8,128)(2,1)}, u32[]{:S(2)}, u32[]{:S(2)}) collective-permute-start(bf16[1024,128]{1,0:T(8,128)(2,1)S(1)} %collective-permute-done.2.refs_1_), channel_id=1, source_target_pairs={{0,4},{2,6},{4,0},{6,2},{8,12},{10,14},{12,8},{14,10},{16,20},{18,... | collective-permute-start | bytes 786440 | tf_op jit(solution)/shard_map/ppermute | solution.py:224
  173.1 13.4 %collective-permute-start.24 = (bf16[1024,128]{1,0:T(8,128)(2,1)S(1)}, bf16[1024,128]{1,0:T(8,128)(2,1)S(1)}, u32[]{:S(2)}, u32[]{:S(2)}) collective-permute-start(bf16[1024,128]{1,0:T(8,128)(2,1)S(1)} %collective-permute-done.20.refs_17_), channel_id=1, source_target_pairs={{0,2},{2,0},{4,6},{6,4},{8,10},{10,8},{12,14},{14,12},{16,18},{18,... | collective-permute-start | bytes 786440 | tf_op jit(solution)/shard_map/ppermute | solution.py:224
  173.2 14.6 %collective-permute-start.15 = (bf16[1024,128]{1,0:T(8,128)(2,1)S(1)}, bf16[1024,128]{1,0:T(8,128)(2,1)S(1)}, u32[]{:S(2)}, u32[]{:S(2)}) collective-permute-start(bf16[1024,128]{1,0:T(8,128)(2,1)S(1)} %collective-permute-done.11.refs_9_), channel_id=1, source_target_pairs={{0,2},{2,0},{4,6},{6,4},{8,10},{10,8},{12,14},{14,12},{16,18},{18,... | collective-permute-start | bytes 786440 | tf_op jit(solution)/shard_map/ppermute | solution.py:224
  176.7 11.8 %collective-permute-start.6 = (bf16[1024,128]{1,0:T(8,128)(2,1)S(1)}, bf16[1024,128]{1,0:T(8,128)(2,1)S(1)}, u32[]{:S(2)}, u32[]{:S(2)}) collective-permute-start(bf16[1024,128]{1,0:T(8,128)(2,1)S(1)} %collective-permute-done.2.refs_1_), channel_id=1, source_target_pairs={{0,2},{2,0},{4,6},{6,4},{8,10},{10,8},{12,14},{14,12},{16,18},{18,... | collective-permute-start | bytes 786440 | tf_op jit(solution)/shard_map/ppermute | solution.py:224
  182.5 7.3 %collective-permute-start.25 = (bf16[1024,128]{1,0:T(8,128)(2,1)S(1)}, bf16[1024,128]{1,0:T(8,128)(2,1)S(1)}, u32[]{:S(2)}, u32[]{:S(2)}) collective-permute-start(bf16[1024,128]{1,0:T(8,128)(2,1)S(1)} %collective-permute-done.21.refs_18_), channel_id=1, source_target_pairs={{0,2},{2,0},{4,6},{6,4},{8,10},{10,8},{12,14},{14,12},{16,18},{18,... | collective-permute-start | bytes 786440 | tf_op jit(solution)/shard_map/ppermute | solution.py:224
  186.6 3.9 %collective-permute-start.16 = (bf16[1024,128]{1,0:T(8,128)(2,1)S(1)}, bf16[1024,128]{1,0:T(8,128)(2,1)}, u32[]{:S(2)}, u32[]{:S(2)}) collective-permute-start(bf16[1024,128]{1,0:T(8,128)(2,1)S(1)} %collective-permute-done.12.refs_10_), channel_id=1, source_target_pairs={{0,2},{2,0},{4,6},{6,4},{8,10},{10,8},{12,14},{14,12},{16,18},{18,... | collective-permute-start | bytes 786440 | tf_op jit(solution)/shard_map/ppermute | solution.py:224
  187.3 3.2 %collective-permute-start.7 = (bf16[1024,128]{1,0:T(8,128)(2,1)S(1)}, bf16[1024,128]{1,0:T(8,128)(2,1)}, u32[]{:S(2)}, u32[]{:S(2)}) collective-permute-start(bf16[1024,128]{1,0:T(8,128)(2,1)S(1)} %collective-permute-done.3.refs_2_), channel_id=1, source_target_pairs={{0,2},{2,0},{4,6},{6,4},{8,10},{10,8},{12,14},{14,12},{16,18},{18,... | collective-permute-start | bytes 786440 | tf_op jit(solution)/shard_map/ppermute | solution.py:224
  188.5 2.0 collective-permute-start.26
  189.2 2.0 collective-permute-start.17
  190.4 1.9 collective-permute-start.8
  192.3 1.0 copy-start.1
  193.3 0.9 copy-start.5
  194.2 0.9 copy-start.9
  195.2 0.9 copy-start.13
  196.1 1.4 copy-start.19
  202.7 14.6 %all-to-all-start.8 = ((bf16[4,256,256]{2,1,0:T(8,128)(2,1)}), bf16[4,256,256]{2,1,0:T(8,128)(2,1)}, u32[]{:S(2)}, u32[]{:S(2)}) async-start(bf16[4,256,256]{2,1,0:T(8,128)(2,1)} %bitcast.75), calls=%async_computation.8 | async-start | bytes 1048576 | tf_op jit(solution)/shard_map/all_to_all | solution.py:221
  206.9 1.0 copy-start.2
  207.9 0.9 copy-start.6
  208.8 0.9 copy-start.10
  209.8 0.9 copy-start.14
  210.7 1.4 copy-start.20
  217.3 14.6 %all-to-all-start.10 = ((bf16[4,256,256]{2,1,0:T(8,128)(2,1)}), bf16[4,256,256]{2,1,0:T(8,128)(2,1)}, u32[]{:S(2)}, u32[]{:S(2)}) async-start(bf16[4,256,256]{2,1,0:T(8,128)(2,1)} %bitcast.73), calls=%async_computation.10 | async-start | bytes 1048576 | tf_op jit(solution)/shard_map/all_to_all | solution.py:221
  221.5 1.0 copy-start.3
  222.5 0.9 copy-start.7
  223.4 0.9 copy-start.11
  224.4 0.9 copy-start.15
  225.3 1.4 copy-start.21
  231.9 12.3 %all-to-all-start.12 = ((bf16[4,256,256]{2,1,0:T(8,128)(2,1)}), bf16[4,256,256]{2,1,0:T(8,128)(2,1)S(1)}, u32[]{:S(2)}, u32[]{:S(2)}) async-start(bf16[4,256,256]{2,1,0:T(8,128)(2,1)} %bitcast.74), calls=%async_computation.12 | async-start | bytes 1048576 | tf_op jit(solution)/shard_map/all_to_all | solution.py:221
  (7 other events, 5.2 us)
Sparse Core Ops, SparseCore 0:
  19.6 37.8 all-gather.4
  59.0 36.2 all-gather.6
  114.8 39.4 all-gather.8

commit v2 on v0

--- a/solution.py
+++ b/solution.py
@@ -1,11 +1,17 @@
+import functools
+
 import jax
 import jax.numpy as jnp
 from jax import lax
+from jax.experimental import pallas as pl
+from jax.experimental.pallas import tpu as pltpu
 from jax.sharding import PartitionSpec as P
 
 HEAD_DIM = 128
 GH = 4
 GW = 4
+LOG2E = 1.4426950408889634
+DEAD = -1e30
 
 
 def passed_along(array, axis, by):
@@ -35,7 +41,7 @@
     return (new_max, run_sum, run_acc)
 
 
-def local(queries, keys, values, window, out_weight):
+def local_general(queries, keys, values, window, out_weight):
     tok_rows = queries.shape[0]
     head_width = HEAD_DIM
     heads_all = queries.shape[1] // head_width
@@ -102,7 +108,113 @@
     return projected.astype(jnp.bfloat16)
 
 
+VMEM_LIMIT = 56 * 2**20
+
+
+def attend_kernel(listed, q_ref, *refs):
+    tiles, o_ref = refs[:9], refs[9]
+    tile, width = q_ref.shape
+    coef = width**-0.5 * LOG2E
+    toward = 1 - 2 * (listed[27] & 1)
+    q = q_ref[...]
+    top = total = acc = None
+    for r in (1, 0, 2):
+        scores, lives = [], []
+        new = top
+        for k, step in enumerate((0, toward, -toward)):
+            s = lax.dot_general(
+                tiles[3 * r + k][:tile, :], q, (((1,), (1,)), ((), ())), preferred_element_type=jnp.float32
+            )
+            live = listed[10 + 3 * r + step] >= 0
+            scores.append(s)
+            lives.append(live)
+            high = jnp.where(live, jnp.max(s, axis=0, keepdims=True), DEAD)
+            new = high if new is None else jnp.maximum(new, high)
+        weights, part = [], None
+        for s, live in zip(scores, lives):
+            w = jnp.exp2((s - jnp.where(live, new, -DEAD)) * coef)
+            w_sum = jnp.sum(w, axis=0, keepdims=True)
+            part = w_sum if part is None else part + w_sum
+            weights.append(w.astype(jnp.bfloat16))
+        values = jnp.concatenate([tiles[3 * r + k][tile:, :].T for k in range(3)], axis=1)
+        pv = jnp.dot(values, jnp.concatenate(weights, axis=0), preferred_element_type=jnp.float32)
+        if top is None:
+            total, acc = part, pv
+        else:
+            again = jnp.exp2((top - new) * coef)
+            total = total * again + part
+            acc = acc * again + pv
+        top = new
+    o_ref[...] = (acc / total).astype(jnp.bfloat16).T
+
+
+def attend_tile(listed, q, first, tiles):
+    rows = q.shape[0]
+    heads = tiles[0].shape[1] // HEAD_DIM
+    return pl.pallas_call(
+        attend_kernel,
+        out_shape=jax.ShapeDtypeStruct((rows, heads * HEAD_DIM), jnp.bfloat16),
+        grid_spec=pltpu.PrefetchScalarGridSpec(
+            num_scalar_prefetch=1,
+            grid=(heads,),
+            in_specs=[pl.BlockSpec((rows, HEAD_DIM), lambda h, listed: (0, first + h))]
+            + [pl.BlockSpec((2 * rows, HEAD_DIM), lambda h, listed: (0, h))] * len(tiles),
+            out_specs=pl.BlockSpec((rows, HEAD_DIM), lambda h, listed: (0, h)),
+        ),
+        compiler_params=pltpu.CompilerParams(vmem_limit_bytes=VMEM_LIMIT),
+        cost_estimate=pl.CostEstimate(
+            flops=heads * 36 * rows * rows * HEAD_DIM,
+            bytes_accessed=40 * heads * rows * HEAD_DIM,
+            transcendentals=heads * 9 * rows * rows,
+        ),
+    )(listed, q, *tiles)
+
+
+def local_plane(queries, keys, values, window, out_weight):
+    span = lax.axis_size("seq")
+    down = [(i, i + GW) for i in range(span - GW)]
+    up = [(i + GW, i) for i in range(span - GW)]
+    mates = [(i, i ^ 1) for i in range(span)]
+    outer = [(i, i ^ 3) for i in range(span) if i % GW in (1, 2)]
+    side = lax.axis_index("head")
+
+    def move(array, pairs):
+        return lax.ppermute(array, "seq", pairs)
+
+    parts = 1
+    wide = out_weight.shape[1] // parts
+    w_all = [
+        lax.all_gather(out_weight[:, n * wide : (n + 1) * wide], "seq", axis=0, tiled=True) for n in range(parts)
+    ]
+
+    chunk = keys.shape[1] // 2
+    listed = jnp.concatenate([window[0], lax.axis_index("seq")[None]])
+    held = []
+    for at in (0, chunk):
+        kv = jnp.concatenate([keys[:, at : at + chunk], values[:, at : at + chunk]], axis=0)
+        kv_out = move(kv, outer)
+        kv_up, kv_dn = move(kv, down), move(kv, up)
+        out_up = move(kv_out, [p for p in down if p[0] % GW in (1, 2)])
+        out_dn = move(kv_out, [p for p in up if p[0] % GW in (1, 2)])
+        held.append([kv_up, move(kv_up, mates), out_up, kv, move(kv, mates), kv_out, kv_dn, move(kv_dn, mates), out_dn])
+
+    q = lax.all_to_all(queries, "head", 1, 0, tiled=True)
+    mine = [attend_tile(listed, q, n * chunk // HEAD_DIM, tiles) for n, tiles in enumerate(held)]
+    other = [lax.ppermute(a, "head", [(0, 1), (1, 0)]) for a in mine]
+    attended = jnp.where(side == 0, jnp.concatenate(mine + other, axis=1), jnp.concatenate(other + mine, axis=1))
+    made = [jnp.dot(attended, w, preferred_element_type=jnp.float32).astype(jnp.bfloat16) for w in w_all]
+    return jnp.concatenate(made, axis=1)
+
+
 def solution(mesh):
+    span, sides = mesh.shape["seq"], mesh.shape["head"]
+
+    def local(queries, keys, values, window, out_weight):
+        one_step = span == GH * GW and sides == 2
+        even = keys.shape[1] % (2 * HEAD_DIM) == 0
+        which = local_plane if one_step and even else local_general
+        return which(queries, keys, values, window, out_weight)
+
     in_specs = (
         P(("seq", "head"), None),
         P("seq", "head"),

time: 325 us -> 191 us (0.59)
  waiting for transfers between devices: 218 us -> 75 us
  matrix products: 40 us -> 12.8 us
  starting transfers between devices: 34.8 us -> 59.9 us
  Pallas kernels: 0 us -> 23.8 us
  other arithmetic: 12.8 us -> 0.77 us
    all_gather x2 -> x1, waiting for transfers between devices: 137 us -> 0.01 us  [local_plane(): lax.all_gather(out_weight[:, n * wide:(n + 1) * wide], 'seq', axis=0, til...]
    dot_general x7 -> x1, matrix products: 40 us -> 12.8 us  [local_plane(): jnp.dot(attended, w, preferred_element_type=jnp.float32)]
    ppermute x4 -> x18, starting transfers between devices: 31 us -> 56.4 us  [the longest x16 54.3 us: move(): return lax.ppermute(array, 'seq', pairs)]
    pallas_call x0 -> x2, Pallas kernels: none -> 23.8 us  [attend_tile(): pl.pallas_call(attend_kernel, out_shape=jax.ShapeDtypeStruct((rows, heads...]
    reduce_sum x2 -> x0, other arithmetic: 10.1 us -> none  [attend_block(): run_sum = run_sum * rescale + jnp.sum(weights, axis=-1)]
    ppermute x4 -> x18, waiting for transfers between devices: 73.4 us -> 63.5 us  [the longest x16 54.5 us: move(): return lax.ppermute(array, 'seq', pairs)]
    all_to_all x1, waiting for transfers between devices: 7.36 us -> 10.7 us  [local_plane(): q = lax.all_to_all(queries, 'head', 1, 0, tiled=True)]
  transfers between devices with their start and end apart: 7 -> 20, of which waited for: 7 -> 5; matrix products, arithmetic and copies ran while one was open for 4% -> 2% of each run, Pallas kernels for 0% -> 13%
where the time goes in v2:
time: 191 us; the launch traced here: 190 us
  waiting for transfers between devices  75 us (39%)
  starting transfers between devices  59.9 us (31%)
  Pallas kernels  23.8 us (12%)
  between operations  13.6 us (7%)
  matrix products  12.8 us (7%)
  local copies, waits for them, and re-layouts  4.27 us (2%)
    ppermute x16, waiting for transfers between devices, move(): return lax.ppermute(array, 'seq', pairs)  54.5 us
    ppermute x16, starting transfers between devices, move(): return lax.ppermute(array, 'seq', pairs)  54.3 us
    pallas_call x2, Pallas kernels, attend_tile(): pl.pallas_call(attend_kernel, out_shape=jax.ShapeDtypeStruct((rows, heads...  23.8 us
    dot_general x1, matrix products, local_plane(): jnp.dot(attended, w, preferred_element_type=jnp.float32)  12.8 us
    all_to_all x1, waiting for transfers between devices, local_plane(): q = lax.all_to_all(queries, 'head', 1, 0, tiled=True)  10.7 us
    ppermute x2, waiting for transfers between devices, local_plane(): other = [lax.ppermute(a, 'head', [(0, 1), (1, 0)]) for a in mine]  9.02 us
  transfers between devices with their start and end apart: 20, of which 5 were waited for; matrix products, arithmetic and copies ran while one was open for 2% of the time, Pallas kernels for 13%

profile of v2, /device:TPU:0, one launch (start us, length us, event | category | flops | bytes accessed | tf_op | source)
XLA Modules:
  0.0 190.1 jit_solution(4237731513306820186)
XLA Ops:
  6.5 0.0 all-gather.2.cloned.1.call-start
  6.5 0.7 all-gather.2.cloned.1.call-update
  7.3 0.4 copy-done.13
  7.7 1.2 fusion.15
  8.9 0.0 copy-start.12
  8.9 0.1 pad_maximum_fusion.refs_3_
  9.0 0.0 copy-start.2
  9.0 0.8 collective-permute-start.2
  9.8 5.0 %collective-permute-start = (bf16[512,768]{1,0:T(8,128)(2,1)S(1)}, bf16[512,768]{1,0:T(8,128)(2,1)S(1)}, u32[]{:S(2)}, u32[]{:S(2)}) collective-permute-start(bf16[512,768]{1,0:T(8,128)(2,1)S(1)} %pad_maximum_fusion.refs_3_), channel_id=1, source_target_pairs={{0,8},{2,10},{4,12},{6,14},{8,16},{10,18},{12,20},{14,22},{16,24},... | collective-permute-start | bytes 2359304 | tf_op jit(solution)/shard_map/ppermute | solution.py:182
  14.8 1.3 collective-permute-start.5
  16.1 2.6 %collective-permute-start.4 = (bf16[512,768]{1,0:T(8,128)(2,1)S(1)}, bf16[512,768]{1,0:T(8,128)(2,1)S(1)}, u32[]{:S(2)}, u32[]{:S(2)}) collective-permute-start(bf16[512,768]{1,0:T(8,128)(2,1)S(1)} %pad_maximum_fusion.refs_3_), channel_id=1, source_target_pairs={{0,2},{2,0},{4,6},{6,4},{8,10},{10,8},{12,14},{14,12},{16,18},{18,... | collective-permute-start | bytes 2359304 | tf_op jit(solution)/shard_map/ppermute | solution.py:182
  18.7 0.1 pad_maximum_fusion.1.refs_3_
  18.8 0.0 copy-start.1
  18.8 0.7 collective-permute-start.10
  19.5 0.0 collective-permute-done.2.refs_5_
  19.5 0.0 copy-start.4
  19.5 1.3 collective-permute-start.13
  20.8 22.7 %collective-permute-done.refs_0_ = bf16[512,768]{1,0:T(8,128)(2,1)S(1)} collective-permute-done((bf16[512,768]{1,0:T(8,128)(2,1)S(1)}, bf16[512,768]{1,0:T(8,128)(2,1)S(1)}, u32[]{:S(2)}, u32[]{:S(2)}) %collective-permute-start) | collective-permute-done | bytes 786464 | tf_op jit(solution)/shard_map/ppermute | solution.py:182
  43.5 5.3 %collective-permute-start.8 = (bf16[512,768]{1,0:T(8,128)(2,1)S(1)}, bf16[512,768]{1,0:T(8,128)(2,1)}, u32[]{:S(2)}, u32[]{:S(2)}) collective-permute-start(bf16[512,768]{1,0:T(8,128)(2,1)S(1)} %pad_maximum_fusion.1.refs_3_), channel_id=1, source_target_pairs={{0,8},{2,10},{4,12},{6,14},{8,16},{10,18},{12,20},{14,22},{16,24},... | collective-permute-start | bytes 2359304 | tf_op jit(solution)/shard_map/ppermute | solution.py:182
  48.8 4.7 %collective-permute-done.5.refs_6_ = bf16[512,768]{1,0:T(8,128)(2,1)S(1)} collective-permute-done((bf16[512,768]{1,0:T(8,128)(2,1)S(1)}, bf16[512,768]{1,0:T(8,128)(2,1)S(1)}, u32[]{:S(2)}, u32[]{:S(2)}) %collective-permute-start.5) | collective-permute-done | bytes 786464 | tf_op jit(solution)/shard_map/ppermute | solution.py:182
  53.4 0.7 collective-permute-start.3
  54.2 0.0 collective-permute-done.4.refs_4_
  54.2 0.0 copy-start.7
  54.2 0.7 collective-permute-start.7
  54.9 0.0 collective-permute-done.10.refs_5_
  54.9 0.0 copy-start.3
  54.9 5.2 %collective-permute-start.1 = (bf16[512,768]{1,0:T(8,128)(2,1)S(1)}, bf16[512,768]{1,0:T(8,128)(2,1)S(1)}, u32[]{:S(2)}, u32[]{:S(2)}) collective-permute-start(bf16[512,768]{1,0:T(8,128)(2,1)S(1)} %collective-permute-done.refs_0_), channel_id=1, source_target_pairs={{0,2},{2,0},{4,6},{6,4},{8,10},{10,8},{12,14},{14,12},{16,18},{18,... | collective-permute-start | bytes 2359304 | tf_op jit(solution)/shard_map/ppermute | solution.py:182
  60.1 27.1 %collective-permute-done.13.refs_6_ = bf16[512,768]{1,0:T(8,128)(2,1)} collective-permute-done((bf16[512,768]{1,0:T(8,128)(2,1)S(1)}, bf16[512,768]{1,0:T(8,128)(2,1)}, u32[]{:S(2)}, u32[]{:S(2)}) %collective-permute-start.13) | collective-permute-done | bytes 786464 | tf_op jit(solution)/shard_map/ppermute | solution.py:182
  87.3 1.5 collective-permute-start.6
  88.8 0.0 collective-permute-done.8.refs_0_
  88.8 0.0 collective-permute-start.12
  88.8 0.0 collective-permute-done.3.refs_2_
  88.8 0.0 copy-start.8
  88.8 1.6 collective-permute-start.11
  90.3 0.0 copy-done.4
  90.3 0.0 collective-permute-done.7.refs_8_
  90.4 0.0 copy-done.5
  90.4 1.5 collective-permute-start.15
  91.9 0.0 collective-permute-done.1.refs_1_
  91.9 0.0 copy-done.6
  91.9 26.0 %collective-permute-start.14 = (bf16[512,768]{1,0:T(8,128)(2,1)}, bf16[512,768]{1,0:T(8,128)(2,1)}, u32[]{:S(2)}, u32[]{:S(2)}) collective-permute-start(bf16[512,768]{1,0:T(8,128)(2,1)} %collective-permute-done.13.refs_6_), channel_id=1, source_target_pairs={{0,2},{2,0},{4,6},{6,4},{8,10},{10,8},{12,14},{14,12},{16,18},{18,... | collective-permute-start | bytes 2359304 | tf_op jit(solution)/shard_map/ppermute | solution.py:182
  117.9 0.0 collective-permute-done.6.refs_7_
  117.9 0.0 copy-done.7
  117.9 0.1 collective-permute-start.9
  118.0 0.0 copy-done.8
  118.0 0.8 copy-done.11
  118.8 0.9 copy.9
  119.7 3.5 %all-to-all-start = ((bf16[128,2,1536]{2,0,1:T(8,128)(2,1)}), bf16[128,2,1536]{2,0,1:T(8,128)(2,1)S(1)}, u32[]{:S(2)}, u32[]{:S(2)}) async-start(bf16[128,2,1536]{2,0,1:T(8,128)(2,1)} %bitcast.9), calls=%async_computation | async-start | bytes 1572864 | tf_op jit(solution)/shard_map/all_to_all | solution.py:201
  123.3 0.7 pad_add_fusion.listed
  124.0 10.7 %all-to-all-done = bf16[128,2,1536]{2,0,1:T(8,128)(2,1)S(1)} async-done(((bf16[128,2,1536]{2,0,1:T(8,128)(2,1)}), bf16[128,2,1536]{2,0,1:T(8,128)(2,1)S(1)}, u32[]{:S(2)}, u32[]{:S(2)}) %all-to-all-start) | async-done | bytes 786464 | tf_op jit(solution)/shard_map/all_to_all | solution.py:201
  134.7 0.9 copy-done
  135.6 11.9 %shard_map.55 = bf16[256,768]{1,0:T(8,128)(2,1)} custom-call(s32[28]{0:T(128)} %pad_add_fusion.listed, bf16[256,1536]{1,0:T(8,128)(2,1)} %bitcast.10, bf16[512,768]{1,0:T(8,128)(2,1)} %copy-done.5, bf16[512,768]{1,0:T(8,128)(2,1)} %copy-done.10, bf16[512,768]{1,0:T(8,128)(2,1)} %copy-done.8, bf16[512,768]{1,0:T(8,128)(2,1)} %copy-done.2, ...), custom_call_target="tpu_custom_call" | custom-call | flops 1811939328 | bytes 7864320 | tf_op jit(solution)/shard_map/pallas_call | solution.py:154
  147.4 0.0 collective-permute-done.12.refs_4_
  147.4 0.4 collective-permute-start.16
  147.8 0.0 collective-permute-done.11.refs_2_
  147.8 0.0 collective-permute-done.15.refs_8_
  147.8 0.0 collective-permute-done.14.refs_7_
  147.8 0.0 collective-permute-done.9.refs_1_
  147.8 11.9 %shard_map.56 = bf16[256,768]{1,0:T(8,128)(2,1)} custom-call(s32[28]{0:T(128)} %pad_add_fusion.listed, bf16[256,1536]{1,0:T(8,128)(2,1)} %bitcast.11, bf16[512,768]{1,0:T(8,128)(2,1)} %collective-permute-done.8.refs_0_, bf16[512,768]{1,0:T(8,128)(2,1)} %collective-permute-done.9.refs_1_, bf16[512,768]{1,0:T(8,128)(2,1)} %collective-permute-done.11.refs_2_, ...), custom_call_target="tpu_custom_call" | custom-call | flops 1811939328 | bytes 7864320 | tf_op jit(solution)/shard_map/pallas_call | solution.py:154
  159.7 1.7 collective-permute-start.17
  161.5 0.0 collective-permute-done.16
  161.5 9.0 %collective-permute-done.17 = bf16[256,768]{1,0:T(8,128)(2,1)S(1)} collective-permute-done((bf16[256,768]{1,0:T(8,128)(2,1)}, bf16[256,768]{1,0:T(8,128)(2,1)S(1)}, u32[]{:S(2)}, u32[]{:S(2)}) %collective-permute-start.17) | collective-permute-done | bytes 393248 | tf_op jit(solution)/shard_map/ppermute | solution.py:203
  170.5 0.0 copy-done.14
  170.5 12.8 %convolution_convert_fusion = bf16[256,3072]{1,0:T(8,128)(2,1)} fusion(bf16[3072,3072]{1,0:T(8,128)(2,1)} %all-gather.2.cloned.1.call-done, bf16[256,768]{1,0:T(8,128)(2,1)S(1)} %collective-permute-done.17, bf16[256,768]{1,0:T(8,128)(2,1)S(1)} %collective-permute-done.16, bf16[256,768]{1,0:T(8,128)(2,1)} %shard_map.56, bf16[256,768]{1,0:T(8,128)(2,1)S(1)} %copy-done.14, ...), kind=kOutput, calls=%fused_computation | convolution fusion | flops 4845993984 | bytes 22020096 | tf_op jit(solution)/shard_map/dot_general | solution.py:205
  (17 shorter events, 0.0 us)
Async XLA Ops:
  6.5 1.1 copy-start.13
  6.5 163.9 %all-gather.2.cloned.1.call-start = ((), (), s32[]{:S(2)}) async-start(), calls=%async_computation.1 | async-start | bytes 20054016 | tf_op jit(solution)/shard_map/all_gather | solution.py:187
  8.9 109.9 %copy-start.12 = (bf16[128,3072]{1,0:T(8,128)(2,1)S(1)}, bf16[128,3072]{1,0:T(8,128)(2,1)}, u32[]{:S(2)}) copy-start(bf16[128,3072]{1,0:T(8,128)(2,1)} %param.5) | copy-start | bytes 2359300
  9.0 110.8 %copy-start.2 = (bf16[512,768]{1,0:T(8,128)(2,1)}, bf16[512,768]{1,0:T(8,128)(2,1)S(1)}, u32[]{:S(2)}) copy-start(bf16[512,768]{1,0:T(8,128)(2,1)S(1)} %pad_maximum_fusion.refs_3_) | copy-start | bytes 2359300
  9.0 10.5 %collective-permute-start.2 = (bf16[512,768]{1,0:T(8,128)(2,1)S(1)}, bf16[512,768]{1,0:T(8,128)(2,1)S(1)}, u32[]{:S(2)}, u32[]{:S(2)}) collective-permute-start(bf16[512,768]{1,0:T(8,128)(2,1)S(1)} %pad_maximum_fusion.refs_3_), channel_id=1, source_target_pairs={{2,4},{4,2},{10,12},{12,10},{18,20},{20,18},{26,28},{28,26},{3,5},... | collective-permute-start | bytes 2359304 | tf_op jit(solution)/shard_map/ppermute | solution.py:182
  9.8 33.7 %collective-permute-start = (bf16[512,768]{1,0:T(8,128)(2,1)S(1)}, bf16[512,768]{1,0:T(8,128)(2,1)S(1)}, u32[]{:S(2)}, u32[]{:S(2)}) collective-permute-start(bf16[512,768]{1,0:T(8,128)(2,1)S(1)} %pad_maximum_fusion.refs_3_), channel_id=1, source_target_pairs={{0,8},{2,10},{4,12},{6,14},{8,16},{10,18},{12,20},{14,22},{16,24},... | collective-permute-start | bytes 2359304 | tf_op jit(solution)/shard_map/ppermute | solution.py:182
  14.8 38.6 %collective-permute-start.5 = (bf16[512,768]{1,0:T(8,128)(2,1)S(1)}, bf16[512,768]{1,0:T(8,128)(2,1)S(1)}, u32[]{:S(2)}, u32[]{:S(2)}) collective-permute-start(bf16[512,768]{1,0:T(8,128)(2,1)S(1)} %pad_maximum_fusion.refs_3_), channel_id=1, source_target_pairs={{8,0},{10,2},{12,4},{14,6},{16,8},{18,10},{20,12},{22,14},{24,16},... | collective-permute-start | bytes 2359304 | tf_op jit(solution)/shard_map/ppermute | solution.py:182
  16.1 38.0 %collective-permute-start.4 = (bf16[512,768]{1,0:T(8,128)(2,1)S(1)}, bf16[512,768]{1,0:T(8,128)(2,1)S(1)}, u32[]{:S(2)}, u32[]{:S(2)}) collective-permute-start(bf16[512,768]{1,0:T(8,128)(2,1)S(1)} %pad_maximum_fusion.refs_3_), channel_id=1, source_target_pairs={{0,2},{2,0},{4,6},{6,4},{8,10},{10,8},{12,14},{14,12},{16,18},{18,... | collective-permute-start | bytes 2359304 | tf_op jit(solution)/shard_map/ppermute | solution.py:182
  18.8 101.0 %copy-start.1 = (bf16[512,768]{1,0:T(8,128)(2,1)}, bf16[512,768]{1,0:T(8,128)(2,1)S(1)}, u32[]{:S(2)}) copy-start(bf16[512,768]{1,0:T(8,128)(2,1)S(1)} %pad_maximum_fusion.1.refs_3_) | copy-start | bytes 2359300
  18.8 36.1 %collective-permute-start.10 = (bf16[512,768]{1,0:T(8,128)(2,1)S(1)}, bf16[512,768]{1,0:T(8,128)(2,1)S(1)}, u32[]{:S(2)}, u32[]{:S(2)}) collective-permute-start(bf16[512,768]{1,0:T(8,128)(2,1)S(1)} %pad_maximum_fusion.1.refs_3_), channel_id=1, source_target_pairs={{2,4},{4,2},{10,12},{12,10},{18,20},{20,18},{26,28},{28,26},{3,5},... | collective-permute-start | bytes 2359304 | tf_op jit(solution)/shard_map/ppermute | solution.py:182
  19.5 70.9 %copy-start.4 = (bf16[512,768]{1,0:T(8,128)(2,1)}, bf16[512,768]{1,0:T(8,128)(2,1)S(1)}, u32[]{:S(2)}) copy-start(bf16[512,768]{1,0:T(8,128)(2,1)S(1)} %collective-permute-done.2.refs_5_) | copy-start | bytes 2359300
  19.5 67.8 %collective-permute-start.13 = (bf16[512,768]{1,0:T(8,128)(2,1)S(1)}, bf16[512,768]{1,0:T(8,128)(2,1)}, u32[]{:S(2)}, u32[]{:S(2)}) collective-permute-start(bf16[512,768]{1,0:T(8,128)(2,1)S(1)} %pad_maximum_fusion.1.refs_3_), channel_id=1, source_target_pairs={{8,0},{10,2},{12,4},{14,6},{16,8},{18,10},{20,12},{22,14},{24,16},... | collective-permute-start | bytes 2359304 | tf_op jit(solution)/shard_map/ppermute | solution.py:182
  43.5 46.9 %copy-start.5 = (bf16[512,768]{1,0:T(8,128)(2,1)}, bf16[512,768]{1,0:T(8,128)(2,1)S(1)}, u32[]{:S(2)}) copy-start(bf16[512,768]{1,0:T(8,128)(2,1)S(1)} %collective-permute-done.refs_0_) | copy-start | bytes 2359300
  43.5 45.3 %collective-permute-start.8 = (bf16[512,768]{1,0:T(8,128)(2,1)S(1)}, bf16[512,768]{1,0:T(8,128)(2,1)}, u32[]{:S(2)}, u32[]{:S(2)}) collective-permute-start(bf16[512,768]{1,0:T(8,128)(2,1)S(1)} %pad_maximum_fusion.1.refs_3_), channel_id=1, source_target_pairs={{0,8},{2,10},{4,12},{6,14},{8,16},{10,18},{12,20},{14,22},{16,24},... | collective-permute-start | bytes 2359304 | tf_op jit(solution)/shard_map/ppermute | solution.py:182
  53.4 38.5 %copy-start.6 = (bf16[512,768]{1,0:T(8,128)(2,1)}, bf16[512,768]{1,0:T(8,128)(2,1)S(1)}, u32[]{:S(2)}) copy-start(bf16[512,768]{1,0:T(8,128)(2,1)S(1)} %collective-permute-done.5.refs_6_) | copy-start | bytes 2359300
  53.4 35.3 %collective-permute-start.3 = (bf16[512,768]{1,0:T(8,128)(2,1)S(1)}, bf16[512,768]{1,0:T(8,128)(2,1)S(1)}, u32[]{:S(2)}, u32[]{:S(2)}) collective-permute-start(bf16[512,768]{1,0:T(8,128)(2,1)S(1)} %collective-permute-done.2.refs_5_), channel_id=1, source_target_pairs={{2,10},{4,12},{10,18},{12,20},{18,26},{20,28},{3,11},{5,13},{11,19... | collective-permute-start | bytes 2359304 | tf_op jit(solution)/shard_map/ppermute | solution.py:182
  54.2 63.7 %copy-start.7 = (bf16[512,768]{1,0:T(8,128)(2,1)}, bf16[512,768]{1,0:T(8,128)(2,1)S(1)}, u32[]{:S(2)}) copy-start(bf16[512,768]{1,0:T(8,128)(2,1)S(1)} %collective-permute-done.4.refs_4_) | copy-start | bytes 2359300
  54.2 36.2 %collective-permute-start.7 = (bf16[512,768]{1,0:T(8,128)(2,1)S(1)}, bf16[512,768]{1,0:T(8,128)(2,1)S(1)}, u32[]{:S(2)}, u32[]{:S(2)}) collective-permute-start(bf16[512,768]{1,0:T(8,128)(2,1)S(1)} %collective-permute-done.2.refs_5_), channel_id=1, source_target_pairs={{10,2},{12,4},{18,10},{20,12},{26,18},{28,20},{11,3},{13,5},{19,11... | collective-permute-start | bytes 2359304 | tf_op jit(solution)/shard_map/ppermute | solution.py:182
  54.9 64.8 %copy-start.3 = (bf16[512,768]{1,0:T(8,128)(2,1)}, bf16[512,768]{1,0:T(8,128)(2,1)S(1)}, u32[]{:S(2)}) copy-start(bf16[512,768]{1,0:T(8,128)(2,1)S(1)} %collective-permute-done.10.refs_5_) | copy-start | bytes 2359300
  54.9 37.0 %collective-permute-start.1 = (bf16[512,768]{1,0:T(8,128)(2,1)S(1)}, bf16[512,768]{1,0:T(8,128)(2,1)S(1)}, u32[]{:S(2)}, u32[]{:S(2)}) collective-permute-start(bf16[512,768]{1,0:T(8,128)(2,1)S(1)} %collective-permute-done.refs_0_), channel_id=1, source_target_pairs={{0,2},{2,0},{4,6},{6,4},{8,10},{10,8},{12,14},{14,12},{16,18},{18,... | collective-permute-start | bytes 2359304 | tf_op jit(solution)/shard_map/ppermute | solution.py:182
  87.3 30.7 %collective-permute-start.6 = (bf16[512,768]{1,0:T(8,128)(2,1)S(1)}, bf16[512,768]{1,0:T(8,128)(2,1)S(1)}, u32[]{:S(2)}, u32[]{:S(2)}) collective-permute-start(bf16[512,768]{1,0:T(8,128)(2,1)S(1)} %collective-permute-done.5.refs_6_), channel_id=1, source_target_pairs={{0,2},{2,0},{4,6},{6,4},{8,10},{10,8},{12,14},{14,12},{16,18},{18,... | collective-permute-start | bytes 2359304 | tf_op jit(solution)/shard_map/ppermute | solution.py:182
  88.8 58.7 %collective-permute-start.12 = (bf16[512,768]{1,0:T(8,128)(2,1)S(1)}, bf16[512,768]{1,0:T(8,128)(2,1)}, u32[]{:S(2)}, u32[]{:S(2)}) collective-permute-start(bf16[512,768]{1,0:T(8,128)(2,1)S(1)} %pad_maximum_fusion.1.refs_3_), channel_id=1, source_target_pairs={{0,2},{2,0},{4,6},{6,4},{8,10},{10,8},{12,14},{14,12},{16,18},{18,... | collective-permute-start | bytes 2359304 | tf_op jit(solution)/shard_map/ppermute | solution.py:182
  88.8 29.2 %copy-start.8 = (bf16[512,768]{1,0:T(8,128)(2,1)}, bf16[512,768]{1,0:T(8,128)(2,1)S(1)}, u32[]{:S(2)}) copy-start(bf16[512,768]{1,0:T(8,128)(2,1)S(1)} %collective-permute-done.3.refs_2_) | copy-start | bytes 2359300
  88.8 59.0 %collective-permute-start.11 = (bf16[512,768]{1,0:T(8,128)(2,1)S(1)}, bf16[512,768]{1,0:T(8,128)(2,1)}, u32[]{:S(2)}, u32[]{:S(2)}) collective-permute-start(bf16[512,768]{1,0:T(8,128)(2,1)S(1)} %collective-permute-done.10.refs_5_), channel_id=1, source_target_pairs={{2,10},{4,12},{10,18},{12,20},{18,26},{20,28},{3,11},{5,13},{11,19... | collective-permute-start | bytes 2359304 | tf_op jit(solution)/shard_map/ppermute | solution.py:182
  90.4 27.7 %copy-start.9 = (bf16[512,768]{1,0:T(8,128)(2,1)}, bf16[512,768]{1,0:T(8,128)(2,1)S(1)}, u32[]{:S(2)}) copy-start(bf16[512,768]{1,0:T(8,128)(2,1)S(1)} %collective-permute-done.7.refs_8_) | copy-start | bytes 2359300
  90.4 57.4 %collective-permute-start.15 = (bf16[512,768]{1,0:T(8,128)(2,1)S(1)}, bf16[512,768]{1,0:T(8,128)(2,1)}, u32[]{:S(2)}, u32[]{:S(2)}) collective-permute-start(bf16[512,768]{1,0:T(8,128)(2,1)S(1)} %collective-permute-done.10.refs_5_), channel_id=1, source_target_pairs={{10,2},{12,4},{18,10},{20,12},{26,18},{28,20},{11,3},{13,5},{19,11... | collective-permute-start | bytes 2359304 | tf_op jit(solution)/shard_map/ppermute | solution.py:182
  91.9 26.1 %copy-start.10 = (bf16[512,768]{1,0:T(8,128)(2,1)}, bf16[512,768]{1,0:T(8,128)(2,1)S(1)}, u32[]{:S(2)}) copy-start(bf16[512,768]{1,0:T(8,128)(2,1)S(1)} %collective-permute-done.1.refs_1_) | copy-start | bytes 2359300
  91.9 55.9 %collective-permute-start.14 = (bf16[512,768]{1,0:T(8,128)(2,1)}, bf16[512,768]{1,0:T(8,128)(2,1)}, u32[]{:S(2)}, u32[]{:S(2)}) collective-permute-start(bf16[512,768]{1,0:T(8,128)(2,1)} %collective-permute-done.13.refs_6_), channel_id=1, source_target_pairs={{0,2},{2,0},{4,6},{6,4},{8,10},{10,8},{12,14},{14,12},{16,18},{18,... | collective-permute-start | bytes 2359304 | tf_op jit(solution)/shard_map/ppermute | solution.py:182
  117.9 0.9 copy-start.11
  117.9 29.9 %collective-permute-start.9 = (bf16[512,768]{1,0:T(8,128)(2,1)}, bf16[512,768]{1,0:T(8,128)(2,1)}, u32[]{:S(2)}, u32[]{:S(2)}) collective-permute-start(bf16[512,768]{1,0:T(8,128)(2,1)} %collective-permute-done.8.refs_0_), channel_id=1, source_target_pairs={{0,2},{2,0},{4,6},{6,4},{8,10},{10,8},{12,14},{14,12},{16,18},{18,... | collective-permute-start | bytes 2359304 | tf_op jit(solution)/shard_map/ppermute | solution.py:182
  118.8 4.5 %copy-start.15 = (s32[1,27]{1,0:T(1,128)S(1)}, s32[1,27]{1,0:T(1,128)}, u32[]{:S(2)}) copy-start(s32[1,27]{1,0:T(1,128)} %param.8) | copy-start | bytes 328
  119.7 14.9 %all-to-all-start = ((bf16[128,2,1536]{2,0,1:T(8,128)(2,1)}), bf16[128,2,1536]{2,0,1:T(8,128)(2,1)S(1)}, u32[]{:S(2)}, u32[]{:S(2)}) async-start(bf16[128,2,1536]{2,0,1:T(8,128)(2,1)} %bitcast.9), calls=%async_computation | async-start | bytes 1572864 | tf_op jit(solution)/shard_map/all_to_all | solution.py:201
  134.7 0.9 copy-start
  147.4 23.0 %copy-start.14 = (bf16[256,768]{1,0:T(8,128)(2,1)S(1)}, bf16[256,768]{1,0:T(8,128)(2,1)}, u32[]{:S(2)}) copy-start(bf16[256,768]{1,0:T(8,128)(2,1)} %shard_map.55) | copy-start | bytes 1179652
  147.4 14.0 %collective-permute-start.16 = (bf16[256,768]{1,0:T(8,128)(2,1)}, bf16[256,768]{1,0:T(8,128)(2,1)S(1)}, u32[]{:S(2)}, u32[]{:S(2)}) collective-permute-start(bf16[256,768]{1,0:T(8,128)(2,1)} %shard_map.55), channel_id=1, source_target_pairs={{0,1},{1,0},{2,3},{3,2},{4,5},{5,4},{6,7},{7,6},{8,9},{9,8},{10,11... | collective-permute-start | bytes 1179656 | tf_op jit(solution)/shard_map/ppermute | solution.py:203
  159.7 10.8 %collective-permute-start.17 = (bf16[256,768]{1,0:T(8,128)(2,1)}, bf16[256,768]{1,0:T(8,128)(2,1)S(1)}, u32[]{:S(2)}, u32[]{:S(2)}) collective-permute-start(bf16[256,768]{1,0:T(8,128)(2,1)} %shard_map.56), channel_id=1, source_target_pairs={{0,1},{1,0},{2,3},{3,2},{4,5},{5,4},{6,7},{7,6},{8,9},{9,8},{10,11... | collective-permute-start | bytes 1179656 | tf_op jit(solution)/shard_map/ppermute | solution.py:203
Sparse Core Ops, SparseCore 0:
  9.0 152.2 all-gather.1

commit v3 on v2

--- a/solution.py
+++ b/solution.py
@@ -112,9 +112,8 @@
 
 
 def attend_kernel(listed, q_ref, *refs):
-    tiles, o_ref = refs[:9], refs[9]
-    tile, width = q_ref.shape
-    coef = width**-0.5 * LOG2E
+    keys, values, o_ref = refs[:9], refs[9:18], refs[-1]
+    coef = q_ref.shape[1] ** -0.5 * LOG2E
     toward = 1 - 2 * (listed[27] & 1)
     q = q_ref[...]
     top = total = acc = None
@@ -123,7 +122,7 @@
         new = top
         for k, step in enumerate((0, toward, -toward)):
             s = lax.dot_general(
-                tiles[3 * r + k][:tile, :], q, (((1,), (1,)), ((), ())), preferred_element_type=jnp.float32
+                keys[3 * r + k][...], q, (((1,), (1,)), ((), ())), preferred_element_type=jnp.float32
             )
             live = listed[10 + 3 * r + step] >= 0
             scores.append(s)
@@ -136,8 +135,8 @@
             w_sum = jnp.sum(w, axis=0, keepdims=True)
             part = w_sum if part is None else part + w_sum
             weights.append(w.astype(jnp.bfloat16))
-        values = jnp.concatenate([tiles[3 * r + k][tile:, :].T for k in range(3)], axis=1)
-        pv = jnp.dot(values, jnp.concatenate(weights, axis=0), preferred_element_type=jnp.float32)
+        sides = jnp.concatenate([values[3 * r + k][...].T for k in range(3)], axis=1)
+        pv = jnp.dot(sides, jnp.concatenate(weights, axis=0), preferred_element_type=jnp.float32)
         if top is None:
             total, acc = part, pv
         else:
@@ -148,62 +147,180 @@
     o_ref[...] = (acc / total).astype(jnp.bfloat16).T
 
 
-def attend_tile(listed, q, first, tiles):
-    rows = q.shape[0]
-    heads = tiles[0].shape[1] // HEAD_DIM
+def attend_tile(listed, q, head, count, first, own, rows, before):
+    tile = q.shape[0]
+
+    def spec(block, at=first):
+        return pl.BlockSpec((tile, HEAD_DIM), lambda h, listed: (block, at + h))
+
     return pl.pallas_call(
         attend_kernel,
-        out_shape=jax.ShapeDtypeStruct((rows, heads * HEAD_DIM), jnp.bfloat16),
+        out_shape=jax.ShapeDtypeStruct((tile, count * HEAD_DIM), jnp.bfloat16),
         grid_spec=pltpu.PrefetchScalarGridSpec(
             num_scalar_prefetch=1,
-            grid=(heads,),
-            in_specs=[pl.BlockSpec((rows, HEAD_DIM), lambda h, listed: (0, first + h))]
-            + [pl.BlockSpec((2 * rows, HEAD_DIM), lambda h, listed: (0, h))] * len(tiles),
-            out_specs=pl.BlockSpec((rows, HEAD_DIM), lambda h, listed: (0, h)),
+            grid=(count,),
+            in_specs=[spec(0, head)]
+            + [spec(0)] * 3
+            + [spec(0, head)] * 3
+            + [spec(2)] * 3
+            + [spec(1)] * 3
+            + [spec(1, head)] * 3
+            + [spec(3)] * 3
+            + [pl.BlockSpec(memory_space=pl.ANY)] * len(before),
+            out_specs=pl.BlockSpec((tile, HEAD_DIM), lambda h, listed: (0, h)),
         ),
         compiler_params=pltpu.CompilerParams(vmem_limit_bytes=VMEM_LIMIT),
         cost_estimate=pl.CostEstimate(
-            flops=heads * 36 * rows * rows * HEAD_DIM,
-            bytes_accessed=40 * heads * rows * HEAD_DIM,
-            transcendentals=heads * 9 * rows * rows,
+            flops=count * 36 * tile * tile * HEAD_DIM,
+            bytes_accessed=40 * count * tile * HEAD_DIM,
+            transcendentals=count * 9 * tile * tile,
         ),
-    )(listed, q, *tiles)
+    )(listed, q, *rows, *own, *rows, *rows, *own, *rows, *before)
+
+
+def project_kernel(planes, wides, spot, *refs):
+    count = 4 * len(wides)
+    pieces, refs = refs[:count], refs[count:]
+    if wides:
+        w_hbm, here, there, a_ref, w_ref, acc, sems = refs
+    else:
+        a_ref, w_hbm, here, there, w_ref, acc, sems = refs
+    outs = (here, there)
+    tile = a_ref.shape[0] // 2
+    shard = w_ref.shape[0] // (planes * GW)
+    block = GW * shard
+    loads, copies, at = [], [], 0
+    for n, wide in enumerate(wides):
+        for i in range(4):
+            col = (spot[0] if i < 2 else 1 - spot[0]) * sum(wides) + at
+            dst = a_ref.at[pl.ds(i % 2 * tile, tile), pl.ds(pl.multiple_of(col, 128), wide)]
+            loads.append(pltpu.make_async_copy(pieces[4 * n + i], dst, sems.at[4 * n + i]))
+        at += wide
+    for z in range(planes):
+        for c in range(GW):
+            src = w_hbm.at[pl.ds((z * GW + c % 2 * 2 + c // 2) * shard, shard), :]
+            dst = w_ref.at[pl.ds((z * GW + c) * shard, shard), :]
+            copies.append(pltpu.make_async_copy(src, dst, sems.at[count + z * GW + c]))
+    for c in loads + copies:
+        c.start()
+    for c in loads:
+        c.wait()
+    for z in range(planes):
+        for c in copies[z * GW : (z + 1) * GW]:
+            c.wait()
+        d = jnp.dot(
+            a_ref[:, z * block : (z + 1) * block],
+            w_ref[z * block : (z + 1) * block, :],
+            preferred_element_type=jnp.float32,
+        )
+        if z == 0:
+            acc[...] = d
+        elif z < planes - 1:
+            acc[...] += d
+        else:
+            d = acc[...] + d
+            for i in range(2):
+                outs[i][...] = d[i * tile : (i + 1) * tile, :].astype(jnp.bfloat16)
+
+
+def project(spot, pieces, w, planes, before):
+    deep, cols = w.shape
+    whole = len(pieces) == 1
+    tile = pieces[0].shape[0] // (2 if whole else 1)
+    wides = [] if whole else [p.shape[1] for p in pieces[::4]]
+    vmem, hbm = pl.BlockSpec(memory_space=pltpu.VMEM), pl.BlockSpec(memory_space=pl.ANY)
+    made = jax.ShapeDtypeStruct((tile, cols), jnp.bfloat16)
+    put = jax.ShapeDtypeStruct((2 * tile, deep), jnp.bfloat16)
+    outs = pl.pallas_call(
+        lambda spot, *refs: project_kernel(
+            planes, wides, spot, *refs[: len(pieces) + 1], *refs[len(pieces) + 1 + len(before) :]
+        ),
+        out_shape=[made, made] + ([] if whole else [put]),
+        in_specs=[pl.BlockSpec(memory_space=pltpu.SMEM)]
+        + [vmem if whole else hbm] * len(pieces)
+        + [hbm] * (1 + len(before)),
+        out_specs=[vmem] * (2 if whole else 3),
+        scratch_shapes=[
+            pltpu.VMEM((deep, cols), jnp.bfloat16),
+            pltpu.VMEM((2 * tile, cols), jnp.float32),
+            pltpu.SemaphoreType.DMA((4 * len(wides) + planes * GW,)),
+        ],
+        compiler_params=pltpu.CompilerParams(vmem_limit_bytes=VMEM_LIMIT),
+        cost_estimate=pl.CostEstimate(
+            flops=4 * tile * deep * cols,
+            bytes_accessed=2 * (2 * tile * deep + deep * cols + 2 * tile * cols),
+            transcendentals=0,
+        ),
+    )(spot, *pieces, w, *before)
+    return [*outs, *(pieces if whole else [])]
 
 
 def local_plane(queries, keys, values, window, out_weight):
     span = lax.axis_size("seq")
+    planes = span // GW
     down = [(i, i + GW) for i in range(span - GW)]
     up = [(i + GW, i) for i in range(span - GW)]
     mates = [(i, i ^ 1) for i in range(span)]
     outer = [(i, i ^ 3) for i in range(span) if i % GW in (1, 2)]
-    side = lax.axis_index("head")
+    partners = [(i, i ^ 2) for i in range(span)]
+    both_cores = [[z * GW + x * 2 + k for z in range(planes) for k in range(2)] for x in range(2)]
+    seq, side = lax.axis_index("seq"), lax.axis_index("head")
+    half = seq // 2 % 2
+    tile, own_width = keys.shape
+    heads = own_width // HEAD_DIM
 
     def move(array, pairs):
         return lax.ppermute(array, "seq", pairs)
 
-    parts = 1
-    wide = out_weight.shape[1] // parts
-    w_all = [
-        lax.all_gather(out_weight[:, n * wide : (n + 1) * wide], "seq", axis=0, tiled=True) for n in range(parts)
+    def in_order(flag, own, other, axis):
+        return jnp.where(
+            flag == 0, jnp.concatenate([own, other], axis=axis), jnp.concatenate([other, own], axis=axis)
+        )
+
+    def line(array):
+        return [array, move(array, mates), move(array, outer)]
+
+    kv = jnp.concatenate([keys, values], axis=0)
+    kv_up, kv_dn = move(kv, down), move(kv, up)
+    q = lax.all_to_all(queries, "head", 1, 0, tiled=True)
+
+    cols = out_weight.shape[1] // 2
+    w_mine = lax.dynamic_slice_in_dim(out_weight, half * cols, cols, 1)
+    w_theirs = move(lax.dynamic_slice_in_dim(out_weight, (1 - half) * cols, cols, 1), partners)
+    w_cuts = [0, cols * 2 // 3 // 256 * 256, cols]
+    w_rows = [in_order(half, w_mine[:, lo:hi], w_theirs[:, lo:hi], 0) for lo, hi in zip(w_cuts[:-1], w_cuts[1:])]
+
+    kv, w_rows = lax.optimization_barrier((kv, w_rows))
+    own = line(kv)
+
+    kv_up, kv_dn, own, q, w_rows = lax.optimization_barrier((kv_up, kv_dn, own, q, w_rows))
+    w_all = [lax.all_gather(r, "seq", axis=0, tiled=True, axis_index_groups=both_cores) for r in w_rows]
+
+    part = heads // 3
+    cuts = [0, 2 * part * HEAD_DIM, own_width]
+    rows = [
+        line(jnp.concatenate([kv_up[:, lo:hi], kv_dn[:, lo:hi]], axis=0)) for lo, hi in zip(cuts[:-1], cuts[1:])
     ]
 
-    chunk = keys.shape[1] // 2
-    listed = jnp.concatenate([window[0], lax.axis_index("seq")[None]])
-    held = []
-    for at in (0, chunk):
-        kv = jnp.concatenate([keys[:, at : at + chunk], values[:, at : at + chunk]], axis=0)
-        kv_out = move(kv, outer)
-        kv_up, kv_dn = move(kv, down), move(kv, up)
-        out_up = move(kv_out, [p for p in down if p[0] % GW in (1, 2)])
-        out_dn = move(kv_out, [p for p in up if p[0] % GW in (1, 2)])
-        held.append([kv_up, move(kv_up, mates), out_up, kv, move(kv, mates), kv_out, kv_dn, move(kv_dn, mates), out_dn])
-
-    q = lax.all_to_all(queries, "head", 1, 0, tiled=True)
-    mine = [attend_tile(listed, q, n * chunk // HEAD_DIM, tiles) for n, tiles in enumerate(held)]
-    other = [lax.ppermute(a, "head", [(0, 1), (1, 0)]) for a in mine]
-    attended = jnp.where(side == 0, jnp.concatenate(mine + other, axis=1), jnp.concatenate(other + mine, axis=1))
-    made = [jnp.dot(attended, w, preferred_element_type=jnp.float32).astype(jnp.bfloat16) for w in w_all]
-    return jnp.concatenate(made, axis=1)
+    listed = jnp.concatenate([window[0], seq[None]])
+    pieces = []
+    for n, (held, first) in enumerate(((0, 0), (0, part), (1, 0))):
+        mine = attend_tile(listed, q, n * part, part, first, own, rows[held], pieces[1:4] if n == 2 else [])
+        pieces += [
+            mine,
+            move(mine, partners),
+            lax.ppermute(mine, "head", [(0, 1), (1, 0)]),
+            lax.ppermute(mine, ("seq", "head"), [(2 * i + y, 2 * (i ^ 2) + 1 - y) for i in range(span) for y in (0, 1)]),
+        ]
+
+    spot = jnp.stack([side, half])
+    own, other = [], []
+    for w in w_all:
+        here, there, *pieces = project(spot, pieces, w, planes, other)
+        own.append(here)
+        other.append(move(there, partners))
+    done = in_order(half, jnp.concatenate(own, axis=1), jnp.pad(other[0], ((0, 0), (0, cols - w_cuts[1]))), 1)
+    return lax.dynamic_update_slice(done, other[1], (0, (1 - half) * cols + w_cuts[1]))
 
 
 def solution(mesh):
@@ -211,7 +328,7 @@
 
     def local(queries, keys, values, window, out_weight):
         one_step = span == GH * GW and sides == 2
-        even = keys.shape[1] % (2 * HEAD_DIM) == 0
+        even = keys.shape[1] % (3 * HEAD_DIM) == 0 and out_weight.shape[1] % 1536 == 0
         which = local_plane if one_step and even else local_general
         return which(queries, keys, values, window, out_weight)
 

time: 191 us -> 183 us (0.958)
  waiting for transfers between devices: 75 us -> 43.7 us
  Pallas kernels: 23.8 us -> 41.4 us
  starting transfers between devices: 59.9 us -> 42.6 us
  local copies, waits for them, and re-layouts: 4.27 us -> 19.6 us
  blocking collectives: 0 us -> 13.3 us
  matrix products: 12.8 us -> 0 us
  other arithmetic: 0.77 us -> 8.24 us
    ppermute x16 -> x14, waiting for transfers between devices: 54.5 us -> 27.3 us  [move(): return lax.ppermute(array, 'seq', pairs)]
    pallas_call x2 -> x5, Pallas kernels: 23.8 us -> 41.4 us  [the longest x3 26.6 us: attend_tile(): pl.pallas_call(attend_kernel, out_shape=jax.ShapeDtypeStruct((tile, count...]
    ppermute x16 -> x14, starting transfers between devices: 54.3 us -> 37.7 us  [move(): return lax.ppermute(array, 'seq', pairs)]
    all_to_all x0 -> x1, blocking collectives: none -> 13.3 us  [local_plane(): q = lax.all_to_all(queries, 'head', 1, 0, tiled=True)]
    dot_general x1 -> x0, matrix products: 12.8 us -> none  [local_plane(): jnp.dot(attended, w, preferred_element_type=jnp.float32)]
    all_to_all x1 -> x0, waiting for transfers between devices: 10.7 us -> none  [local_plane(): q = lax.all_to_all(queries, 'head', 1, 0, tiled=True)]
    all_gather x1 -> x2, waiting for transfers between devices: 0.01 us -> 9.66 us  [local_plane(): lax.all_gather(r, 'seq', axis=0, tiled=True, axis_index_groups=both_cores)]
    unnamed x32 -> x45, local copies, waits for them, and re-layouts: 2.12 us -> 9.24 us
  transfers between devices with their start and end apart: 20 -> 22, of which waited for: 5 -> 10; matrix products, arithmetic and copies ran while one was open for 2% -> 9% of each run, Pallas kernels for 13% -> 19%
where the time goes in v3:
time: 183 us; the launch traced here: 182 us
  waiting for transfers between devices  43.7 us (24%)
  starting transfers between devices  42.6 us (23%)
  Pallas kernels  41.4 us (23%)
  local copies, waits for them, and re-layouts  19.6 us (11%)
  between operations  13.7 us (7%)
  blocking collectives  13.3 us (7%)
  other arithmetic  8.24 us (5%)
    ppermute x14, starting transfers between devices, move(): return lax.ppermute(array, 'seq', pairs)  37.7 us
    ppermute x14, waiting for transfers between devices, move(): return lax.ppermute(array, 'seq', pairs)  27.3 us
    pallas_call x3, Pallas kernels, attend_tile(): pl.pallas_call(attend_kernel, out_shape=jax.ShapeDtypeStruct((tile, count...  26.6 us
    pallas_call x2, Pallas kernels, project(): pl.pallas_call(lambda spot, *refs: project_kernel(planes, wides, spot, *r...  14.8 us
    all_to_all x1, blocking collectives, local_plane(): q = lax.all_to_all(queries, 'head', 1, 0, tiled=True)  13.3 us
    all_gather x2, waiting for transfers between devices, local_plane(): lax.all_gather(r, 'seq', axis=0, tiled=True, axis_index_groups=both_cores)  9.66 us
    unnamed x45, local copies, waits for them, and re-layouts  9.24 us
    select_n x3, other arithmetic, in_order(): jnp.where(flag == 0, jnp.concatenate([own, other], axis=axis), jnp.concat...  5.81 us
  transfers between devices with their start and end apart: 22, of which 10 were waited for; matrix products, arithmetic and copies ran while one was open for 9% of the time, Pallas kernels for 19%

profile of v3, /device:TPU:0, one launch (start us, length us, event | category | flops | bytes accessed | tf_op | source)
XLA Modules:
  0.0 182.5 jit_solution(10935073023330512201)
XLA Ops:
  6.5 1.3 copy-done
  7.8 0.8 constant_dynamic-slice_fusion.1
  8.7 2.9 %collective-permute-start.2 = (bf16[192,1536]{1,0:T(8,128)(2,1)}, bf16[192,1536]{1,0:T(8,128)(2,1)}, u32[]{:S(2)}, u32[]{:S(2)}) collective-permute-start(bf16[192,1536]{1,0:T(8,128)(2,1)} %constant_dynamic-slice_fusion.1), channel_id=1, source_target_pairs={{0,4},{2,6},{4,0},{6,2},{8,12},{10,14},{12,8},{14,10},{16,20},{18,... | collective-permute-start | bytes 1769480 | tf_op jit(solution)/shard_map/ppermute | solution.py:273
  11.6 0.1 constant_dynamic-update-slice_fusion.1
  11.7 0.1 constant_dynamic-update-slice_fusion.refs_3_.refs_12_
  11.7 4.7 %collective-permute-start = (bf16[512,1536]{1,0:T(8,128)(2,1)S(1)}, bf16[512,1536]{1,0:T(8,128)(2,1)}, u32[]{:S(2)}, u32[]{:S(2)}) collective-permute-start(bf16[512,1536]{1,0:T(8,128)(2,1)S(1)} %constant_dynamic-update-slice_fusion.refs_3_.refs_12_), channel_id=1, source_target_pairs={{0,8},{2,10},{4,12},{6,14},{8,16},{10,18},{12,20},{14,22},{16,24},... | collective-permute-start | bytes 4718600 | tf_op jit(solution)/shard_map/ppermute | solution.py:273
  16.5 1.3 collective-permute-start.1
  17.8 0.7 constant_dynamic-slice_fusion.2
  18.5 6.7 %collective-permute-done.2 = bf16[192,1536]{1,0:T(8,128)(2,1)} collective-permute-done((bf16[192,1536]{1,0:T(8,128)(2,1)}, bf16[192,1536]{1,0:T(8,128)(2,1)}, u32[]{:S(2)}, u32[]{:S(2)}) %collective-permute-start.2) | collective-permute-done | bytes 589856 | tf_op jit(solution)/shard_map/ppermute | solution.py:273
  25.2 1.0 slice.32
  26.3 1.2 maximum_select_fusion.1
  27.5 0.9 slice.33
  28.4 1.9 %maximum_select_fusion.2 = bf16[384,512]{1,0:T(8,128)(2,1)} fusion(bf16[192,512]{1,0:T(8,128)(2,1)S(1)} %slice.33, bf16[192,512]{1,0:T(8,128)(2,1)} %constant_dynamic-slice_fusion.2, pred[]{:T(512)S(6)} %eq.4), kind=kLoop, calls=%fused_computation.5 | loop fusion | flops 1769472 | bytes 786433 | tf_op jit(solution)/shard_map/jit(_where)/select_n | solution.py:276
  30.3 0.8 collective-permute-start.4
  31.1 0.1 copy.9
  31.2 13.3 %all_to_all.19 = bf16[128,2,1536]{2,0,1:T(8,128)(2,1)} all-to-all(bf16[128,2,1536]{2,0,1:T(8,128)(2,1)S(1)} %bitcast.14), channel_id=1, replica_groups=mesh['seq'=16,'head'=2] {'head'}, dimensions={1} | all-to-all | bytes 1572864 | tf_op jit(solution)/shard_map/all_to_all | solution.py:285
  44.4 4.1 %collective-permute-done = bf16[512,1536]{1,0:T(8,128)(2,1)} collective-permute-done((bf16[512,1536]{1,0:T(8,128)(2,1)S(1)}, bf16[512,1536]{1,0:T(8,128)(2,1)}, u32[]{:S(2)}, u32[]{:S(2)}) %collective-permute-start) | collective-permute-done | bytes 1572896 | tf_op jit(solution)/shard_map/ppermute | solution.py:273
  48.6 5.4 %collective-permute-done.1 = bf16[512,1536]{1,0:T(8,128)(2,1)} collective-permute-done((bf16[512,1536]{1,0:T(8,128)(2,1)S(1)}, bf16[512,1536]{1,0:T(8,128)(2,1)}, u32[]{:S(2)}, u32[]{:S(2)}) %collective-permute-start.1) | collective-permute-done | bytes 1572896 | tf_op jit(solution)/shard_map/ppermute | solution.py:273
  54.0 1.1 copy-done.5
  55.2 1.2 copy-done.6
  56.4 0.7 all-gather.5.cloned.1.call-update
  57.1 1.3 slice.29
  58.4 1.3 slice.28
  59.7 0.2 pad_maximum_fusion.refs_0_.refs_6_.refs_9_.refs_15_
  59.9 0.1 collective-permute-start.5
  60.0 0.8 collective-permute-start.6
  60.8 1.1 slice.31
  61.9 1.1 slice.30
  63.1 1.0 pad_maximum_fusion.1.refs_0_.refs_6_.refs_9_.refs_15_
  64.1 2.0 %collective-permute-start.13 = (bf16[1024,512]{1,0:T(8,128)(2,1)}, bf16[1024,512]{1,0:T(8,128)(2,1)}, u32[]{:S(2)}, u32[]{:S(2)}) collective-permute-start(bf16[1024,512]{1,0:T(8,128)(2,1)} %pad_maximum_fusion.1.refs_0_.refs_6_.refs_9_.refs_15_), channel_id=1, source_target_pairs={{0,2},{2,0},{4,6},{6,4},{8,10},{10,8},{12,14},{14,12},{16,18},{18,... | collective-permute-start | bytes 3145736 | tf_op jit(solution)/shard_map/ppermute | solution.py:273
  66.1 1.7 collective-permute-start.14
  67.7 0.7 pad_add_fusion.1.listed
  68.4 1.4 copy-done.2
  69.8 1.3 copy-done.3
  71.1 8.9 %shard_map.55.refs_0_ = bf16[256,512]{1,0:T(8,128)(2,1)} custom-call(s32[28]{0:T(128)} %pad_add_fusion.1.listed, bf16[256,1536]{1,0:T(8,128)(2,1)} %bitcast.11, bf16[1024,1024]{1,0:T(8,128)(2,1)} %copy-done.1, bf16[1024,1024]{1,0:T(8,128)(2,1)} %copy-done.2, bf16[1024,1024]{1,0:T(8,128)(2,1)} %copy-done.3, bf16[512,1536]{1,0:T(8,128)(2,1)} %copy-done.4, ...), custom_call_target="tpu_custom_call" | custom-call | flops 1207959552 | bytes 5242880 | tf_op jit(solution)/shard_map/pallas_call | solution.py:156
  80.0 18.4 %collective-permute-start.7 = (bf16[256,512]{1,0:T(8,128)(2,1)}, bf16[256,512]{1,0:T(8,128)(2,1)S(1)}, u32[]{:S(2)}, u32[]{:S(2)}) collective-permute-start(bf16[256,512]{1,0:T(8,128)(2,1)} %shard_map.55.refs_0_), channel_id=1, source_target_pairs={{0,4},{2,6},{4,0},{6,2},{8,12},{10,14},{12,8},{14,10},{16,20},{18,... | collective-permute-start | bytes 786440 | tf_op jit(solution)/shard_map/ppermute | solution.py:273
  98.3 1.5 collective-permute-start.8
  99.9 8.8 %shard_map.56.refs_4_ = bf16[256,512]{1,0:T(8,128)(2,1)} custom-call(s32[28]{0:T(128)} %pad_add_fusion.1.listed, bf16[256,1536]{1,0:T(8,128)(2,1)} %bitcast.12, bf16[1024,1024]{1,0:T(8,128)(2,1)} %copy-done.1, bf16[1024,1024]{1,0:T(8,128)(2,1)} %copy-done.2, bf16[1024,1024]{1,0:T(8,128)(2,1)} %copy-done.3, bf16[512,1536]{1,0:T(8,128)(2,1)} %copy-done.4, ...), custom_call_target="tpu_custom_call" | custom-call | flops 1207959552 | bytes 5242880 | tf_op jit(solution)/shard_map/pallas_call | solution.py:156
  108.7 2.0 %collective-permute-start.10 = (bf16[256,512]{1,0:T(8,128)(2,1)}, bf16[256,512]{1,0:T(8,128)(2,1)S(1)}, u32[]{:S(2)}, u32[]{:S(2)}) collective-permute-start(bf16[256,512]{1,0:T(8,128)(2,1)} %shard_map.56.refs_4_), channel_id=1, source_target_pairs={{0,4},{2,6},{4,0},{6,2},{8,12},{10,14},{12,8},{14,10},{16,20},{18,... | collective-permute-start | bytes 786440 | tf_op jit(solution)/shard_map/ppermute | solution.py:273
  110.8 1.5 collective-permute-start.11
  112.3 0.2 collective-permute-done.8.refs_19_.refs_2_
  112.6 0.4 copy-done.12
  113.0 0.3 copy-done.13
  113.3 0.7 copy-done.14
  114.0 8.9 %shard_map.57.refs_8_ = bf16[256,512]{1,0:T(8,128)(2,1)} custom-call(s32[28]{0:T(128)} %pad_add_fusion.1.listed, bf16[256,1536]{1,0:T(8,128)(2,1)} %bitcast.13, bf16[1024,512]{1,0:T(8,128)(2,1)} %pad_maximum_fusion.1.refs_0_.refs_6_.refs_9_.refs_15_, bf16[1024,512]{1,0:T(8,128)(2,1)} %collective-permute-done.13.refs_1_.refs_7_.refs_10_.refs_16_, ...), custom_call_target="tpu_custom_call" | custom-call | flops 1207959552 | bytes 5242880 | tf_op jit(solution)/shard_map/pallas_call | solution.py:156
  122.9 1.8 collective-permute-start.15
  124.6 1.5 collective-permute-start.16
  126.2 0.3 collective-permute-start.17
  126.4 0.6 pad_add_fusion.spot
  127.0 5.3 %collective-permute-done.15.refs_9_ = bf16[256,512]{1,0:T(8,128)(2,1)S(1)} collective-permute-done((bf16[256,512]{1,0:T(8,128)(2,1)}, bf16[256,512]{1,0:T(8,128)(2,1)S(1)}, u32[]{:S(2)}, u32[]{:S(2)}) %collective-permute-start.15) | collective-permute-done | bytes 262176 | tf_op jit(solution)/shard_map/ppermute | solution.py:273
  132.3 4.6 %collective-permute-done.16.refs_10_ = bf16[256,512]{1,0:T(8,128)(2,1)S(1)} collective-permute-done((bf16[256,512]{1,0:T(8,128)(2,1)}, bf16[256,512]{1,0:T(8,128)(2,1)S(1)}, u32[]{:S(2)}, u32[]{:S(2)}) %collective-permute-start.16) | collective-permute-done | bytes 262176 | tf_op jit(solution)/shard_map/ppermute | solution.py:312
  136.9 1.1 collective-permute-done.17.refs_11_
  138.1 0.7 copy-done.20
  138.8 8.8 %shard_map.58 = (bf16[256,1024]{1,0:T(8,128)(2,1)}, bf16[256,1024]{1,0:T(8,128)(2,1)}, bf16[512,3072]{1,0:T(8,128)(2,1)}) custom-call(s32[2]{0:T(128)} %pad_add_fusion.spot, bf16[256,512]{1,0:T(8,128)(2,1)} %shard_map.55.refs_0_, bf16[256,512]{1,0:T(8,128)(2,1)} %copy-done.12, bf16[256,512]{1,0:T(8,128)(2,1)} %copy-done.13, bf16[256,512]{1,0:T(8,128)(2,1)} %copy-done.14, ...), custom_call_target="tpu_custom_call" | custom-call | flops 3221225472 | bytes 10485760 | tf_op jit(solution)/shard_map/pallas_call | solution.py:234
  147.6 1.0 collective-permute-start.18
  148.6 9.7 %all-gather.5.cloned.1.call-done.refs_1_ = bf16[3072,512]{1,0:T(8,128)(2,1)} async-done(((bf16[384,512]{1,0:T(8,128)(2,1)}), bf16[3072,512]{1,0:T(8,128)(2,1)}) %all-gather.5.cloned.1.call-update) | async-done | bytes 3145744 | tf_op jit(solution)/shard_map/all_gather | solution.py:297
  158.3 2.9 %collective-permute-done.18.refs_2_ = bf16[256,1024]{1,0:T(8,128)(2,1)S(1)} collective-permute-done((bf16[256,1024]{1,0:T(8,128)(2,1)}, bf16[256,1024]{1,0:T(8,128)(2,1)S(1)}, u32[]{:S(2)}, u32[]{:S(2)}) %collective-permute-start.18) | collective-permute-done | bytes 524320 | tf_op jit(solution)/shard_map/ppermute | solution.py:273
  161.1 0.8 copy-done.7
  161.9 6.0 %shard_map.59 = (bf16[256,512]{1,0:T(8,128)(2,1)}, bf16[256,512]{1,0:T(8,128)(2,1)}) custom-call(s32[2]{0:T(128)} %pad_add_fusion.spot, bf16[512,3072]{1,0:T(8,128)(2,1)} %get-tuple-element.32.refs_0_, bf16[3072,512]{1,0:T(8,128)(2,1)} %all-gather.5.cloned.1.call-done.refs_1_, bf16[256,1024]{1,0:T(8,128)(2,1)} %copy-done.7), custom_call_target="tpu_custom_call" | custom-call | flops 1610612736 | bytes 6815744 | tf_op jit(solution)/shard_map/pallas_call | solution.py:234
  167.9 0.3 collective-permute-start.19
  168.3 1.1 pad.4
  169.4 2.7 %maximum_select_fusion = bf16[256,3072]{1,0:T(8,128)(2,1)} fusion(bf16[256,1536]{1,0:T(8,128)(2,1)S(1)} %pad.4, bf16[256,512]{1,0:T(8,128)(2,1)} %get-tuple-element.35, bf16[256,1024]{1,0:T(8,128)(2,1)S(1)} %copy-done.11, pred[]{:T(512)S(6)} %eq.4), kind=kLoop, calls=%fused_computation.1 | loop fusion | flops 10223616 | bytes 3145729 | tf_op jit(solution)/shard_map/jit(_where)/select_n | solution.py:276
  172.1 2.8 %collective-permute-done.19 = bf16[256,512]{1,0:T(8,128)(2,1)S(1)} collective-permute-done((bf16[256,512]{1,0:T(8,128)(2,1)}, bf16[256,512]{1,0:T(8,128)(2,1)S(1)}, u32[]{:S(2)}, u32[]{:S(2)}) %collective-permute-start.19) | collective-permute-done | bytes 262176 | tf_op jit(solution)/shard_map/ppermute | solution.py:273
  174.9 0.7 constant_dynamic-update-slice_fusion.2
  (53 shorter events, 0.2 us)
Async XLA Ops:
  6.5 1.3 copy-start
  6.5 5.1 %copy-start.8 = (bf16[256,1536]{1,0:T(8,128)(2,1)S(1)}, bf16[256,1536]{1,0:T(8,128)(2,1)}, u32[]{:S(2)}) copy-start(bf16[256,1536]{1,0:T(8,128)(2,1)} %param.6) | copy-start | bytes 2359300
  6.5 131.5 %all-gather.3.cloned.1.call-start = ((), (), s32[]{:S(2)}) async-start(), calls=%async_computation.1 | async-start | bytes 7077888 | tf_op jit(solution)/shard_map/all_gather | solution.py:297
  7.8 3.9 %copy-start.9 = (bf16[256,1536]{1,0:T(8,128)(2,1)S(1)}, bf16[256,1536]{1,0:T(8,128)(2,1)}, u32[]{:S(2)}) copy-start(bf16[256,1536]{1,0:T(8,128)(2,1)} %param.7) | copy-start | bytes 2359300
  8.7 16.6 %collective-permute-start.2 = (bf16[192,1536]{1,0:T(8,128)(2,1)}, bf16[192,1536]{1,0:T(8,128)(2,1)}, u32[]{:S(2)}, u32[]{:S(2)}) collective-permute-start(bf16[192,1536]{1,0:T(8,128)(2,1)} %constant_dynamic-slice_fusion.1), channel_id=1, source_target_pairs={{0,4},{2,6},{4,0},{6,2},{8,12},{10,14},{12,8},{14,10},{16,20},{18,... | collective-permute-start | bytes 1769480 | tf_op jit(solution)/shard_map/ppermute | solution.py:273
  11.7 18.6 %copy-start.4 = (bf16[512,1536]{1,0:T(8,128)(2,1)}, bf16[512,1536]{1,0:T(8,128)(2,1)S(1)}, u32[]{:S(2)}) copy-start(bf16[512,1536]{1,0:T(8,128)(2,1)S(1)} %constant_dynamic-update-slice_fusion.refs_3_.refs_12_) | copy-start | bytes 4718596
  11.7 36.8 %collective-permute-start = (bf16[512,1536]{1,0:T(8,128)(2,1)S(1)}, bf16[512,1536]{1,0:T(8,128)(2,1)}, u32[]{:S(2)}, u32[]{:S(2)}) collective-permute-start(bf16[512,1536]{1,0:T(8,128)(2,1)S(1)} %constant_dynamic-update-slice_fusion.refs_3_.refs_12_), channel_id=1, source_target_pairs={{0,8},{2,10},{4,12},{6,14},{8,16},{10,18},{12,20},{14,22},{16,24},... | collective-permute-start | bytes 4718600 | tf_op jit(solution)/shard_map/ppermute | solution.py:273
  16.5 37.6 %collective-permute-start.1 = (bf16[512,1536]{1,0:T(8,128)(2,1)S(1)}, bf16[512,1536]{1,0:T(8,128)(2,1)}, u32[]{:S(2)}, u32[]{:S(2)}) collective-permute-start(bf16[512,1536]{1,0:T(8,128)(2,1)S(1)} %constant_dynamic-update-slice_fusion.refs_3_.refs_12_), channel_id=1, source_target_pairs={{8,0},{10,2},{12,4},{14,6},{16,8},{18,10},{20,12},{22,14},{24,16},... | collective-permute-start | bytes 4718600 | tf_op jit(solution)/shard_map/ppermute | solution.py:273
  26.3 4.8 %copy-start.10 = (bf16[128,3072]{1,0:T(8,128)(2,1)S(1)}, bf16[128,3072]{1,0:T(8,128)(2,1)}, u32[]{:S(2)}) copy-start(bf16[128,3072]{1,0:T(8,128)(2,1)} %param.5) | copy-start | bytes 2359300
  30.3 23.7 %collective-permute-start.3 = (bf16[512,1536]{1,0:T(8,128)(2,1)S(1)}, bf16[512,1536]{1,0:T(8,128)(2,1)S(1)}, u32[]{:S(2)}, u32[]{:S(2)}) collective-permute-start(bf16[512,1536]{1,0:T(8,128)(2,1)S(1)} %constant_dynamic-update-slice_fusion.refs_3_.refs_12_), channel_id=1, source_target_pairs={{0,2},{2,0},{4,6},{6,4},{8,10},{10,8},{12,14},{14,12},{16,18},{18,... | collective-permute-start | bytes 4718600 | tf_op jit(solution)/shard_map/ppermute | solution.py:273
  30.3 23.7 %collective-permute-start.4 = (bf16[512,1536]{1,0:T(8,128)(2,1)S(1)}, bf16[512,1536]{1,0:T(8,128)(2,1)S(1)}, u32[]{:S(2)}, u32[]{:S(2)}) collective-permute-start(bf16[512,1536]{1,0:T(8,128)(2,1)S(1)} %constant_dynamic-update-slice_fusion.refs_3_.refs_12_), channel_id=1, source_target_pairs={{2,4},{4,2},{10,12},{12,10},{18,20},{20,18},{26,28},{28,26},{3,5},... | collective-permute-start | bytes 4718600 | tf_op jit(solution)/shard_map/ppermute | solution.py:273
  54.0 1.2 copy-start.5
  55.2 1.2 copy-start.6
  56.4 101.9 %all-gather.5.cloned.1.call-start = ((), (), s32[]{:S(2)}) async-start(), calls=%async_computation.2 | async-start | bytes 3538944 | tf_op jit(solution)/shard_map/all_gather | solution.py:297
  59.9 4.2 %copy-start.1 = (bf16[1024,1024]{1,0:T(8,128)(2,1)}, bf16[1024,1024]{1,0:T(8,128)(2,1)S(1)}, u32[]{:S(2)}) copy-start(bf16[1024,1024]{1,0:T(8,128)(2,1)S(1)} %pad_maximum_fusion.refs_0_.refs_6_.refs_9_.refs_15_) | copy-start | bytes 6291460
  59.9 8.5 %collective-permute-start.5 = (bf16[1024,1024]{1,0:T(8,128)(2,1)S(1)}, bf16[1024,1024]{1,0:T(8,128)(2,1)S(1)}, u32[]{:S(2)}, u32[]{:S(2)}) collective-permute-start(bf16[1024,1024]{1,0:T(8,128)(2,1)S(1)} %pad_maximum_fusion.refs_0_.refs_6_.refs_9_.refs_15_), channel_id=1, source_target_pairs={{0,2},{2,0},{4,6},{6,4},{8,10},{10,8},{12,14},{14,12},{16,18},{18,... | collective-permute-start | bytes 6291464 | tf_op jit(solution)/shard_map/ppermute | solution.py:273
  60.0 8.4 %collective-permute-start.6 = (bf16[1024,1024]{1,0:T(8,128)(2,1)S(1)}, bf16[1024,1024]{1,0:T(8,128)(2,1)S(1)}, u32[]{:S(2)}, u32[]{:S(2)}) collective-permute-start(bf16[1024,1024]{1,0:T(8,128)(2,1)S(1)} %pad_maximum_fusion.refs_0_.refs_6_.refs_9_.refs_15_), channel_id=1, source_target_pairs={{2,4},{4,2},{10,12},{12,10},{18,20},{20,18},{26,28},{28,26},{3,5},... | collective-permute-start | bytes 6291464 | tf_op jit(solution)/shard_map/ppermute | solution.py:273
  61.9 5.8 %copy-start.21 = (s32[1,27]{1,0:T(1,128)S(1)}, s32[1,27]{1,0:T(1,128)}, u32[]{:S(2)}) copy-start(s32[1,27]{1,0:T(1,128)} %param.8) | copy-start | bytes 328
  64.1 44.6 %collective-permute-start.13 = (bf16[1024,512]{1,0:T(8,128)(2,1)}, bf16[1024,512]{1,0:T(8,128)(2,1)}, u32[]{:S(2)}, u32[]{:S(2)}) collective-permute-start(bf16[1024,512]{1,0:T(8,128)(2,1)} %pad_maximum_fusion.1.refs_0_.refs_6_.refs_9_.refs_15_), channel_id=1, source_target_pairs={{0,2},{2,0},{4,6},{6,4},{8,10},{10,8},{12,14},{14,12},{16,18},{18,... | collective-permute-start | bytes 3145736 | tf_op jit(solution)/shard_map/ppermute | solution.py:273
  66.1 44.7 %collective-permute-start.14 = (bf16[1024,512]{1,0:T(8,128)(2,1)}, bf16[1024,512]{1,0:T(8,128)(2,1)}, u32[]{:S(2)}, u32[]{:S(2)}) collective-permute-start(bf16[1024,512]{1,0:T(8,128)(2,1)} %pad_maximum_fusion.1.refs_0_.refs_6_.refs_9_.refs_15_), channel_id=1, source_target_pairs={{2,4},{4,2},{10,12},{12,10},{18,20},{20,18},{26,28},{28,26},{3,5},... | collective-permute-start | bytes 3145736 | tf_op jit(solution)/shard_map/ppermute | solution.py:273
  68.4 1.4 copy-start.2
  69.8 1.3 copy-start.3
  80.0 32.3 %collective-permute-start.7 = (bf16[256,512]{1,0:T(8,128)(2,1)}, bf16[256,512]{1,0:T(8,128)(2,1)S(1)}, u32[]{:S(2)}, u32[]{:S(2)}) collective-permute-start(bf16[256,512]{1,0:T(8,128)(2,1)} %shard_map.55.refs_0_), channel_id=1, source_target_pairs={{0,4},{2,6},{4,0},{6,2},{8,12},{10,14},{12,8},{14,10},{16,20},{18,... | collective-permute-start | bytes 786440 | tf_op jit(solution)/shard_map/ppermute | solution.py:273
  98.3 14.2 %collective-permute-start.8 = (bf16[256,512]{1,0:T(8,128)(2,1)}, bf16[256,512]{1,0:T(8,128)(2,1)S(1)}, u32[]{:S(2)}, u32[]{:S(2)}) collective-permute-start(bf16[256,512]{1,0:T(8,128)(2,1)} %shard_map.55.refs_0_), channel_id=1, source_target_pairs={{0,1},{1,0},{2,3},{3,2},{4,5},{5,4},{6,7},{7,6},{8,9},{9,8},{10,11... | collective-permute-start | bytes 786440 | tf_op jit(solution)/shard_map/ppermute | solution.py:312
  99.9 12.7 %collective-permute-start.9 = (bf16[256,512]{1,0:T(8,128)(2,1)}, bf16[256,512]{1,0:T(8,128)(2,1)S(1)}, u32[]{:S(2)}, u32[]{:S(2)}) collective-permute-start(bf16[256,512]{1,0:T(8,128)(2,1)} %shard_map.55.refs_0_), channel_id=1, source_target_pairs={{0,5},{1,4},{2,7},{3,6},{4,1},{5,0},{6,3},{7,2},{8,13},{9,12},{10,... | collective-permute-start | bytes 786440 | tf_op jit(solution)/shard_map/ppermute | solution.py:313
  108.7 17.4 %collective-permute-start.10 = (bf16[256,512]{1,0:T(8,128)(2,1)}, bf16[256,512]{1,0:T(8,128)(2,1)S(1)}, u32[]{:S(2)}, u32[]{:S(2)}) collective-permute-start(bf16[256,512]{1,0:T(8,128)(2,1)} %shard_map.56.refs_4_), channel_id=1, source_target_pairs={{0,4},{2,6},{4,0},{6,2},{8,12},{10,14},{12,8},{14,10},{16,20},{18,... | collective-permute-start | bytes 786440 | tf_op jit(solution)/shard_map/ppermute | solution.py:273
  110.8 16.2 %collective-permute-start.11 = (bf16[256,512]{1,0:T(8,128)(2,1)}, bf16[256,512]{1,0:T(8,128)(2,1)S(1)}, u32[]{:S(2)}, u32[]{:S(2)}) collective-permute-start(bf16[256,512]{1,0:T(8,128)(2,1)} %shard_map.56.refs_4_), channel_id=1, source_target_pairs={{0,1},{1,0},{2,3},{3,2},{4,5},{5,4},{6,7},{7,6},{8,9},{9,8},{10,11... | collective-permute-start | bytes 786440 | tf_op jit(solution)/shard_map/ppermute | solution.py:312
  112.3 0.7 copy-start.12
  112.3 14.7 %collective-permute-start.12 = (bf16[256,512]{1,0:T(8,128)(2,1)}, bf16[256,512]{1,0:T(8,128)(2,1)S(1)}, u32[]{:S(2)}, u32[]{:S(2)}) collective-permute-start(bf16[256,512]{1,0:T(8,128)(2,1)} %shard_map.56.refs_4_), channel_id=1, source_target_pairs={{0,5},{1,4},{2,7},{3,6},{4,1},{5,0},{6,3},{7,2},{8,13},{9,12},{10,... | collective-permute-start | bytes 786440 | tf_op jit(solution)/shard_map/ppermute | solution.py:313
  112.6 0.7 copy-start.13
  113.3 0.7 copy-start.14
  122.9 9.4 %collective-permute-start.15 = (bf16[256,512]{1,0:T(8,128)(2,1)}, bf16[256,512]{1,0:T(8,128)(2,1)S(1)}, u32[]{:S(2)}, u32[]{:S(2)}) collective-permute-start(bf16[256,512]{1,0:T(8,128)(2,1)} %shard_map.57.refs_8_), channel_id=1, source_target_pairs={{0,4},{2,6},{4,0},{6,2},{8,12},{10,14},{12,8},{14,10},{16,20},{18,... | collective-permute-start | bytes 786440 | tf_op jit(solution)/shard_map/ppermute | solution.py:273
  124.6 12.3 %collective-permute-start.16 = (bf16[256,512]{1,0:T(8,128)(2,1)}, bf16[256,512]{1,0:T(8,128)(2,1)S(1)}, u32[]{:S(2)}, u32[]{:S(2)}) collective-permute-start(bf16[256,512]{1,0:T(8,128)(2,1)} %shard_map.57.refs_8_), channel_id=1, source_target_pairs={{0,1},{1,0},{2,3},{3,2},{4,5},{5,4},{6,7},{7,6},{8,9},{9,8},{10,11... | collective-permute-start | bytes 786440 | tf_op jit(solution)/shard_map/ppermute | solution.py:312
  126.2 11.9 %copy-start.15 = (bf16[256,512]{1,0:T(8,128)(2,1)}, bf16[256,512]{1,0:T(8,128)(2,1)S(1)}, u32[]{:S(2)}) copy-start(bf16[256,512]{1,0:T(8,128)(2,1)S(1)} %collective-permute-done.10.refs_5_) | copy-start | bytes 786436
  126.2 11.9 %collective-permute-start.17 = (bf16[256,512]{1,0:T(8,128)(2,1)}, bf16[256,512]{1,0:T(8,128)(2,1)S(1)}, u32[]{:S(2)}, u32[]{:S(2)}) collective-permute-start(bf16[256,512]{1,0:T(8,128)(2,1)} %shard_map.57.refs_8_), channel_id=1, source_target_pairs={{0,5},{1,4},{2,7},{3,6},{4,1},{5,0},{6,3},{7,2},{8,13},{9,12},{10,... | collective-permute-start | bytes 786440 | tf_op jit(solution)/shard_map/ppermute | solution.py:313
  127.0 11.1 %copy-start.16 = (bf16[256,512]{1,0:T(8,128)(2,1)}, bf16[256,512]{1,0:T(8,128)(2,1)S(1)}, u32[]{:S(2)}) copy-start(bf16[256,512]{1,0:T(8,128)(2,1)S(1)} %collective-permute-done.11.refs_6_) | copy-start | bytes 786436
  127.0 11.1 %copy-start.17 = (bf16[256,512]{1,0:T(8,128)(2,1)}, bf16[256,512]{1,0:T(8,128)(2,1)S(1)}, u32[]{:S(2)}) copy-start(bf16[256,512]{1,0:T(8,128)(2,1)S(1)} %collective-permute-done.12.refs_7_) | copy-start | bytes 786436
  132.3 5.8 %copy-start.18 = (bf16[256,512]{1,0:T(8,128)(2,1)}, bf16[256,512]{1,0:T(8,128)(2,1)S(1)}, u32[]{:S(2)}) copy-start(bf16[256,512]{1,0:T(8,128)(2,1)S(1)} %collective-permute-done.15.refs_9_) | copy-start | bytes 786436
  136.9 1.2 copy-start.19
  138.0 0.7 copy-start.20
  147.6 13.5 %collective-permute-start.18 = (bf16[256,1024]{1,0:T(8,128)(2,1)}, bf16[256,1024]{1,0:T(8,128)(2,1)S(1)}, u32[]{:S(2)}, u32[]{:S(2)}) collective-permute-start(bf16[256,1024]{1,0:T(8,128)(2,1)} %get-tuple-element.34), channel_id=1, source_target_pairs={{0,4},{2,6},{4,0},{6,2},{8,12},{10,14},{12,8},{14,10},{16,20},{18,... | collective-permute-start | bytes 1572872 | tf_op jit(solution)/shard_map/ppermute | solution.py:273
  161.1 0.8 copy-start.7
  167.9 1.5 copy-start.11
  167.9 7.0 %collective-permute-start.19 = (bf16[256,512]{1,0:T(8,128)(2,1)}, bf16[256,512]{1,0:T(8,128)(2,1)S(1)}, u32[]{:S(2)}, u32[]{:S(2)}) collective-permute-start(bf16[256,512]{1,0:T(8,128)(2,1)} %get-tuple-element.36), channel_id=1, source_target_pairs={{0,4},{2,6},{4,0},{6,2},{8,12},{10,14},{12,8},{14,10},{16,20},{18,... | collective-permute-start | bytes 786440 | tf_op jit(solution)/shard_map/ppermute | solution.py:273
Sparse Core Ops, SparseCore 0:
  56.5 63.1 all-gather.2
  121.3 36.9 all-gather.4

commit v4 on v0

--- a/solution.py
+++ b/solution.py
@@ -1,11 +1,17 @@
+import functools
+
 import jax
 import jax.numpy as jnp
 from jax import lax
+from jax.experimental import pallas as pl
+from jax.experimental.pallas import tpu as pltpu
 from jax.sharding import PartitionSpec as P
 
 HEAD_DIM = 128
 GH = 4
 GW = 4
+LOG2E = 1.4426950408889634
+DEAD = -1e30
 
 
 def passed_along(array, axis, by):
@@ -35,7 +41,7 @@
     return (new_max, run_sum, run_acc)
 
 
-def local(queries, keys, values, window, out_weight):
+def local_general(queries, keys, values, window, out_weight):
     tok_rows = queries.shape[0]
     head_width = HEAD_DIM
     heads_all = queries.shape[1] // head_width
@@ -102,7 +108,268 @@
     return projected.astype(jnp.bfloat16)
 
 
+VMEM_LIMIT = 56 * 2**20
+
+
+def attend_kernel(listed, q_ref, *refs):
+    o_ref = refs[-1]
+    keys, values = refs[:9], refs[9:18]
+    coef = HEAD_DIM**-0.5 * LOG2E
+    toward = 1 - 2 * (listed[27] & 1)
+    for head in range(q_ref.shape[1] // HEAD_DIM):
+        at = slice(head * HEAD_DIM, (head + 1) * HEAD_DIM)
+        q = q_ref[:, at]
+        top = total = acc = None
+        for r in (1, 0, 2):
+            scores, lives = [], []
+            new = top
+            for k, step in enumerate((0, toward, -toward)):
+                s = lax.dot_general(
+                    keys[3 * r + k][:, at], q, (((1,), (1,)), ((), ())), preferred_element_type=jnp.float32
+                )
+                live = listed[10 + 3 * r + step] >= 0
+                scores.append(s)
+                lives.append(live)
+                high = jnp.where(live, jnp.max(s, axis=0, keepdims=True), DEAD)
+                new = high if new is None else jnp.maximum(new, high)
+            weights, part = [], None
+            for s, live in zip(scores, lives):
+                w = jnp.exp2((s - jnp.where(live, new, -DEAD)) * coef)
+                w_sum = jnp.sum(w, axis=0, keepdims=True)
+                part = w_sum if part is None else part + w_sum
+                weights.append(w.astype(jnp.bfloat16))
+            sides = jnp.concatenate([values[3 * r + k][:, at].T for k in range(3)], axis=1)
+            pv = jnp.dot(sides, jnp.concatenate(weights, axis=0), preferred_element_type=jnp.float32)
+            if top is None:
+                total, acc = part, pv
+            else:
+                again = jnp.exp2((top - new) * coef)
+                total = total * again + part
+                acc = acc * again + pv
+            top = new
+        o_ref[:, at] = (acc / total).astype(jnp.bfloat16).T
+
+
+AT_ONCE = 2
+
+
+def attend_tile(listed, q, head, count, first, own, rows, before):
+    tile = q.shape[0]
+
+    def spec(block, at=first):
+        return pl.BlockSpec((tile, AT_ONCE * HEAD_DIM), lambda h, listed: (block, at // AT_ONCE + h))
+
+    return pl.pallas_call(
+        attend_kernel,
+        out_shape=jax.ShapeDtypeStruct((tile, count * HEAD_DIM), jnp.bfloat16),
+        grid_spec=pltpu.PrefetchScalarGridSpec(
+            num_scalar_prefetch=1,
+            grid=(count // AT_ONCE,),
+            in_specs=[spec(0, head)]
+            + [spec(0)] * 3
+            + [spec(0, head)] * 3
+            + [spec(2)] * 3
+            + [spec(1)] * 3
+            + [spec(1, head)] * 3
+            + [spec(3)] * 3
+            + [pl.BlockSpec(memory_space=pl.ANY)] * len(before),
+            out_specs=pl.BlockSpec((tile, AT_ONCE * HEAD_DIM), lambda h, listed: (0, h)),
+        ),
+        compiler_params=pltpu.CompilerParams(vmem_limit_bytes=VMEM_LIMIT),
+        cost_estimate=pl.CostEstimate(flops=1, bytes_accessed=1, transcendentals=0),
+    )(listed, q, *rows, *own, *rows, *rows, *own, *rows, *before)
+
+
+def gather_kernel(spot, *refs):
+    pieces, a_ref, sems = refs[:-2], refs[-2], refs[-1]
+    tile = a_ref.shape[0] // 2
+    side_width = a_ref.shape[1] // 2
+    copies, at = [], 0
+    for i, piece in enumerate(pieces):
+        wide = piece.shape[1]
+        col = (spot[0] if i % 4 < 2 else 1 - spot[0]) * side_width + at
+        dst = a_ref.at[pl.ds(i % 2 * tile, tile), pl.ds(pl.multiple_of(col, 128), wide)]
+        copies.append(pltpu.make_async_copy(piece, dst, sems.at[i]))
+        at += wide if i % 4 == 3 else 0
+    for c in copies:
+        c.start()
+    for c in copies:
+        c.wait()
+
+
+def gather_heads(spot, pieces):
+    rows, width = 2 * pieces[0].shape[0], 2 * sum(p.shape[1] for p in pieces[::4])
+    return pl.pallas_call(
+        gather_kernel,
+        out_shape=pltpu.VMEM((rows, width), jnp.bfloat16),
+        in_specs=[pl.BlockSpec(memory_space=pltpu.SMEM)] + [pl.BlockSpec(memory_space=pl.ANY)] * len(pieces),
+        out_specs=pl.BlockSpec(memory_space=pltpu.VMEM),
+        scratch_shapes=[pltpu.SemaphoreType.DMA((len(pieces),))],
+        compiler_params=pltpu.CompilerParams(vmem_limit_bytes=VMEM_LIMIT),
+        cost_estimate=pl.CostEstimate(flops=0, bytes_accessed=4 * rows * width, transcendentals=0),
+    )(spot, *pieces)
+
+
+def project_kernel(planes, at, spot, a_ref, *refs):
+    blocks, (here, there, w_ref, acc, sems) = refs[:12], refs[12:]
+    tile = a_ref.shape[0] // 2
+    cols = w_ref.shape[1]
+    shard = w_ref.shape[0] // (planes * GW)
+    block = GW * shard
+    plane, core = spot[2], spot[3]
+    last = planes - 1
+
+    def copies(i, source):
+        for j in range(2):
+            side = core if j == 0 else 1 - core
+            for x in range(2):
+                src = blocks[2 * i + j].at[pl.ds(x * shard, shard), pl.ds(at, cols)]
+                row = pl.multiple_of(source * block + (2 * x + side) * shard, shard)
+                yield pltpu.make_async_copy(src, w_ref.at[pl.ds(row, shard), :], sems.at[4 * i + 2 * j + x])
+
+    middle = (plane > 0) & (plane < last)
+    wanted = (
+        (0, plane, None),
+        (1, plane - 1, plane > 0),
+        (2, plane + 1, plane < last),
+        (3, jnp.where(plane == 1, 3, 0), middle),
+        (4, jnp.where(plane == 0, 2, 1), jnp.logical_not(middle)),
+        (5, last - plane, jnp.logical_not(middle)),
+    )
+
+    def each(act):
+        for i, source, when in wanted:
+            if when is None:
+                for c in copies(i, source):
+                    act(c)
+            else:
+
+                @pl.when(when)
+                def _():
+                    for c in copies(i, source):
+                        act(c)
+
+    each(lambda c: c.start())
+    each(lambda c: c.wait())
+    acc[...] = jnp.dot(a_ref[...], w_ref[...], preferred_element_type=jnp.float32)
+    here[...] = acc[:tile, :].astype(jnp.bfloat16)
+    there[...] = acc[tile:, :].astype(jnp.bfloat16)
+
+
+def project(spot, a, blocks, at, cols, planes):
+    rows, deep = a.shape
+    vmem, hbm = pl.BlockSpec(memory_space=pltpu.VMEM), pl.BlockSpec(memory_space=pltpu.HBM)
+    return pl.pallas_call(
+        functools.partial(project_kernel, planes, at),
+        out_shape=[jax.ShapeDtypeStruct((rows // 2, cols), jnp.bfloat16)] * 2,
+        in_specs=[pl.BlockSpec(memory_space=pltpu.SMEM), vmem] + [hbm] * len(blocks),
+        out_specs=[vmem] * 2,
+        scratch_shapes=[
+            pltpu.VMEM((deep, cols), jnp.bfloat16),
+            pltpu.VMEM((rows, cols), jnp.float32),
+            pltpu.SemaphoreType.DMA((24,)),
+        ],
+        compiler_params=pltpu.CompilerParams(vmem_limit_bytes=VMEM_LIMIT // 4),
+        cost_estimate=pl.CostEstimate(
+            flops=2 * rows * deep * cols,
+            bytes_accessed=2 * (rows * deep + deep * cols + rows * cols),
+            transcendentals=0,
+        ),
+    )(spot, a, *blocks)
+
+
+def local_plane(queries, keys, values, window, out_weight):
+    span = lax.axis_size("seq")
+    planes = span // GW
+    down = [(i, i + GW) for i in range(span - GW)]
+    up = [(i + GW, i) for i in range(span - GW)]
+    mates = [(i, i ^ 1) for i in range(span)]
+    outer = [(i, i ^ 3) for i in range(span) if i % GW in (1, 2)]
+    partners = [(i, i ^ 2) for i in range(span)]
+    seq, side = lax.axis_index("seq"), lax.axis_index("head")
+    half = seq // 2 % 2
+    tile, own_width = keys.shape
+    heads = own_width // HEAD_DIM
+
+    def move(array, pairs):
+        return lax.ppermute(array, "seq", pairs)
+
+    def in_order(flag, own, other, axis):
+        return jnp.where(
+            flag == 0, jnp.concatenate([own, other], axis=axis), jnp.concatenate([other, own], axis=axis)
+        )
+
+    def line(array):
+        return [array, move(array, mates), move(array, outer)]
+
+    kv = jnp.concatenate([keys, values], axis=0)
+    kv_up, kv_dn = move(kv, down), move(kv, up)
+    q_own = lax.dynamic_slice_in_dim(queries, side * own_width, own_width, 1)
+    q_else = lax.dynamic_slice_in_dim(queries, (1 - side) * own_width, own_width, 1)
+    q = in_order(side, q_own, lax.ppermute(q_else, "head", [(0, 1), (1, 0)]), 0)
+
+    cols = out_weight.shape[1] // 2
+    w_mine = lax.dynamic_slice_in_dim(out_weight, half * cols, cols, 1)
+    w_theirs = move(lax.dynamic_slice_in_dim(out_weight, (1 - half) * cols, cols, 1), partners)
+    w_own = in_order(half, w_mine, w_theirs, 0)
+
+    kv, w_own = lax.optimization_barrier((kv, w_own))
+    own = line(kv)
+
+    kv_up, kv_dn, own, q, w_own = lax.optimization_barrier((kv_up, kv_dn, own, q, w_own))
+    plane = seq // GW
+    w_up, w_dn = move(w_own, down), move(w_own, up)
+    w_mate = move(w_own, mates)
+
+    part = heads // 3
+    cuts = [0, 2 * part * HEAD_DIM, own_width]
+    rows = [
+        line(jnp.concatenate([kv_up[:, lo:hi], kv_dn[:, lo:hi]], axis=0)) for lo, hi in zip(cuts[:-1], cuts[1:])
+    ]
+
+    def between(*pairs):
+        return [(a * GW + c, b * GW + c) for a, b in pairs for c in range(GW)]
+
+    w_own, w_up, w_dn = lax.optimization_barrier((w_own, w_up, w_dn))
+    blocks = [w_own, w_mate, w_up, move(w_up, mates), w_dn, move(w_dn, mates)]
+    for far in (
+        move(w_own, between((0, 2), (3, 1))),
+        move(jnp.where(plane == planes - 2, w_up, w_dn), between((2, 3), (1, 0))),
+        move(w_own, between((0, 3), (3, 0))),
+    ):
+        blocks += [far, move(far, mates)]
+
+    listed = jnp.concatenate([window[0], seq[None]])
+    pieces = []
+    for n, (held, first) in enumerate(((0, 0), (0, part), (1, 0))):
+        mine = attend_tile(listed, q, n * part, part, first, own, rows[held], pieces[1:2] if n == 2 else [])
+        pieces += [
+            mine,
+            move(mine, partners),
+            lax.ppermute(mine, "head", [(0, 1), (1, 0)]),
+            lax.ppermute(mine, ("seq", "head"), [(2 * i + y, 2 * (i ^ 2) + 1 - y) for i in range(span) for y in (0, 1)]),
+        ]
+
+    spot = jnp.stack([side, half, plane, seq % 2])
+    made, sent = [], []
+    third = cols // 3
+    attended = gather_heads(spot, pieces)
+    for at in range(0, cols, third):
+        here, there = project(spot, attended, blocks, at, third, planes)
+        made.append(here)
+        sent.append(move(there, partners))
+    return in_order(half, jnp.concatenate(made, axis=1), jnp.concatenate(sent, axis=1), 1)
+
+
 def solution(mesh):
+    span, sides = mesh.shape["seq"], mesh.shape["head"]
+
+    def local(queries, keys, values, window, out_weight):
+        one_step = span == GH * GW and sides == 2
+        even = keys.shape[1] % (3 * HEAD_DIM) == 0 and out_weight.shape[1] % 1536 == 0
+        which = local_plane if one_step and even else local_general
+        return which(queries, keys, values, window, out_weight)
+
     in_specs = (
         P(("seq", "head"), None),
         P("seq", "head"),

time: 325 us -> 179 us (0.55)
  waiting for transfers between devices: 218 us -> 71.1 us
  Pallas kernels: 0 us -> 41.5 us
  matrix products: 40 us -> 0 us
  between operations: 13.6 us -> 0.4 us
  starting transfers between devices: 34.8 us -> 46.6 us
  local copies, waits for them, and re-layouts: 5.53 us -> 9.28 us
  other arithmetic: 12.8 us -> 9.13 us
    all_gather x2 -> x0, waiting for transfers between devices: 137 us -> none  [the longest x1 101 us: local(): lax.all_gather(out_weight, 'seq', axis=0, tiled=True)]
    pallas_call x0 -> x7, Pallas kernels: none -> 41.5 us  [the longest x3 25.8 us: attend_tile(): pl.pallas_call(attend_kernel, out_shape=jax.ShapeDtypeStruct((tile, count...]
    dot_general x7 -> x0, matrix products: 40 us -> none  [the longest x3 16.9 us: attend_block(): jnp.einsum('qhk,khd->qhd', weights.astype(jnp.bfloat16), kv_block[1], pre...]
    ppermute x4 -> x33, starting transfers between devices: 31 us -> 46.6 us  [the longest x26 35.7 us: move(): return lax.ppermute(array, 'seq', pairs)]
    reduce_sum x2 -> x0, other arithmetic: 10.1 us -> none  [attend_block(): run_sum = run_sum * rescale + jnp.sum(weights, axis=-1)]
    all_to_all x1 -> x0, waiting for transfers between devices: 7.36 us -> none  [local(): lax.all_to_all(queries.reshape(tok_rows, heads_all, head_width), 'head',...]
    select_n x0 -> x4, other arithmetic: none -> 5.33 us  [the longest x3 5.21 us: in_order(): jnp.where(flag == 0, jnp.concatenate([own, other], axis=axis), jnp.concat...]
    slice x1 -> x4, local copies, waits for them, and re-layouts: 0.08 us -> 4.74 us  [the longest x2 2.37 us: local_plane(): kv_up[:, lo:hi]]
  transfers between devices with their start and end apart: 7 -> 33, of which waited for: 7 -> 14; matrix products, arithmetic and copies ran while one was open for 4% -> 8% of each run, Pallas kernels for 0% -> 21%
where the time goes in v4:
time: 179 us; the launch traced here: 178 us
  waiting for transfers between devices  71.1 us (40%)
  starting transfers between devices  46.6 us (26%)
  Pallas kernels  41.5 us (23%)
  local copies, waits for them, and re-layouts  9.28 us (5%)
  other arithmetic  9.13 us (5%)
    ppermute x26, waiting for transfers between devices, move(): return lax.ppermute(array, 'seq', pairs)  50.8 us
    ppermute x26, starting transfers between devices, move(): return lax.ppermute(array, 'seq', pairs)  35.7 us
    pallas_call x3, Pallas kernels, attend_tile(): pl.pallas_call(attend_kernel, out_shape=jax.ShapeDtypeStruct((tile, count...  25.8 us
    pallas_call x3, Pallas kernels, project(): pl.pallas_call(functools.partial(project_kernel, planes, at), out_shape=[...  13 us
    ppermute x1, waiting for transfers between devices, local_plane(): q = in_order(side, q_own, lax.ppermute(q_else, 'head', [(0, 1), (1, 0)]), 0)  9.4 us
    ppermute x3, waiting for transfers between devices, local_plane(): lax.ppermute(mine, ('seq', 'head'), [(2 * i + y, 2 * (i ^ 2) + 1 - y) for...  8.18 us
    ppermute x3, starting transfers between devices, local_plane(): lax.ppermute(mine, ('seq', 'head'), [(2 * i + y, 2 * (i ^ 2) + 1 - y) for...  6.55 us
    select_n x3, other arithmetic, in_order(): jnp.where(flag == 0, jnp.concatenate([own, other], axis=axis), jnp.concat...  5.21 us
  transfers between devices with their start and end apart: 33, of which 14 were waited for; matrix products, arithmetic and copies ran while one was open for 8% of the time, Pallas kernels for 21%

profile of v4, /device:TPU:0, one launch (start us, length us, event | category | flops | bytes accessed | tf_op | source)
XLA Modules:
  0.0 178.0 jit_solution(14826647405559175428)
XLA Ops:
  0.0 2.3 %constant_dynamic-slice_fusion.3 = (bf16[192,1536]{1,0:T(8,128)(2,1)S(1)}, bf16[192,1536]{1,0:T(8,128)(2,1)}) fusion(bf16[192,3072]{1,0:T(8,128)(2,1)} %param.9, s32[]{:T(128)S(6)} %select_n.66, s32[]{:T(128)S(6)} %select_n.67), kind=kLoop, calls=%fused_computation.23 | loop fusion | bytes 2359304 | tf_op jit(solution)/shard_map/dynamic_slice | solution.py:312
  2.3 2.9 %collective-permute-start.2 = (bf16[192,1536]{1,0:T(8,128)(2,1)}, bf16[192,1536]{1,0:T(8,128)(2,1)}, u32[]{:S(2)}, u32[]{:S(2)}) collective-permute-start(bf16[192,1536]{1,0:T(8,128)(2,1)} %get-tuple-element.42), channel_id=1, source_target_pairs={{0,4},{2,6},{4,0},{6,2},{8,12},{10,14},{12,8},{14,10},{16,20},{18,... | collective-permute-start | bytes 1769480 | tf_op jit(solution)/shard_map/ppermute | solution.py:295
  5.3 4.6 %collective-permute-start = (bf16[512,1536]{1,0:T(8,128)(2,1)S(1)}, bf16[512,1536]{1,0:T(8,128)(2,1)}, u32[]{:S(2)}, u32[]{:S(2)}) collective-permute-start(bf16[512,1536]{1,0:T(8,128)(2,1)S(1)} %constant_dynamic-update-slice_fusion.refs_3_.refs_12_), channel_id=1, source_target_pairs={{0,8},{2,10},{4,12},{6,14},{8,16},{10,18},{12,20},{14,22},{16,24},... | collective-permute-start | bytes 4718600 | tf_op jit(solution)/shard_map/ppermute | solution.py:295
  10.0 1.3 collective-permute-start.1
  11.3 7.6 %collective-permute-done.2 = bf16[192,1536]{1,0:T(8,128)(2,1)} collective-permute-done((bf16[192,1536]{1,0:T(8,128)(2,1)}, bf16[192,1536]{1,0:T(8,128)(2,1)}, u32[]{:S(2)}, u32[]{:S(2)}) %collective-permute-start.2) | collective-permute-done | bytes 589856 | tf_op jit(solution)/shard_map/ppermute | solution.py:295
  18.8 1.7 maximum_select_fusion.refs_0_
  20.5 0.1 collective-permute-start.3
  20.6 1.9 %collective-permute-start.4 = (bf16[512,1536]{1,0:T(8,128)(2,1)S(1)}, bf16[512,1536]{1,0:T(8,128)(2,1)}, u32[]{:S(2)}, u32[]{:S(2)}) collective-permute-start(bf16[512,1536]{1,0:T(8,128)(2,1)S(1)} %constant_dynamic-update-slice_fusion.refs_3_.refs_12_), channel_id=1, source_target_pairs={{2,4},{4,2},{10,12},{12,10},{18,20},{20,18},{26,28},{28,26},{3,5},... | collective-permute-start | bytes 4718600 | tf_op jit(solution)/shard_map/ppermute | solution.py:295
  22.5 1.2 constant_dynamic-slice_fusion.1
  23.7 1.8 %collective-permute-start.5 = (bf16[128,1536]{1,0:T(8,128)(2,1)S(1)}, bf16[128,1536]{1,0:T(8,128)(2,1)}, u32[]{:S(2)}, u32[]{:S(2)}) collective-permute-start(bf16[128,1536]{1,0:T(8,128)(2,1)S(1)} %get-tuple-element.44), channel_id=1, source_target_pairs={{0,1},{1,0},{2,3},{3,2},{4,5},{5,4},{6,7},{7,6},{8,9},{9,8},{10,11... | collective-permute-start | bytes 1179656 | tf_op jit(solution)/shard_map/ppermute | solution.py:309
  25.5 9.4 %collective-permute-done.5 = bf16[128,1536]{1,0:T(8,128)(2,1)} collective-permute-done((bf16[128,1536]{1,0:T(8,128)(2,1)S(1)}, bf16[128,1536]{1,0:T(8,128)(2,1)}, u32[]{:S(2)}, u32[]{:S(2)}) %collective-permute-start.5) | collective-permute-done | bytes 393248 | tf_op jit(solution)/shard_map/ppermute | solution.py:309
  34.9 2.2 %maximum_select_fusion.1.q_ref = bf16[256,1536]{1,0:T(8,128)(2,1)} fusion(bf16[128,1536]{1,0:T(8,128)(2,1)} %collective-permute-done.5, bf16[128,1536]{1,0:T(8,128)(2,1)S(1)} %get-tuple-element.43, pred[]{:T(512)S(6)} %eq.14), kind=kLoop, calls=%fused_computation.5 | loop fusion | flops 3538944 | bytes 1572865 | tf_op jit(solution)/shard_map/jit(_where)/select_n | solution.py:298
  37.1 5.1 %collective-permute-done = bf16[512,1536]{1,0:T(8,128)(2,1)} collective-permute-done((bf16[512,1536]{1,0:T(8,128)(2,1)S(1)}, bf16[512,1536]{1,0:T(8,128)(2,1)}, u32[]{:S(2)}, u32[]{:S(2)}) %collective-permute-start) | collective-permute-done | bytes 1572896 | tf_op jit(solution)/shard_map/ppermute | solution.py:295
  42.2 5.4 %collective-permute-done.1 = bf16[512,1536]{1,0:T(8,128)(2,1)} collective-permute-done((bf16[512,1536]{1,0:T(8,128)(2,1)S(1)}, bf16[512,1536]{1,0:T(8,128)(2,1)}, u32[]{:S(2)}, u32[]{:S(2)}) %collective-permute-start.1) | collective-permute-done | bytes 1572896 | tf_op jit(solution)/shard_map/ppermute | solution.py:295
  47.5 2.4 %collective-permute-start.19 = (bf16[384,1536]{1,0:T(8,128)(2,1)S(1)}, bf16[384,1536]{1,0:T(8,128)(2,1)S(1)}, u32[]{:S(2)}, u32[]{:S(2)}) collective-permute-start(bf16[384,1536]{1,0:T(8,128)(2,1)S(1)} %maximum_select_fusion.refs_0_), channel_id=1, source_target_pairs={{0,8},{2,10},{4,12},{6,14},{8,16},{10,18},{12,20},{14,22},{16,24},... | collective-permute-start | bytes 3538952 | tf_op jit(solution)/shard_map/ppermute | solution.py:295
  50.0 1.3 collective-permute-start.20
  51.3 1.3 slice.13
  52.6 1.3 slice.12
  53.9 1.5 pad_maximum_fusion.refs_0_.refs_6_.refs_9_.refs_15_
  55.4 2.0 %collective-permute-start.7 = (bf16[1024,1024]{1,0:T(8,128)(2,1)}, bf16[1024,1024]{1,0:T(8,128)(2,1)}, u32[]{:S(2)}, u32[]{:S(2)}) collective-permute-start(bf16[1024,1024]{1,0:T(8,128)(2,1)} %pad_maximum_fusion.refs_0_.refs_6_.refs_9_.refs_15_), channel_id=1, source_target_pairs={{2,4},{4,2},{10,12},{12,10},{18,20},{20,18},{26,28},{28,26},{3,5},... | collective-permute-start | bytes 6291464 | tf_op jit(solution)/shard_map/ppermute | solution.py:295
  57.4 1.1 slice.15
  58.5 1.1 slice.14
  59.6 1.1 pad_maximum_fusion.1.refs_0_.refs_6_.refs_9_.refs_15_
  60.6 0.5 collective-permute-start.14
  61.2 12.5 %collective-permute-done.19.refs_2_ = bf16[384,1536]{1,0:T(8,128)(2,1)S(1)} collective-permute-done((bf16[384,1536]{1,0:T(8,128)(2,1)S(1)}, bf16[384,1536]{1,0:T(8,128)(2,1)S(1)}, u32[]{:S(2)}, u32[]{:S(2)}) %collective-permute-start.19) | collective-permute-done | bytes 1179680 | tf_op jit(solution)/shard_map/ppermute | solution.py:295
  73.6 4.2 %collective-permute-done.20.refs_4_ = bf16[384,1536]{1,0:T(8,128)(2,1)S(1)} collective-permute-done((bf16[384,1536]{1,0:T(8,128)(2,1)S(1)}, bf16[384,1536]{1,0:T(8,128)(2,1)S(1)}, u32[]{:S(2)}, u32[]{:S(2)}) %collective-permute-start.20) | collective-permute-done | bytes 1179680 | tf_op jit(solution)/shard_map/ppermute | solution.py:295
  77.8 1.6 collective-permute-start.15
  79.5 4.3 %collective-permute-start.24 = (bf16[384,1536]{1,0:T(8,128)(2,1)S(1)}, bf16[384,1536]{1,0:T(8,128)(2,1)}, u32[]{:S(2)}, u32[]{:S(2)}) collective-permute-start(bf16[384,1536]{1,0:T(8,128)(2,1)S(1)} %maximum_select_fusion.refs_0_), channel_id=1, source_target_pairs={{0,16},{2,18},{4,20},{6,22},{24,8},{26,10},{28,12},{30,14},{1,17},... | collective-permute-start | bytes 3538952 | tf_op jit(solution)/shard_map/ppermute | solution.py:295
  83.8 0.1 broadcast_select_fusion.1
  83.9 1.3 collective-permute-start.26
  85.2 4.5 %collective-permute-start.28 = (bf16[384,1536]{1,0:T(8,128)(2,1)S(1)}, bf16[384,1536]{1,0:T(8,128)(2,1)}, u32[]{:S(2)}, u32[]{:S(2)}) collective-permute-start(bf16[384,1536]{1,0:T(8,128)(2,1)S(1)} %maximum_select_fusion.refs_0_), channel_id=1, source_target_pairs={{0,24},{2,26},{4,28},{6,30},{24,0},{26,2},{28,4},{30,6},{1,25},{3,... | collective-permute-start | bytes 3538952 | tf_op jit(solution)/shard_map/ppermute | solution.py:295
  89.8 0.6 pad_add_fusion.1.listed
  90.4 8.6 %shard_map.55.refs_0_ = bf16[256,512]{1,0:T(8,128)(2,1)} custom-call(s32[28]{0:T(128)} %pad_add_fusion.1.listed, bf16[256,1536]{1,0:T(8,128)(2,1)} %maximum_select_fusion.1.q_ref, bf16[1024,1024]{1,0:T(8,128)(2,1)} %pad_maximum_fusion.refs_0_.refs_6_.refs_9_.refs_15_, bf16[1024,1024]{1,0:T(8,128)(2,1)} %collective-permute-done.6.refs_1_.refs_7_.refs_10_.refs_16_, ...), custom_call_target="tpu_custom_call" | custom-call | flops 1 | bytes 1 | tf_op jit(solution)/shard_map/pallas_call | solution.py:162
  99.0 0.8 collective-permute-start.8
  99.8 1.5 collective-permute-start.9
  101.3 8.6 %shard_map.56.refs_4_ = bf16[256,512]{1,0:T(8,128)(2,1)} custom-call(s32[28]{0:T(128)} %pad_add_fusion.1.listed, bf16[256,1536]{1,0:T(8,128)(2,1)} %maximum_select_fusion.1.q_ref, bf16[1024,1024]{1,0:T(8,128)(2,1)} %pad_maximum_fusion.refs_0_.refs_6_.refs_9_.refs_15_, bf16[1024,1024]{1,0:T(8,128)(2,1)} %collective-permute-done.6.refs_1_.refs_7_.refs_10_.refs_16_, ...), custom_call_target="tpu_custom_call" | custom-call | flops 1 | bytes 1 | tf_op jit(solution)/shard_map/pallas_call | solution.py:162
  109.9 1.3 collective-permute-start.10
  111.3 0.7 collective-permute-start.11
  112.0 8.2 %collective-permute-done.10.refs_3_ = bf16[256,512]{1,0:T(8,128)(2,1)S(1)} collective-permute-done((bf16[256,512]{1,0:T(8,128)(2,1)S(1)}, bf16[256,512]{1,0:T(8,128)(2,1)S(1)}, u32[]{:S(2)}, u32[]{:S(2)}) %collective-permute-start.10) | collective-permute-done | bytes 262176 | tf_op jit(solution)/shard_map/ppermute | solution.py:350
  120.2 0.5 collective-permute-start.12
  120.7 2.5 %collective-permute-done.11.refs_5_ = bf16[256,512]{1,0:T(8,128)(2,1)S(1)} collective-permute-done((bf16[256,512]{1,0:T(8,128)(2,1)}, bf16[256,512]{1,0:T(8,128)(2,1)S(1)}, u32[]{:S(2)}, u32[]{:S(2)}) %collective-permute-start.11) | collective-permute-done | bytes 262176 | tf_op jit(solution)/shard_map/ppermute | solution.py:295
  123.1 2.6 %collective-permute-start.13 = (bf16[256,512]{1,0:T(8,128)(2,1)}, bf16[256,512]{1,0:T(8,128)(2,1)S(1)}, u32[]{:S(2)}, u32[]{:S(2)}) collective-permute-start(bf16[256,512]{1,0:T(8,128)(2,1)} %shard_map.56.refs_4_), channel_id=1, source_target_pairs={{0,5},{1,4},{2,7},{3,6},{4,1},{5,0},{6,3},{7,2},{8,13},{9,12},{10,... | collective-permute-start | bytes 786440 | tf_op jit(solution)/shard_map/ppermute | solution.py:350
  125.8 8.6 %shard_map.57.refs_8_ = bf16[256,512]{1,0:T(8,128)(2,1)} custom-call(s32[28]{0:T(128)} %pad_add_fusion.1.listed, bf16[256,1536]{1,0:T(8,128)(2,1)} %maximum_select_fusion.1.q_ref, bf16[1024,512]{1,0:T(8,128)(2,1)} %pad_maximum_fusion.1.refs_0_.refs_6_.refs_9_.refs_15_, bf16[1024,512]{1,0:T(8,128)(2,1)} %collective-permute-done.14.refs_1_.refs_7_.refs_10_.refs_16_, ...), custom_call_target="tpu_custom_call" | custom-call | flops 1 | bytes 1 | tf_op jit(solution)/shard_map/pallas_call | solution.py:162
  134.4 0.4 collective-permute-start.16
  134.8 0.5 collective-permute-start.17
  135.3 2.6 %collective-permute-start.18 = (bf16[256,512]{1,0:T(8,128)(2,1)}, bf16[256,512]{1,0:T(8,128)(2,1)}, u32[]{:S(2)}, u32[]{:S(2)}) collective-permute-start(bf16[256,512]{1,0:T(8,128)(2,1)} %shard_map.57.refs_8_), channel_id=1, source_target_pairs={{0,5},{1,4},{2,7},{3,6},{4,1},{5,0},{6,3},{7,2},{8,13},{9,12},{10,... | collective-permute-start | bytes 786440 | tf_op jit(solution)/shard_map/ppermute | solution.py:350
  138.0 1.6 collective-permute-done.26.refs_8_
  139.6 0.5 collective-permute-start.23
  140.1 3.8 %collective-permute-done.16.refs_9_ = bf16[256,512]{1,0:T(8,128)(2,1)S(1)} collective-permute-done((bf16[256,512]{1,0:T(8,128)(2,1)}, bf16[256,512]{1,0:T(8,128)(2,1)S(1)}, u32[]{:S(2)}, u32[]{:S(2)}) %collective-permute-start.16) | collective-permute-done | bytes 262176 | tf_op jit(solution)/shard_map/ppermute | solution.py:295
  143.9 0.7 copy-done.11
  144.6 2.7 %collective-permute-done.17.refs_10_ = bf16[256,512]{1,0:T(8,128)(2,1)} collective-permute-done((bf16[256,512]{1,0:T(8,128)(2,1)}, bf16[256,512]{1,0:T(8,128)(2,1)}, u32[]{:S(2)}, u32[]{:S(2)}) %collective-permute-start.17) | collective-permute-done | bytes 262176 | tf_op jit(solution)/shard_map/ppermute | solution.py:349
  147.4 0.5 collective-permute-start.29
  147.9 0.6 pad_add_fusion.spot
  148.5 2.7 %shard_map.58.a_ref = bf16[512,3072]{1,0:T(8,128)(2,1)S(1)} custom-call(s32[4]{0:T(128)} %pad_add_fusion.spot, bf16[256,512]{1,0:T(8,128)(2,1)} %shard_map.55.refs_0_, bf16[256,512]{1,0:T(8,128)(2,1)} %copy-done.3, bf16[256,512]{1,0:T(8,128)(2,1)} %copy-done.6, bf16[256,512]{1,0:T(8,128)(2,1)} %copy-done.7, bf16[256,512]{1,0:T(8,128)(2,1)} %shard_map.56.refs_4_, ...), custom_call_target="tpu_custom_call" | custom-call | bytes 6291456 | tf_op jit(solution)/shard_map/pallas_call | solution.py:202
  151.2 1.0 collective-permute-done.29.refs_11_
  152.2 4.4 %shard_map.59 = (bf16[256,512]{1,0:T(8,128)(2,1)S(1)}, bf16[256,512]{1,0:T(8,128)(2,1)S(1)}) custom-call(s32[4]{0:T(128)S(1)} %copy-done, bf16[512,3072]{1,0:T(8,128)(2,1)S(1)} %shard_map.58.a_ref, bf16[384,1536]{1,0:T(8,128)(2,1)S(1)} %maximum_select_fusion.refs_0_, bf16[384,1536]{1,0:T(8,128)(2,1)} %collective-permute-done.21.refs_1_, ...), custom_call_target="tpu_custom_call" | custom-call | flops 1610612736 | bytes 6815744 | tf_op jit(solution)/shard_map/pallas_call | solution.py:262
  156.6 1.7 collective-permute-start.30
  158.3 4.3 %shard_map.60 = (bf16[256,512]{1,0:T(8,128)(2,1)S(1)}, bf16[256,512]{1,0:T(8,128)(2,1)S(1)}) custom-call(s32[4]{0:T(128)S(1)} %copy-done, bf16[512,3072]{1,0:T(8,128)(2,1)S(1)} %shard_map.58.a_ref, bf16[384,1536]{1,0:T(8,128)(2,1)S(1)} %maximum_select_fusion.refs_0_, bf16[384,1536]{1,0:T(8,128)(2,1)} %collective-permute-done.21.refs_1_, ...), custom_call_target="tpu_custom_call" | custom-call | flops 1610612736 | bytes 6815744 | tf_op jit(solution)/shard_map/pallas_call | solution.py:262
  162.6 0.4 collective-permute-start.31
  163.1 4.3 %shard_map.61 = (bf16[256,512]{1,0:T(8,128)(2,1)S(1)}, bf16[256,512]{1,0:T(8,128)(2,1)S(1)}) custom-call(s32[4]{0:T(128)S(1)} %copy-done, bf16[512,3072]{1,0:T(8,128)(2,1)S(1)} %shard_map.58.a_ref, bf16[384,1536]{1,0:T(8,128)(2,1)S(1)} %maximum_select_fusion.refs_0_, bf16[384,1536]{1,0:T(8,128)(2,1)} %collective-permute-done.21.refs_1_, ...), custom_call_target="tpu_custom_call" | custom-call | flops 1610612736 | bytes 6815744 | tf_op jit(solution)/shard_map/pallas_call | solution.py:262
  167.4 1.7 collective-permute-start.32
  169.1 2.7 %collective-permute-done.31 = bf16[256,512]{1,0:T(8,128)(2,1)S(1)} collective-permute-done((bf16[256,512]{1,0:T(8,128)(2,1)S(1)}, bf16[256,512]{1,0:T(8,128)(2,1)S(1)}, u32[]{:S(2)}, u32[]{:S(2)}) %collective-permute-start.31) | collective-permute-done | bytes 262176 | tf_op jit(solution)/shard_map/ppermute | solution.py:295
  171.9 4.5 %collective-permute-done.32 = bf16[256,512]{1,0:T(8,128)(2,1)S(1)} collective-permute-done((bf16[256,512]{1,0:T(8,128)(2,1)S(1)}, bf16[256,512]{1,0:T(8,128)(2,1)S(1)}, u32[]{:S(2)}, u32[]{:S(2)}) %collective-permute-start.32) | collective-permute-done | bytes 262176 | tf_op jit(solution)/shard_map/ppermute | solution.py:295
  176.7 1.3 broadcast_select_fusion
  (60 shorter events, 0.5 us)
Async XLA Ops:
  0.0 5.2 %copy-start.4 = (bf16[256,1536]{1,0:T(8,128)(2,1)S(1)}, bf16[256,1536]{1,0:T(8,128)(2,1)}, u32[]{:S(2)}) copy-start(bf16[256,1536]{1,0:T(8,128)(2,1)} %param.6) | copy-start | bytes 2359300
  0.0 5.3 %copy-start.5 = (bf16[256,1536]{1,0:T(8,128)(2,1)S(1)}, bf16[256,1536]{1,0:T(8,128)(2,1)}, u32[]{:S(2)}) copy-start(bf16[256,1536]{1,0:T(8,128)(2,1)} %param.7) | copy-start | bytes 2359300
  2.3 16.6 %collective-permute-start.2 = (bf16[192,1536]{1,0:T(8,128)(2,1)}, bf16[192,1536]{1,0:T(8,128)(2,1)}, u32[]{:S(2)}, u32[]{:S(2)}) collective-permute-start(bf16[192,1536]{1,0:T(8,128)(2,1)} %get-tuple-element.42), channel_id=1, source_target_pairs={{0,4},{2,6},{4,0},{6,2},{8,12},{10,14},{12,8},{14,10},{16,20},{18,... | collective-permute-start | bytes 1769480 | tf_op jit(solution)/shard_map/ppermute | solution.py:295
  5.3 18.3 %copy-start.1 = (bf16[512,1536]{1,0:T(8,128)(2,1)}, bf16[512,1536]{1,0:T(8,128)(2,1)S(1)}, u32[]{:S(2)}) copy-start(bf16[512,1536]{1,0:T(8,128)(2,1)S(1)} %constant_dynamic-update-slice_fusion.refs_3_.refs_12_) | copy-start | bytes 4718596
  5.3 36.8 %collective-permute-start = (bf16[512,1536]{1,0:T(8,128)(2,1)S(1)}, bf16[512,1536]{1,0:T(8,128)(2,1)}, u32[]{:S(2)}, u32[]{:S(2)}) collective-permute-start(bf16[512,1536]{1,0:T(8,128)(2,1)S(1)} %constant_dynamic-update-slice_fusion.refs_3_.refs_12_), channel_id=1, source_target_pairs={{0,8},{2,10},{4,12},{6,14},{8,16},{10,18},{12,20},{14,22},{16,24},... | collective-permute-start | bytes 4718600 | tf_op jit(solution)/shard_map/ppermute | solution.py:295
  10.0 37.6 %collective-permute-start.1 = (bf16[512,1536]{1,0:T(8,128)(2,1)S(1)}, bf16[512,1536]{1,0:T(8,128)(2,1)}, u32[]{:S(2)}, u32[]{:S(2)}) collective-permute-start(bf16[512,1536]{1,0:T(8,128)(2,1)S(1)} %constant_dynamic-update-slice_fusion.refs_3_.refs_12_), channel_id=1, source_target_pairs={{8,0},{10,2},{12,4},{14,6},{16,8},{18,10},{20,12},{22,14},{24,16},... | collective-permute-start | bytes 4718600 | tf_op jit(solution)/shard_map/ppermute | solution.py:295
  20.5 27.0 %collective-permute-start.3 = (bf16[512,1536]{1,0:T(8,128)(2,1)S(1)}, bf16[512,1536]{1,0:T(8,128)(2,1)}, u32[]{:S(2)}, u32[]{:S(2)}) collective-permute-start(bf16[512,1536]{1,0:T(8,128)(2,1)S(1)} %constant_dynamic-update-slice_fusion.refs_3_.refs_12_), channel_id=1, source_target_pairs={{0,2},{2,0},{4,6},{6,4},{8,10},{10,8},{12,14},{14,12},{16,18},{18,... | collective-permute-start | bytes 4718600 | tf_op jit(solution)/shard_map/ppermute | solution.py:295
  20.6 26.9 %collective-permute-start.4 = (bf16[512,1536]{1,0:T(8,128)(2,1)S(1)}, bf16[512,1536]{1,0:T(8,128)(2,1)}, u32[]{:S(2)}, u32[]{:S(2)}) collective-permute-start(bf16[512,1536]{1,0:T(8,128)(2,1)S(1)} %constant_dynamic-update-slice_fusion.refs_3_.refs_12_), channel_id=1, source_target_pairs={{2,4},{4,2},{10,12},{12,10},{18,20},{20,18},{26,28},{28,26},{3,5},... | collective-permute-start | bytes 4718600 | tf_op jit(solution)/shard_map/ppermute | solution.py:295
  23.7 11.2 %collective-permute-start.5 = (bf16[128,1536]{1,0:T(8,128)(2,1)S(1)}, bf16[128,1536]{1,0:T(8,128)(2,1)}, u32[]{:S(2)}, u32[]{:S(2)}) collective-permute-start(bf16[128,1536]{1,0:T(8,128)(2,1)S(1)} %get-tuple-element.44), channel_id=1, source_target_pairs={{0,1},{1,0},{2,3},{3,2},{4,5},{5,4},{6,7},{7,6},{8,9},{9,8},{10,11... | collective-permute-start | bytes 1179656 | tf_op jit(solution)/shard_map/ppermute | solution.py:309
  47.5 26.1 %collective-permute-start.19 = (bf16[384,1536]{1,0:T(8,128)(2,1)S(1)}, bf16[384,1536]{1,0:T(8,128)(2,1)S(1)}, u32[]{:S(2)}, u32[]{:S(2)}) collective-permute-start(bf16[384,1536]{1,0:T(8,128)(2,1)S(1)} %maximum_select_fusion.refs_0_), channel_id=1, source_target_pairs={{0,8},{2,10},{4,12},{6,14},{8,16},{10,18},{12,20},{14,22},{16,24},... | collective-permute-start | bytes 3538952 | tf_op jit(solution)/shard_map/ppermute | solution.py:295
  50.0 27.8 %collective-permute-start.20 = (bf16[384,1536]{1,0:T(8,128)(2,1)S(1)}, bf16[384,1536]{1,0:T(8,128)(2,1)S(1)}, u32[]{:S(2)}, u32[]{:S(2)}) collective-permute-start(bf16[384,1536]{1,0:T(8,128)(2,1)S(1)} %maximum_select_fusion.refs_0_), channel_id=1, source_target_pairs={{8,0},{10,2},{12,4},{14,6},{16,8},{18,10},{20,12},{22,14},{24,16},... | collective-permute-start | bytes 3538952 | tf_op jit(solution)/shard_map/ppermute | solution.py:295
  55.4 28.5 %collective-permute-start.6 = (bf16[1024,1024]{1,0:T(8,128)(2,1)}, bf16[1024,1024]{1,0:T(8,128)(2,1)}, u32[]{:S(2)}, u32[]{:S(2)}) collective-permute-start(bf16[1024,1024]{1,0:T(8,128)(2,1)} %pad_maximum_fusion.refs_0_.refs_6_.refs_9_.refs_15_), channel_id=1, source_target_pairs={{0,2},{2,0},{4,6},{6,4},{8,10},{10,8},{12,14},{14,12},{16,18},{18,... | collective-permute-start | bytes 6291464 | tf_op jit(solution)/shard_map/ppermute | solution.py:295
  55.4 29.8 %collective-permute-start.7 = (bf16[1024,1024]{1,0:T(8,128)(2,1)}, bf16[1024,1024]{1,0:T(8,128)(2,1)}, u32[]{:S(2)}, u32[]{:S(2)}) collective-permute-start(bf16[1024,1024]{1,0:T(8,128)(2,1)} %pad_maximum_fusion.refs_0_.refs_6_.refs_9_.refs_15_), channel_id=1, source_target_pairs={{2,4},{4,2},{10,12},{12,10},{18,20},{20,18},{26,28},{28,26},{3,5},... | collective-permute-start | bytes 6291464 | tf_op jit(solution)/shard_map/ppermute | solution.py:295
  60.6 18.8 %collective-permute-start.14 = (bf16[1024,512]{1,0:T(8,128)(2,1)}, bf16[1024,512]{1,0:T(8,128)(2,1)}, u32[]{:S(2)}, u32[]{:S(2)}) collective-permute-start(bf16[1024,512]{1,0:T(8,128)(2,1)} %pad_maximum_fusion.1.refs_0_.refs_6_.refs_9_.refs_15_), channel_id=1, source_target_pairs={{0,2},{2,0},{4,6},{6,4},{8,10},{10,8},{12,14},{14,12},{16,18},{18,... | collective-permute-start | bytes 3145736 | tf_op jit(solution)/shard_map/ppermute | solution.py:295
  73.6 26.2 %collective-permute-start.21 = (bf16[384,1536]{1,0:T(8,128)(2,1)S(1)}, bf16[384,1536]{1,0:T(8,128)(2,1)}, u32[]{:S(2)}, u32[]{:S(2)}) collective-permute-start(bf16[384,1536]{1,0:T(8,128)(2,1)S(1)} %maximum_select_fusion.refs_0_), channel_id=1, source_target_pairs={{0,2},{2,0},{4,6},{6,4},{8,10},{10,8},{12,14},{14,12},{16,18},{18,... | collective-permute-start | bytes 3538952 | tf_op jit(solution)/shard_map/ppermute | solution.py:295
  77.8 21.2 %collective-permute-start.15 = (bf16[1024,512]{1,0:T(8,128)(2,1)}, bf16[1024,512]{1,0:T(8,128)(2,1)}, u32[]{:S(2)}, u32[]{:S(2)}) collective-permute-start(bf16[1024,512]{1,0:T(8,128)(2,1)} %pad_maximum_fusion.1.refs_0_.refs_6_.refs_9_.refs_15_), channel_id=1, source_target_pairs={{2,4},{4,2},{10,12},{12,10},{18,20},{20,18},{26,28},{28,26},{3,5},... | collective-permute-start | bytes 3145736 | tf_op jit(solution)/shard_map/ppermute | solution.py:295
  79.5 10.3 %copy-start.12 = (s32[1,27]{1,0:T(1,128)S(1)}, s32[1,27]{1,0:T(1,128)}, u32[]{:S(2)}) copy-start(s32[1,27]{1,0:T(1,128)} %param.8) | copy-start | bytes 328
  79.5 55.9 %collective-permute-start.24 = (bf16[384,1536]{1,0:T(8,128)(2,1)S(1)}, bf16[384,1536]{1,0:T(8,128)(2,1)}, u32[]{:S(2)}, u32[]{:S(2)}) collective-permute-start(bf16[384,1536]{1,0:T(8,128)(2,1)S(1)} %maximum_select_fusion.refs_0_), channel_id=1, source_target_pairs={{0,16},{2,18},{4,20},{6,22},{24,8},{26,10},{28,12},{30,14},{1,17},... | collective-permute-start | bytes 3538952 | tf_op jit(solution)/shard_map/ppermute | solution.py:295
  83.9 55.7 %collective-permute-start.26 = (bf16[384,1536]{1,0:T(8,128)(2,1)S(1)}, bf16[384,1536]{1,0:T(8,128)(2,1)}, u32[]{:S(2)}, u32[]{:S(2)}) collective-permute-start(bf16[384,1536]{1,0:T(8,128)(2,1)S(1)} %broadcast_select_fusion.1), channel_id=1, source_target_pairs={{16,24},{18,26},{20,28},{22,30},{8,0},{10,2},{12,4},{14,6},{17,25}... | collective-permute-start | bytes 3538952 | tf_op jit(solution)/shard_map/ppermute | solution.py:295
  85.2 54.4 %collective-permute-start.28 = (bf16[384,1536]{1,0:T(8,128)(2,1)S(1)}, bf16[384,1536]{1,0:T(8,128)(2,1)}, u32[]{:S(2)}, u32[]{:S(2)}) collective-permute-start(bf16[384,1536]{1,0:T(8,128)(2,1)S(1)} %maximum_select_fusion.refs_0_), channel_id=1, source_target_pairs={{0,24},{2,26},{4,28},{6,30},{24,0},{26,2},{28,4},{30,6},{1,25},{3,... | collective-permute-start | bytes 3538952 | tf_op jit(solution)/shard_map/ppermute | solution.py:295
  99.0 10.9 %copy-start.2 = (bf16[256,512]{1,0:T(8,128)(2,1)S(1)}, bf16[256,512]{1,0:T(8,128)(2,1)}, u32[]{:S(2)}) copy-start(bf16[256,512]{1,0:T(8,128)(2,1)} %shard_map.55.refs_0_) | copy-start | bytes 786436
  99.0 10.9 %collective-permute-start.8 = (bf16[256,512]{1,0:T(8,128)(2,1)}, bf16[256,512]{1,0:T(8,128)(2,1)S(1)}, u32[]{:S(2)}, u32[]{:S(2)}) collective-permute-start(bf16[256,512]{1,0:T(8,128)(2,1)} %shard_map.55.refs_0_), channel_id=1, source_target_pairs={{0,4},{2,6},{4,0},{6,2},{8,12},{10,14},{12,8},{14,10},{16,20},{18,... | collective-permute-start | bytes 786440 | tf_op jit(solution)/shard_map/ppermute | solution.py:295
  99.8 11.5 %collective-permute-start.9 = (bf16[256,512]{1,0:T(8,128)(2,1)}, bf16[256,512]{1,0:T(8,128)(2,1)S(1)}, u32[]{:S(2)}, u32[]{:S(2)}) collective-permute-start(bf16[256,512]{1,0:T(8,128)(2,1)} %shard_map.55.refs_0_), channel_id=1, source_target_pairs={{0,1},{1,0},{2,3},{3,2},{4,5},{5,4},{6,7},{7,6},{8,9},{9,8},{10,11... | collective-permute-start | bytes 786440 | tf_op jit(solution)/shard_map/ppermute | solution.py:349
  109.9 15.8 %copy-start.3 = (bf16[256,512]{1,0:T(8,128)(2,1)}, bf16[256,512]{1,0:T(8,128)(2,1)S(1)}, u32[]{:S(2)}) copy-start(bf16[256,512]{1,0:T(8,128)(2,1)S(1)} %collective-permute-done.8.refs_18_.refs_1_) | copy-start | bytes 786436
  109.9 10.2 %collective-permute-start.10 = (bf16[256,512]{1,0:T(8,128)(2,1)S(1)}, bf16[256,512]{1,0:T(8,128)(2,1)S(1)}, u32[]{:S(2)}, u32[]{:S(2)}) collective-permute-start(bf16[256,512]{1,0:T(8,128)(2,1)S(1)} %copy-done.2), channel_id=1, source_target_pairs={{0,5},{1,4},{2,7},{3,6},{4,1},{5,0},{6,3},{7,2},{8,13},{9,12},{10,... | collective-permute-start | bytes 786440 | tf_op jit(solution)/shard_map/ppermute | solution.py:350
  111.3 23.1 %copy-start.6 = (bf16[256,512]{1,0:T(8,128)(2,1)}, bf16[256,512]{1,0:T(8,128)(2,1)S(1)}, u32[]{:S(2)}) copy-start(bf16[256,512]{1,0:T(8,128)(2,1)S(1)} %collective-permute-done.9.refs_2_) | copy-start | bytes 786436
  111.3 11.9 %collective-permute-start.11 = (bf16[256,512]{1,0:T(8,128)(2,1)}, bf16[256,512]{1,0:T(8,128)(2,1)S(1)}, u32[]{:S(2)}, u32[]{:S(2)}) collective-permute-start(bf16[256,512]{1,0:T(8,128)(2,1)} %shard_map.56.refs_4_), channel_id=1, source_target_pairs={{0,4},{2,6},{4,0},{6,2},{8,12},{10,14},{12,8},{14,10},{16,20},{18,... | collective-permute-start | bytes 786440 | tf_op jit(solution)/shard_map/ppermute | solution.py:295
  120.2 14.2 %copy-start.7 = (bf16[256,512]{1,0:T(8,128)(2,1)}, bf16[256,512]{1,0:T(8,128)(2,1)S(1)}, u32[]{:S(2)}) copy-start(bf16[256,512]{1,0:T(8,128)(2,1)S(1)} %collective-permute-done.10.refs_3_) | copy-start | bytes 786436
  120.2 14.2 %collective-permute-start.12 = (bf16[256,512]{1,0:T(8,128)(2,1)}, bf16[256,512]{1,0:T(8,128)(2,1)S(1)}, u32[]{:S(2)}, u32[]{:S(2)}) collective-permute-start(bf16[256,512]{1,0:T(8,128)(2,1)} %shard_map.56.refs_4_), channel_id=1, source_target_pairs={{0,1},{1,0},{2,3},{3,2},{4,5},{5,4},{6,7},{7,6},{8,9},{9,8},{10,11... | collective-permute-start | bytes 786440 | tf_op jit(solution)/shard_map/ppermute | solution.py:349
  123.1 11.2 %copy-start.8 = (bf16[256,512]{1,0:T(8,128)(2,1)}, bf16[256,512]{1,0:T(8,128)(2,1)S(1)}, u32[]{:S(2)}) copy-start(bf16[256,512]{1,0:T(8,128)(2,1)S(1)} %collective-permute-done.11.refs_5_) | copy-start | bytes 786436
  123.1 11.7 %collective-permute-start.13 = (bf16[256,512]{1,0:T(8,128)(2,1)}, bf16[256,512]{1,0:T(8,128)(2,1)S(1)}, u32[]{:S(2)}, u32[]{:S(2)}) collective-permute-start(bf16[256,512]{1,0:T(8,128)(2,1)} %shard_map.56.refs_4_), channel_id=1, source_target_pairs={{0,5},{1,4},{2,7},{3,6},{4,1},{5,0},{6,3},{7,2},{8,13},{9,12},{10,... | collective-permute-start | bytes 786440 | tf_op jit(solution)/shard_map/ppermute | solution.py:350
  134.4 5.2 %copy-start.9 = (bf16[256,512]{1,0:T(8,128)(2,1)}, bf16[256,512]{1,0:T(8,128)(2,1)S(1)}, u32[]{:S(2)}) copy-start(bf16[256,512]{1,0:T(8,128)(2,1)S(1)} %collective-permute-done.12.refs_6_) | copy-start | bytes 786436
  134.4 9.5 %collective-permute-start.16 = (bf16[256,512]{1,0:T(8,128)(2,1)}, bf16[256,512]{1,0:T(8,128)(2,1)S(1)}, u32[]{:S(2)}, u32[]{:S(2)}) collective-permute-start(bf16[256,512]{1,0:T(8,128)(2,1)} %shard_map.57.refs_8_), channel_id=1, source_target_pairs={{0,4},{2,6},{4,0},{6,2},{8,12},{10,14},{12,8},{14,10},{16,20},{18,... | collective-permute-start | bytes 786440 | tf_op jit(solution)/shard_map/ppermute | solution.py:295
  134.8 5.3 %copy-start.10 = (bf16[256,512]{1,0:T(8,128)(2,1)}, bf16[256,512]{1,0:T(8,128)(2,1)S(1)}, u32[]{:S(2)}) copy-start(bf16[256,512]{1,0:T(8,128)(2,1)S(1)} %collective-permute-done.13.refs_7_) | copy-start | bytes 786436
  134.8 12.5 %collective-permute-start.17 = (bf16[256,512]{1,0:T(8,128)(2,1)}, bf16[256,512]{1,0:T(8,128)(2,1)}, u32[]{:S(2)}, u32[]{:S(2)}) collective-permute-start(bf16[256,512]{1,0:T(8,128)(2,1)} %shard_map.57.refs_8_), channel_id=1, source_target_pairs={{0,1},{1,0},{2,3},{3,2},{4,5},{5,4},{6,7},{7,6},{8,9},{9,8},{10,11... | collective-permute-start | bytes 786440 | tf_op jit(solution)/shard_map/ppermute | solution.py:349
  135.3 12.0 %collective-permute-start.18 = (bf16[256,512]{1,0:T(8,128)(2,1)}, bf16[256,512]{1,0:T(8,128)(2,1)}, u32[]{:S(2)}, u32[]{:S(2)}) collective-permute-start(bf16[256,512]{1,0:T(8,128)(2,1)} %shard_map.57.refs_8_), channel_id=1, source_target_pairs={{0,5},{1,4},{2,7},{3,6},{4,1},{5,0},{6,3},{7,2},{8,13},{9,12},{10,... | collective-permute-start | bytes 786440 | tf_op jit(solution)/shard_map/ppermute | solution.py:350
  139.6 11.6 %collective-permute-start.22 = (bf16[384,1536]{1,0:T(8,128)(2,1)S(1)}, bf16[384,1536]{1,0:T(8,128)(2,1)}, u32[]{:S(2)}, u32[]{:S(2)}) collective-permute-start(bf16[384,1536]{1,0:T(8,128)(2,1)S(1)} %collective-permute-done.19.refs_2_), channel_id=1, source_target_pairs={{0,2},{2,0},{4,6},{6,4},{8,10},{10,8},{12,14},{14,12},{16,18},{18,... | collective-permute-start | bytes 3538952 | tf_op jit(solution)/shard_map/ppermute | solution.py:295
  139.6 11.6 %collective-permute-start.23 = (bf16[384,1536]{1,0:T(8,128)(2,1)S(1)}, bf16[384,1536]{1,0:T(8,128)(2,1)}, u32[]{:S(2)}, u32[]{:S(2)}) collective-permute-start(bf16[384,1536]{1,0:T(8,128)(2,1)S(1)} %collective-permute-done.20.refs_4_), channel_id=1, source_target_pairs={{0,2},{2,0},{4,6},{6,4},{8,10},{10,8},{12,14},{14,12},{16,18},{18,... | collective-permute-start | bytes 3538952 | tf_op jit(solution)/shard_map/ppermute | solution.py:295
  143.9 0.7 copy-start.11
  144.6 6.6 %collective-permute-start.25 = (bf16[384,1536]{1,0:T(8,128)(2,1)}, bf16[384,1536]{1,0:T(8,128)(2,1)}, u32[]{:S(2)}, u32[]{:S(2)}) collective-permute-start(bf16[384,1536]{1,0:T(8,128)(2,1)} %collective-permute-done.24.refs_6_), channel_id=1, source_target_pairs={{0,2},{2,0},{4,6},{6,4},{8,10},{10,8},{12,14},{14,12},{16,18},{18,... | collective-permute-start | bytes 3538952 | tf_op jit(solution)/shard_map/ppermute | solution.py:295
  147.4 3.9 %collective-permute-start.27 = (bf16[384,1536]{1,0:T(8,128)(2,1)}, bf16[384,1536]{1,0:T(8,128)(2,1)}, u32[]{:S(2)}, u32[]{:S(2)}) collective-permute-start(bf16[384,1536]{1,0:T(8,128)(2,1)} %collective-permute-done.26.refs_8_), channel_id=1, source_target_pairs={{0,2},{2,0},{4,6},{6,4},{8,10},{10,8},{12,14},{14,12},{16,18},{18,... | collective-permute-start | bytes 3538952 | tf_op jit(solution)/shard_map/ppermute | solution.py:295
  147.4 4.9 %collective-permute-start.29 = (bf16[384,1536]{1,0:T(8,128)(2,1)}, bf16[384,1536]{1,0:T(8,128)(2,1)}, u32[]{:S(2)}, u32[]{:S(2)}) collective-permute-start(bf16[384,1536]{1,0:T(8,128)(2,1)} %collective-permute-done.28.refs_10_), channel_id=1, source_target_pairs={{0,2},{2,0},{4,6},{6,4},{8,10},{10,8},{12,14},{14,12},{16,18},{18,... | collective-permute-start | bytes 3538952 | tf_op jit(solution)/shard_map/ppermute | solution.py:295
  148.5 3.8 %copy-start = (s32[4]{0:T(128)S(1)}, s32[4]{0:T(128)}, u32[]{:S(2)}) copy-start(s32[4]{0:T(128)} %pad_add_fusion.spot) | copy-start | bytes 52
  156.6 12.5 %collective-permute-start.30 = (bf16[256,512]{1,0:T(8,128)(2,1)S(1)}, bf16[256,512]{1,0:T(8,128)(2,1)S(1)}, u32[]{:S(2)}, u32[]{:S(2)}) collective-permute-start(bf16[256,512]{1,0:T(8,128)(2,1)S(1)} %get-tuple-element.38), channel_id=1, source_target_pairs={{0,4},{2,6},{4,0},{6,2},{8,12},{10,14},{12,8},{14,10},{16,20},{18,... | collective-permute-start | bytes 786440 | tf_op jit(solution)/shard_map/ppermute | solution.py:295
  162.6 9.3 %collective-permute-start.31 = (bf16[256,512]{1,0:T(8,128)(2,1)S(1)}, bf16[256,512]{1,0:T(8,128)(2,1)S(1)}, u32[]{:S(2)}, u32[]{:S(2)}) collective-permute-start(bf16[256,512]{1,0:T(8,128)(2,1)S(1)} %get-tuple-element.39), channel_id=1, source_target_pairs={{0,4},{2,6},{4,0},{6,2},{8,12},{10,14},{12,8},{14,10},{16,20},{18,... | collective-permute-start | bytes 786440 | tf_op jit(solution)/shard_map/ppermute | solution.py:295
  167.4 9.0 %collective-permute-start.32 = (bf16[256,512]{1,0:T(8,128)(2,1)S(1)}, bf16[256,512]{1,0:T(8,128)(2,1)S(1)}, u32[]{:S(2)}, u32[]{:S(2)}) collective-permute-start(bf16[256,512]{1,0:T(8,128)(2,1)S(1)} %get-tuple-element.40), channel_id=1, source_target_pairs={{0,4},{2,6},{4,0},{6,2},{8,12},{10,14},{12,8},{14,10},{16,20},{18,... | collective-permute-start | bytes 786440 | tf_op jit(solution)/shard_map/ppermute | solution.py:295

commit v5 on v4

--- a/solution.py
+++ b/solution.py
@@ -332,11 +332,9 @@
 
     w_own, w_up, w_dn = lax.optimization_barrier((w_own, w_up, w_dn))
     blocks = [w_own, w_mate, w_up, move(w_up, mates), w_dn, move(w_dn, mates)]
-    for far in (
-        move(w_own, between((0, 2), (3, 1))),
-        move(jnp.where(plane == planes - 2, w_up, w_dn), between((2, 3), (1, 0))),
-        move(w_own, between((0, 3), (3, 0))),
-    ):
+    passed = move(jnp.where(plane == planes - 2, w_up, w_dn), between((2, 3), (1, 0)))
+    ends = move(w_own, between((0, 3), (3, 0)))
+    for far in (move(w_own, between((0, 2), (3, 1))), passed, ends):
         blocks += [far, move(far, mates)]
 
     listed = jnp.concatenate([window[0], seq[None]])

time: 179 us -> 179 us (level)
  no operation moved by 1% of the time
where the time goes in v5:
time: 179 us; the launch traced here: 178 us
  waiting for transfers between devices  71.1 us (40%)
  starting transfers between devices  46.6 us (26%)
  Pallas kernels  41.5 us (23%)
  local copies, waits for them, and re-layouts  9.28 us (5%)
  other arithmetic  9.13 us (5%)
    ppermute x26, waiting for transfers between devices, move(): return lax.ppermute(array, 'seq', pairs)  50.8 us
    ppermute x26, starting transfers between devices, move(): return lax.ppermute(array, 'seq', pairs)  35.7 us
    pallas_call x3, Pallas kernels, attend_tile(): pl.pallas_call(attend_kernel, out_shape=jax.ShapeDtypeStruct((tile, count...  25.8 us
    pallas_call x3, Pallas kernels, project(): pl.pallas_call(functools.partial(project_kernel, planes, at), out_shape=[...  13 us
    ppermute x1, waiting for transfers between devices, local_plane(): q = in_order(side, q_own, lax.ppermute(q_else, 'head', [(0, 1), (1, 0)]), 0)  9.4 us
    ppermute x3, waiting for transfers between devices, local_plane(): lax.ppermute(mine, ('seq', 'head'), [(2 * i + y, 2 * (i ^ 2) + 1 - y) for...  8.18 us
    ppermute x3, starting transfers between devices, local_plane(): lax.ppermute(mine, ('seq', 'head'), [(2 * i + y, 2 * (i ^ 2) + 1 - y) for...  6.55 us
    select_n x3, other arithmetic, in_order(): jnp.where(flag == 0, jnp.concatenate([own, other], axis=axis), jnp.concat...  5.21 us
  transfers between devices with their start and end apart: 33, of which 14 were waited for; matrix products, arithmetic and copies ran while one was open for 8% of the time, Pallas kernels for 21%

profile of v5, /device:TPU:0, one launch (start us, length us, event | category | flops | bytes accessed | tf_op | source)
XLA Modules:
  0.0 178.0 jit_solution(14826647405559175428)
XLA Ops:
  0.0 2.3 %constant_dynamic-slice_fusion.3 = (bf16[192,1536]{1,0:T(8,128)(2,1)S(1)}, bf16[192,1536]{1,0:T(8,128)(2,1)}) fusion(bf16[192,3072]{1,0:T(8,128)(2,1)} %param.9, s32[]{:T(128)S(6)} %select_n.66, s32[]{:T(128)S(6)} %select_n.67), kind=kLoop, calls=%fused_computation.23 | loop fusion | bytes 2359304 | tf_op jit(solution)/shard_map/dynamic_slice | solution.py:312
  2.3 2.9 %collective-permute-start.2 = (bf16[192,1536]{1,0:T(8,128)(2,1)}, bf16[192,1536]{1,0:T(8,128)(2,1)}, u32[]{:S(2)}, u32[]{:S(2)}) collective-permute-start(bf16[192,1536]{1,0:T(8,128)(2,1)} %get-tuple-element.42), channel_id=1, source_target_pairs={{0,4},{2,6},{4,0},{6,2},{8,12},{10,14},{12,8},{14,10},{16,20},{18,... | collective-permute-start | bytes 1769480 | tf_op jit(solution)/shard_map/ppermute | solution.py:295
  5.3 4.6 %collective-permute-start = (bf16[512,1536]{1,0:T(8,128)(2,1)S(1)}, bf16[512,1536]{1,0:T(8,128)(2,1)}, u32[]{:S(2)}, u32[]{:S(2)}) collective-permute-start(bf16[512,1536]{1,0:T(8,128)(2,1)S(1)} %constant_dynamic-update-slice_fusion.refs_3_.refs_12_), channel_id=1, source_target_pairs={{0,8},{2,10},{4,12},{6,14},{8,16},{10,18},{12,20},{14,22},{16,24},... | collective-permute-start | bytes 4718600 | tf_op jit(solution)/shard_map/ppermute | solution.py:295
  10.0 1.3 collective-permute-start.1
  11.3 7.6 %collective-permute-done.2 = bf16[192,1536]{1,0:T(8,128)(2,1)} collective-permute-done((bf16[192,1536]{1,0:T(8,128)(2,1)}, bf16[192,1536]{1,0:T(8,128)(2,1)}, u32[]{:S(2)}, u32[]{:S(2)}) %collective-permute-start.2) | collective-permute-done | bytes 589856 | tf_op jit(solution)/shard_map/ppermute | solution.py:295
  18.8 1.7 maximum_select_fusion.refs_0_
  20.5 0.1 collective-permute-start.3
  20.6 1.9 %collective-permute-start.4 = (bf16[512,1536]{1,0:T(8,128)(2,1)S(1)}, bf16[512,1536]{1,0:T(8,128)(2,1)}, u32[]{:S(2)}, u32[]{:S(2)}) collective-permute-start(bf16[512,1536]{1,0:T(8,128)(2,1)S(1)} %constant_dynamic-update-slice_fusion.refs_3_.refs_12_), channel_id=1, source_target_pairs={{2,4},{4,2},{10,12},{12,10},{18,20},{20,18},{26,28},{28,26},{3,5},... | collective-permute-start | bytes 4718600 | tf_op jit(solution)/shard_map/ppermute | solution.py:295
  22.5 1.2 constant_dynamic-slice_fusion.1
  23.7 1.8 %collective-permute-start.5 = (bf16[128,1536]{1,0:T(8,128)(2,1)S(1)}, bf16[128,1536]{1,0:T(8,128)(2,1)}, u32[]{:S(2)}, u32[]{:S(2)}) collective-permute-start(bf16[128,1536]{1,0:T(8,128)(2,1)S(1)} %get-tuple-element.44), channel_id=1, source_target_pairs={{0,1},{1,0},{2,3},{3,2},{4,5},{5,4},{6,7},{7,6},{8,9},{9,8},{10,11... | collective-permute-start | bytes 1179656 | tf_op jit(solution)/shard_map/ppermute | solution.py:309
  25.5 9.4 %collective-permute-done.5 = bf16[128,1536]{1,0:T(8,128)(2,1)} collective-permute-done((bf16[128,1536]{1,0:T(8,128)(2,1)S(1)}, bf16[128,1536]{1,0:T(8,128)(2,1)}, u32[]{:S(2)}, u32[]{:S(2)}) %collective-permute-start.5) | collective-permute-done | bytes 393248 | tf_op jit(solution)/shard_map/ppermute | solution.py:309
  34.9 2.2 %maximum_select_fusion.1.q_ref = bf16[256,1536]{1,0:T(8,128)(2,1)} fusion(bf16[128,1536]{1,0:T(8,128)(2,1)} %collective-permute-done.5, bf16[128,1536]{1,0:T(8,128)(2,1)S(1)} %get-tuple-element.43, pred[]{:T(512)S(6)} %eq.14), kind=kLoop, calls=%fused_computation.5 | loop fusion | flops 3538944 | bytes 1572865 | tf_op jit(solution)/shard_map/jit(_where)/select_n | solution.py:298
  37.1 5.1 %collective-permute-done = bf16[512,1536]{1,0:T(8,128)(2,1)} collective-permute-done((bf16[512,1536]{1,0:T(8,128)(2,1)S(1)}, bf16[512,1536]{1,0:T(8,128)(2,1)}, u32[]{:S(2)}, u32[]{:S(2)}) %collective-permute-start) | collective-permute-done | bytes 1572896 | tf_op jit(solution)/shard_map/ppermute | solution.py:295
  42.2 5.4 %collective-permute-done.1 = bf16[512,1536]{1,0:T(8,128)(2,1)} collective-permute-done((bf16[512,1536]{1,0:T(8,128)(2,1)S(1)}, bf16[512,1536]{1,0:T(8,128)(2,1)}, u32[]{:S(2)}, u32[]{:S(2)}) %collective-permute-start.1) | collective-permute-done | bytes 1572896 | tf_op jit(solution)/shard_map/ppermute | solution.py:295
  47.5 2.4 %collective-permute-start.19 = (bf16[384,1536]{1,0:T(8,128)(2,1)S(1)}, bf16[384,1536]{1,0:T(8,128)(2,1)S(1)}, u32[]{:S(2)}, u32[]{:S(2)}) collective-permute-start(bf16[384,1536]{1,0:T(8,128)(2,1)S(1)} %maximum_select_fusion.refs_0_), channel_id=1, source_target_pairs={{0,8},{2,10},{4,12},{6,14},{8,16},{10,18},{12,20},{14,22},{16,24},... | collective-permute-start | bytes 3538952 | tf_op jit(solution)/shard_map/ppermute | solution.py:295
  50.0 1.3 collective-permute-start.20
  51.3 1.3 slice.13
  52.6 1.3 slice.12
  53.9 1.5 pad_maximum_fusion.refs_0_.refs_6_.refs_9_.refs_15_
  55.4 2.0 %collective-permute-start.7 = (bf16[1024,1024]{1,0:T(8,128)(2,1)}, bf16[1024,1024]{1,0:T(8,128)(2,1)}, u32[]{:S(2)}, u32[]{:S(2)}) collective-permute-start(bf16[1024,1024]{1,0:T(8,128)(2,1)} %pad_maximum_fusion.refs_0_.refs_6_.refs_9_.refs_15_), channel_id=1, source_target_pairs={{2,4},{4,2},{10,12},{12,10},{18,20},{20,18},{26,28},{28,26},{3,5},... | collective-permute-start | bytes 6291464 | tf_op jit(solution)/shard_map/ppermute | solution.py:295
  57.4 1.1 slice.15
  58.5 1.1 slice.14
  59.6 1.1 pad_maximum_fusion.1.refs_0_.refs_6_.refs_9_.refs_15_
  60.6 0.5 collective-permute-start.14
  61.2 12.5 %collective-permute-done.19.refs_2_ = bf16[384,1536]{1,0:T(8,128)(2,1)S(1)} collective-permute-done((bf16[384,1536]{1,0:T(8,128)(2,1)S(1)}, bf16[384,1536]{1,0:T(8,128)(2,1)S(1)}, u32[]{:S(2)}, u32[]{:S(2)}) %collective-permute-start.19) | collective-permute-done | bytes 1179680 | tf_op jit(solution)/shard_map/ppermute | solution.py:295
  73.6 4.2 %collective-permute-done.20.refs_4_ = bf16[384,1536]{1,0:T(8,128)(2,1)S(1)} collective-permute-done((bf16[384,1536]{1,0:T(8,128)(2,1)S(1)}, bf16[384,1536]{1,0:T(8,128)(2,1)S(1)}, u32[]{:S(2)}, u32[]{:S(2)}) %collective-permute-start.20) | collective-permute-done | bytes 1179680 | tf_op jit(solution)/shard_map/ppermute | solution.py:295
  77.8 1.6 collective-permute-start.15
  79.5 4.3 %collective-permute-start.24 = (bf16[384,1536]{1,0:T(8,128)(2,1)S(1)}, bf16[384,1536]{1,0:T(8,128)(2,1)}, u32[]{:S(2)}, u32[]{:S(2)}) collective-permute-start(bf16[384,1536]{1,0:T(8,128)(2,1)S(1)} %maximum_select_fusion.refs_0_), channel_id=1, source_target_pairs={{0,16},{2,18},{4,20},{6,22},{24,8},{26,10},{28,12},{30,14},{1,17},... | collective-permute-start | bytes 3538952 | tf_op jit(solution)/shard_map/ppermute | solution.py:295
  83.8 0.1 broadcast_select_fusion.1
  83.9 1.3 collective-permute-start.26
  85.2 4.5 %collective-permute-start.28 = (bf16[384,1536]{1,0:T(8,128)(2,1)S(1)}, bf16[384,1536]{1,0:T(8,128)(2,1)}, u32[]{:S(2)}, u32[]{:S(2)}) collective-permute-start(bf16[384,1536]{1,0:T(8,128)(2,1)S(1)} %maximum_select_fusion.refs_0_), channel_id=1, source_target_pairs={{0,24},{2,26},{4,28},{6,30},{24,0},{26,2},{28,4},{30,6},{1,25},{3,... | collective-permute-start | bytes 3538952 | tf_op jit(solution)/shard_map/ppermute | solution.py:295
  89.8 0.6 pad_add_fusion.1.listed
  90.4 8.6 %shard_map.55.refs_0_ = bf16[256,512]{1,0:T(8,128)(2,1)} custom-call(s32[28]{0:T(128)} %pad_add_fusion.1.listed, bf16[256,1536]{1,0:T(8,128)(2,1)} %maximum_select_fusion.1.q_ref, bf16[1024,1024]{1,0:T(8,128)(2,1)} %pad_maximum_fusion.refs_0_.refs_6_.refs_9_.refs_15_, bf16[1024,1024]{1,0:T(8,128)(2,1)} %collective-permute-done.6.refs_1_.refs_7_.refs_10_.refs_16_, ...), custom_call_target="tpu_custom_call" | custom-call | flops 1 | bytes 1 | tf_op jit(solution)/shard_map/pallas_call | solution.py:162
  99.0 0.8 collective-permute-start.8
  99.8 1.5 collective-permute-start.9
  101.3 8.6 %shard_map.56.refs_4_ = bf16[256,512]{1,0:T(8,128)(2,1)} custom-call(s32[28]{0:T(128)} %pad_add_fusion.1.listed, bf16[256,1536]{1,0:T(8,128)(2,1)} %maximum_select_fusion.1.q_ref, bf16[1024,1024]{1,0:T(8,128)(2,1)} %pad_maximum_fusion.refs_0_.refs_6_.refs_9_.refs_15_, bf16[1024,1024]{1,0:T(8,128)(2,1)} %collective-permute-done.6.refs_1_.refs_7_.refs_10_.refs_16_, ...), custom_call_target="tpu_custom_call" | custom-call | flops 1 | bytes 1 | tf_op jit(solution)/shard_map/pallas_call | solution.py:162
  109.9 1.3 collective-permute-start.10
  111.3 0.7 collective-permute-start.11
  112.0 8.2 %collective-permute-done.10.refs_3_ = bf16[256,512]{1,0:T(8,128)(2,1)S(1)} collective-permute-done((bf16[256,512]{1,0:T(8,128)(2,1)S(1)}, bf16[256,512]{1,0:T(8,128)(2,1)S(1)}, u32[]{:S(2)}, u32[]{:S(2)}) %collective-permute-start.10) | collective-permute-done | bytes 262176 | tf_op jit(solution)/shard_map/ppermute | solution.py:348
  120.2 0.5 collective-permute-start.12
  120.7 2.5 %collective-permute-done.11.refs_5_ = bf16[256,512]{1,0:T(8,128)(2,1)S(1)} collective-permute-done((bf16[256,512]{1,0:T(8,128)(2,1)}, bf16[256,512]{1,0:T(8,128)(2,1)S(1)}, u32[]{:S(2)}, u32[]{:S(2)}) %collective-permute-start.11) | collective-permute-done | bytes 262176 | tf_op jit(solution)/shard_map/ppermute | solution.py:295
  123.1 2.6 %collective-permute-start.13 = (bf16[256,512]{1,0:T(8,128)(2,1)}, bf16[256,512]{1,0:T(8,128)(2,1)S(1)}, u32[]{:S(2)}, u32[]{:S(2)}) collective-permute-start(bf16[256,512]{1,0:T(8,128)(2,1)} %shard_map.56.refs_4_), channel_id=1, source_target_pairs={{0,5},{1,4},{2,7},{3,6},{4,1},{5,0},{6,3},{7,2},{8,13},{9,12},{10,... | collective-permute-start | bytes 786440 | tf_op jit(solution)/shard_map/ppermute | solution.py:348
  125.8 8.6 %shard_map.57.refs_8_ = bf16[256,512]{1,0:T(8,128)(2,1)} custom-call(s32[28]{0:T(128)} %pad_add_fusion.1.listed, bf16[256,1536]{1,0:T(8,128)(2,1)} %maximum_select_fusion.1.q_ref, bf16[1024,512]{1,0:T(8,128)(2,1)} %pad_maximum_fusion.1.refs_0_.refs_6_.refs_9_.refs_15_, bf16[1024,512]{1,0:T(8,128)(2,1)} %collective-permute-done.14.refs_1_.refs_7_.refs_10_.refs_16_, ...), custom_call_target="tpu_custom_call" | custom-call | flops 1 | bytes 1 | tf_op jit(solution)/shard_map/pallas_call | solution.py:162
  134.4 0.4 collective-permute-start.16
  134.8 0.5 collective-permute-start.17
  135.3 2.6 %collective-permute-start.18 = (bf16[256,512]{1,0:T(8,128)(2,1)}, bf16[256,512]{1,0:T(8,128)(2,1)}, u32[]{:S(2)}, u32[]{:S(2)}) collective-permute-start(bf16[256,512]{1,0:T(8,128)(2,1)} %shard_map.57.refs_8_), channel_id=1, source_target_pairs={{0,5},{1,4},{2,7},{3,6},{4,1},{5,0},{6,3},{7,2},{8,13},{9,12},{10,... | collective-permute-start | bytes 786440 | tf_op jit(solution)/shard_map/ppermute | solution.py:348
  138.0 1.6 collective-permute-done.26.refs_8_
  139.6 0.5 collective-permute-start.23
  140.1 3.8 %collective-permute-done.16.refs_9_ = bf16[256,512]{1,0:T(8,128)(2,1)S(1)} collective-permute-done((bf16[256,512]{1,0:T(8,128)(2,1)}, bf16[256,512]{1,0:T(8,128)(2,1)S(1)}, u32[]{:S(2)}, u32[]{:S(2)}) %collective-permute-start.16) | collective-permute-done | bytes 262176 | tf_op jit(solution)/shard_map/ppermute | solution.py:295
  143.9 0.7 copy-done.11
  144.6 2.7 %collective-permute-done.17.refs_10_ = bf16[256,512]{1,0:T(8,128)(2,1)} collective-permute-done((bf16[256,512]{1,0:T(8,128)(2,1)}, bf16[256,512]{1,0:T(8,128)(2,1)}, u32[]{:S(2)}, u32[]{:S(2)}) %collective-permute-start.17) | collective-permute-done | bytes 262176 | tf_op jit(solution)/shard_map/ppermute | solution.py:347
  147.4 0.5 collective-permute-start.29
  147.9 0.6 pad_add_fusion.spot
  148.5 2.7 %shard_map.58.a_ref = bf16[512,3072]{1,0:T(8,128)(2,1)S(1)} custom-call(s32[4]{0:T(128)} %pad_add_fusion.spot, bf16[256,512]{1,0:T(8,128)(2,1)} %shard_map.55.refs_0_, bf16[256,512]{1,0:T(8,128)(2,1)} %copy-done.3, bf16[256,512]{1,0:T(8,128)(2,1)} %copy-done.6, bf16[256,512]{1,0:T(8,128)(2,1)} %copy-done.7, bf16[256,512]{1,0:T(8,128)(2,1)} %shard_map.56.refs_4_, ...), custom_call_target="tpu_custom_call" | custom-call | bytes 6291456 | tf_op jit(solution)/shard_map/pallas_call | solution.py:202
  151.2 1.0 collective-permute-done.29.refs_11_
  152.2 4.4 %shard_map.59 = (bf16[256,512]{1,0:T(8,128)(2,1)S(1)}, bf16[256,512]{1,0:T(8,128)(2,1)S(1)}) custom-call(s32[4]{0:T(128)S(1)} %copy-done, bf16[512,3072]{1,0:T(8,128)(2,1)S(1)} %shard_map.58.a_ref, bf16[384,1536]{1,0:T(8,128)(2,1)S(1)} %maximum_select_fusion.refs_0_, bf16[384,1536]{1,0:T(8,128)(2,1)} %collective-permute-done.21.refs_1_, ...), custom_call_target="tpu_custom_call" | custom-call | flops 1610612736 | bytes 6815744 | tf_op jit(solution)/shard_map/pallas_call | solution.py:262
  156.6 1.7 collective-permute-start.30
  158.3 4.3 %shard_map.60 = (bf16[256,512]{1,0:T(8,128)(2,1)S(1)}, bf16[256,512]{1,0:T(8,128)(2,1)S(1)}) custom-call(s32[4]{0:T(128)S(1)} %copy-done, bf16[512,3072]{1,0:T(8,128)(2,1)S(1)} %shard_map.58.a_ref, bf16[384,1536]{1,0:T(8,128)(2,1)S(1)} %maximum_select_fusion.refs_0_, bf16[384,1536]{1,0:T(8,128)(2,1)} %collective-permute-done.21.refs_1_, ...), custom_call_target="tpu_custom_call" | custom-call | flops 1610612736 | bytes 6815744 | tf_op jit(solution)/shard_map/pallas_call | solution.py:262
  162.6 0.4 collective-permute-start.31
  163.1 4.3 %shard_map.61 = (bf16[256,512]{1,0:T(8,128)(2,1)S(1)}, bf16[256,512]{1,0:T(8,128)(2,1)S(1)}) custom-call(s32[4]{0:T(128)S(1)} %copy-done, bf16[512,3072]{1,0:T(8,128)(2,1)S(1)} %shard_map.58.a_ref, bf16[384,1536]{1,0:T(8,128)(2,1)S(1)} %maximum_select_fusion.refs_0_, bf16[384,1536]{1,0:T(8,128)(2,1)} %collective-permute-done.21.refs_1_, ...), custom_call_target="tpu_custom_call" | custom-call | flops 1610612736 | bytes 6815744 | tf_op jit(solution)/shard_map/pallas_call | solution.py:262
  167.4 1.7 collective-permute-start.32
  169.1 2.7 %collective-permute-done.31 = bf16[256,512]{1,0:T(8,128)(2,1)S(1)} collective-permute-done((bf16[256,512]{1,0:T(8,128)(2,1)S(1)}, bf16[256,512]{1,0:T(8,128)(2,1)S(1)}, u32[]{:S(2)}, u32[]{:S(2)}) %collective-permute-start.31) | collective-permute-done | bytes 262176 | tf_op jit(solution)/shard_map/ppermute | solution.py:295
  171.9 4.5 %collective-permute-done.32 = bf16[256,512]{1,0:T(8,128)(2,1)S(1)} collective-permute-done((bf16[256,512]{1,0:T(8,128)(2,1)S(1)}, bf16[256,512]{1,0:T(8,128)(2,1)S(1)}, u32[]{:S(2)}, u32[]{:S(2)}) %collective-permute-start.32) | collective-permute-done | bytes 262176 | tf_op jit(solution)/shard_map/ppermute | solution.py:295
  176.7 1.3 broadcast_select_fusion
  (60 shorter events, 0.5 us)
Async XLA Ops:
  0.0 5.2 %copy-start.4 = (bf16[256,1536]{1,0:T(8,128)(2,1)S(1)}, bf16[256,1536]{1,0:T(8,128)(2,1)}, u32[]{:S(2)}) copy-start(bf16[256,1536]{1,0:T(8,128)(2,1)} %param.6) | copy-start | bytes 2359300
  0.0 5.3 %copy-start.5 = (bf16[256,1536]{1,0:T(8,128)(2,1)S(1)}, bf16[256,1536]{1,0:T(8,128)(2,1)}, u32[]{:S(2)}) copy-start(bf16[256,1536]{1,0:T(8,128)(2,1)} %param.7) | copy-start | bytes 2359300
  2.3 16.6 %collective-permute-start.2 = (bf16[192,1536]{1,0:T(8,128)(2,1)}, bf16[192,1536]{1,0:T(8,128)(2,1)}, u32[]{:S(2)}, u32[]{:S(2)}) collective-permute-start(bf16[192,1536]{1,0:T(8,128)(2,1)} %get-tuple-element.42), channel_id=1, source_target_pairs={{0,4},{2,6},{4,0},{6,2},{8,12},{10,14},{12,8},{14,10},{16,20},{18,... | collective-permute-start | bytes 1769480 | tf_op jit(solution)/shard_map/ppermute | solution.py:295
  5.3 18.3 %copy-start.1 = (bf16[512,1536]{1,0:T(8,128)(2,1)}, bf16[512,1536]{1,0:T(8,128)(2,1)S(1)}, u32[]{:S(2)}) copy-start(bf16[512,1536]{1,0:T(8,128)(2,1)S(1)} %constant_dynamic-update-slice_fusion.refs_3_.refs_12_) | copy-start | bytes 4718596
  5.3 36.8 %collective-permute-start = (bf16[512,1536]{1,0:T(8,128)(2,1)S(1)}, bf16[512,1536]{1,0:T(8,128)(2,1)}, u32[]{:S(2)}, u32[]{:S(2)}) collective-permute-start(bf16[512,1536]{1,0:T(8,128)(2,1)S(1)} %constant_dynamic-update-slice_fusion.refs_3_.refs_12_), channel_id=1, source_target_pairs={{0,8},{2,10},{4,12},{6,14},{8,16},{10,18},{12,20},{14,22},{16,24},... | collective-permute-start | bytes 4718600 | tf_op jit(solution)/shard_map/ppermute | solution.py:295
  10.0 37.6 %collective-permute-start.1 = (bf16[512,1536]{1,0:T(8,128)(2,1)S(1)}, bf16[512,1536]{1,0:T(8,128)(2,1)}, u32[]{:S(2)}, u32[]{:S(2)}) collective-permute-start(bf16[512,1536]{1,0:T(8,128)(2,1)S(1)} %constant_dynamic-update-slice_fusion.refs_3_.refs_12_), channel_id=1, source_target_pairs={{8,0},{10,2},{12,4},{14,6},{16,8},{18,10},{20,12},{22,14},{24,16},... | collective-permute-start | bytes 4718600 | tf_op jit(solution)/shard_map/ppermute | solution.py:295
  20.5 27.0 %collective-permute-start.3 = (bf16[512,1536]{1,0:T(8,128)(2,1)S(1)}, bf16[512,1536]{1,0:T(8,128)(2,1)}, u32[]{:S(2)}, u32[]{:S(2)}) collective-permute-start(bf16[512,1536]{1,0:T(8,128)(2,1)S(1)} %constant_dynamic-update-slice_fusion.refs_3_.refs_12_), channel_id=1, source_target_pairs={{0,2},{2,0},{4,6},{6,4},{8,10},{10,8},{12,14},{14,12},{16,18},{18,... | collective-permute-start | bytes 4718600 | tf_op jit(solution)/shard_map/ppermute | solution.py:295
  20.6 26.9 %collective-permute-start.4 = (bf16[512,1536]{1,0:T(8,128)(2,1)S(1)}, bf16[512,1536]{1,0:T(8,128)(2,1)}, u32[]{:S(2)}, u32[]{:S(2)}) collective-permute-start(bf16[512,1536]{1,0:T(8,128)(2,1)S(1)} %constant_dynamic-update-slice_fusion.refs_3_.refs_12_), channel_id=1, source_target_pairs={{2,4},{4,2},{10,12},{12,10},{18,20},{20,18},{26,28},{28,26},{3,5},... | collective-permute-start | bytes 4718600 | tf_op jit(solution)/shard_map/ppermute | solution.py:295
  23.7 11.2 %collective-permute-start.5 = (bf16[128,1536]{1,0:T(8,128)(2,1)S(1)}, bf16[128,1536]{1,0:T(8,128)(2,1)}, u32[]{:S(2)}, u32[]{:S(2)}) collective-permute-start(bf16[128,1536]{1,0:T(8,128)(2,1)S(1)} %get-tuple-element.44), channel_id=1, source_target_pairs={{0,1},{1,0},{2,3},{3,2},{4,5},{5,4},{6,7},{7,6},{8,9},{9,8},{10,11... | collective-permute-start | bytes 1179656 | tf_op jit(solution)/shard_map/ppermute | solution.py:309
  47.5 26.1 %collective-permute-start.19 = (bf16[384,1536]{1,0:T(8,128)(2,1)S(1)}, bf16[384,1536]{1,0:T(8,128)(2,1)S(1)}, u32[]{:S(2)}, u32[]{:S(2)}) collective-permute-start(bf16[384,1536]{1,0:T(8,128)(2,1)S(1)} %maximum_select_fusion.refs_0_), channel_id=1, source_target_pairs={{0,8},{2,10},{4,12},{6,14},{8,16},{10,18},{12,20},{14,22},{16,24},... | collective-permute-start | bytes 3538952 | tf_op jit(solution)/shard_map/ppermute | solution.py:295
  50.0 27.8 %collective-permute-start.20 = (bf16[384,1536]{1,0:T(8,128)(2,1)S(1)}, bf16[384,1536]{1,0:T(8,128)(2,1)S(1)}, u32[]{:S(2)}, u32[]{:S(2)}) collective-permute-start(bf16[384,1536]{1,0:T(8,128)(2,1)S(1)} %maximum_select_fusion.refs_0_), channel_id=1, source_target_pairs={{8,0},{10,2},{12,4},{14,6},{16,8},{18,10},{20,12},{22,14},{24,16},... | collective-permute-start | bytes 3538952 | tf_op jit(solution)/shard_map/ppermute | solution.py:295
  55.4 28.5 %collective-permute-start.6 = (bf16[1024,1024]{1,0:T(8,128)(2,1)}, bf16[1024,1024]{1,0:T(8,128)(2,1)}, u32[]{:S(2)}, u32[]{:S(2)}) collective-permute-start(bf16[1024,1024]{1,0:T(8,128)(2,1)} %pad_maximum_fusion.refs_0_.refs_6_.refs_9_.refs_15_), channel_id=1, source_target_pairs={{0,2},{2,0},{4,6},{6,4},{8,10},{10,8},{12,14},{14,12},{16,18},{18,... | collective-permute-start | bytes 6291464 | tf_op jit(solution)/shard_map/ppermute | solution.py:295
  55.4 29.8 %collective-permute-start.7 = (bf16[1024,1024]{1,0:T(8,128)(2,1)}, bf16[1024,1024]{1,0:T(8,128)(2,1)}, u32[]{:S(2)}, u32[]{:S(2)}) collective-permute-start(bf16[1024,1024]{1,0:T(8,128)(2,1)} %pad_maximum_fusion.refs_0_.refs_6_.refs_9_.refs_15_), channel_id=1, source_target_pairs={{2,4},{4,2},{10,12},{12,10},{18,20},{20,18},{26,28},{28,26},{3,5},... | collective-permute-start | bytes 6291464 | tf_op jit(solution)/shard_map/ppermute | solution.py:295
  60.6 18.8 %collective-permute-start.14 = (bf16[1024,512]{1,0:T(8,128)(2,1)}, bf16[1024,512]{1,0:T(8,128)(2,1)}, u32[]{:S(2)}, u32[]{:S(2)}) collective-permute-start(bf16[1024,512]{1,0:T(8,128)(2,1)} %pad_maximum_fusion.1.refs_0_.refs_6_.refs_9_.refs_15_), channel_id=1, source_target_pairs={{0,2},{2,0},{4,6},{6,4},{8,10},{10,8},{12,14},{14,12},{16,18},{18,... | collective-permute-start | bytes 3145736 | tf_op jit(solution)/shard_map/ppermute | solution.py:295
  73.6 26.2 %collective-permute-start.21 = (bf16[384,1536]{1,0:T(8,128)(2,1)S(1)}, bf16[384,1536]{1,0:T(8,128)(2,1)}, u32[]{:S(2)}, u32[]{:S(2)}) collective-permute-start(bf16[384,1536]{1,0:T(8,128)(2,1)S(1)} %maximum_select_fusion.refs_0_), channel_id=1, source_target_pairs={{0,2},{2,0},{4,6},{6,4},{8,10},{10,8},{12,14},{14,12},{16,18},{18,... | collective-permute-start | bytes 3538952 | tf_op jit(solution)/shard_map/ppermute | solution.py:295
  77.8 21.2 %collective-permute-start.15 = (bf16[1024,512]{1,0:T(8,128)(2,1)}, bf16[1024,512]{1,0:T(8,128)(2,1)}, u32[]{:S(2)}, u32[]{:S(2)}) collective-permute-start(bf16[1024,512]{1,0:T(8,128)(2,1)} %pad_maximum_fusion.1.refs_0_.refs_6_.refs_9_.refs_15_), channel_id=1, source_target_pairs={{2,4},{4,2},{10,12},{12,10},{18,20},{20,18},{26,28},{28,26},{3,5},... | collective-permute-start | bytes 3145736 | tf_op jit(solution)/shard_map/ppermute | solution.py:295
  79.5 10.3 %copy-start.12 = (s32[1,27]{1,0:T(1,128)S(1)}, s32[1,27]{1,0:T(1,128)}, u32[]{:S(2)}) copy-start(s32[1,27]{1,0:T(1,128)} %param.8) | copy-start | bytes 328
  79.5 55.9 %collective-permute-start.24 = (bf16[384,1536]{1,0:T(8,128)(2,1)S(1)}, bf16[384,1536]{1,0:T(8,128)(2,1)}, u32[]{:S(2)}, u32[]{:S(2)}) collective-permute-start(bf16[384,1536]{1,0:T(8,128)(2,1)S(1)} %maximum_select_fusion.refs_0_), channel_id=1, source_target_pairs={{0,16},{2,18},{4,20},{6,22},{24,8},{26,10},{28,12},{30,14},{1,17},... | collective-permute-start | bytes 3538952 | tf_op jit(solution)/shard_map/ppermute | solution.py:295
  83.9 55.7 %collective-permute-start.26 = (bf16[384,1536]{1,0:T(8,128)(2,1)S(1)}, bf16[384,1536]{1,0:T(8,128)(2,1)}, u32[]{:S(2)}, u32[]{:S(2)}) collective-permute-start(bf16[384,1536]{1,0:T(8,128)(2,1)S(1)} %broadcast_select_fusion.1), channel_id=1, source_target_pairs={{16,24},{18,26},{20,28},{22,30},{8,0},{10,2},{12,4},{14,6},{17,25}... | collective-permute-start | bytes 3538952 | tf_op jit(solution)/shard_map/ppermute | solution.py:295
  85.2 54.4 %collective-permute-start.28 = (bf16[384,1536]{1,0:T(8,128)(2,1)S(1)}, bf16[384,1536]{1,0:T(8,128)(2,1)}, u32[]{:S(2)}, u32[]{:S(2)}) collective-permute-start(bf16[384,1536]{1,0:T(8,128)(2,1)S(1)} %maximum_select_fusion.refs_0_), channel_id=1, source_target_pairs={{0,24},{2,26},{4,28},{6,30},{24,0},{26,2},{28,4},{30,6},{1,25},{3,... | collective-permute-start | bytes 3538952 | tf_op jit(solution)/shard_map/ppermute | solution.py:295
  99.0 10.9 %copy-start.2 = (bf16[256,512]{1,0:T(8,128)(2,1)S(1)}, bf16[256,512]{1,0:T(8,128)(2,1)}, u32[]{:S(2)}) copy-start(bf16[256,512]{1,0:T(8,128)(2,1)} %shard_map.55.refs_0_) | copy-start | bytes 786436
  99.0 10.9 %collective-permute-start.8 = (bf16[256,512]{1,0:T(8,128)(2,1)}, bf16[256,512]{1,0:T(8,128)(2,1)S(1)}, u32[]{:S(2)}, u32[]{:S(2)}) collective-permute-start(bf16[256,512]{1,0:T(8,128)(2,1)} %shard_map.55.refs_0_), channel_id=1, source_target_pairs={{0,4},{2,6},{4,0},{6,2},{8,12},{10,14},{12,8},{14,10},{16,20},{18,... | collective-permute-start | bytes 786440 | tf_op jit(solution)/shard_map/ppermute | solution.py:295
  99.8 11.5 %collective-permute-start.9 = (bf16[256,512]{1,0:T(8,128)(2,1)}, bf16[256,512]{1,0:T(8,128)(2,1)S(1)}, u32[]{:S(2)}, u32[]{:S(2)}) collective-permute-start(bf16[256,512]{1,0:T(8,128)(2,1)} %shard_map.55.refs_0_), channel_id=1, source_target_pairs={{0,1},{1,0},{2,3},{3,2},{4,5},{5,4},{6,7},{7,6},{8,9},{9,8},{10,11... | collective-permute-start | bytes 786440 | tf_op jit(solution)/shard_map/ppermute | solution.py:347
  109.9 15.8 %copy-start.3 = (bf16[256,512]{1,0:T(8,128)(2,1)}, bf16[256,512]{1,0:T(8,128)(2,1)S(1)}, u32[]{:S(2)}) copy-start(bf16[256,512]{1,0:T(8,128)(2,1)S(1)} %collective-permute-done.8.refs_18_.refs_1_) | copy-start | bytes 786436
  109.9 10.2 %collective-permute-start.10 = (bf16[256,512]{1,0:T(8,128)(2,1)S(1)}, bf16[256,512]{1,0:T(8,128)(2,1)S(1)}, u32[]{:S(2)}, u32[]{:S(2)}) collective-permute-start(bf16[256,512]{1,0:T(8,128)(2,1)S(1)} %copy-done.2), channel_id=1, source_target_pairs={{0,5},{1,4},{2,7},{3,6},{4,1},{5,0},{6,3},{7,2},{8,13},{9,12},{10,... | collective-permute-start | bytes 786440 | tf_op jit(solution)/shard_map/ppermute | solution.py:348
  111.3 23.1 %copy-start.6 = (bf16[256,512]{1,0:T(8,128)(2,1)}, bf16[256,512]{1,0:T(8,128)(2,1)S(1)}, u32[]{:S(2)}) copy-start(bf16[256,512]{1,0:T(8,128)(2,1)S(1)} %collective-permute-done.9.refs_2_) | copy-start | bytes 786436
  111.3 11.9 %collective-permute-start.11 = (bf16[256,512]{1,0:T(8,128)(2,1)}, bf16[256,512]{1,0:T(8,128)(2,1)S(1)}, u32[]{:S(2)}, u32[]{:S(2)}) collective-permute-start(bf16[256,512]{1,0:T(8,128)(2,1)} %shard_map.56.refs_4_), channel_id=1, source_target_pairs={{0,4},{2,6},{4,0},{6,2},{8,12},{10,14},{12,8},{14,10},{16,20},{18,... | collective-permute-start | bytes 786440 | tf_op jit(solution)/shard_map/ppermute | solution.py:295
  120.2 14.2 %copy-start.7 = (bf16[256,512]{1,0:T(8,128)(2,1)}, bf16[256,512]{1,0:T(8,128)(2,1)S(1)}, u32[]{:S(2)}) copy-start(bf16[256,512]{1,0:T(8,128)(2,1)S(1)} %collective-permute-done.10.refs_3_) | copy-start | bytes 786436
  120.2 14.2 %collective-permute-start.12 = (bf16[256,512]{1,0:T(8,128)(2,1)}, bf16[256,512]{1,0:T(8,128)(2,1)S(1)}, u32[]{:S(2)}, u32[]{:S(2)}) collective-permute-start(bf16[256,512]{1,0:T(8,128)(2,1)} %shard_map.56.refs_4_), channel_id=1, source_target_pairs={{0,1},{1,0},{2,3},{3,2},{4,5},{5,4},{6,7},{7,6},{8,9},{9,8},{10,11... | collective-permute-start | bytes 786440 | tf_op jit(solution)/shard_map/ppermute | solution.py:347
  123.1 11.2 %copy-start.8 = (bf16[256,512]{1,0:T(8,128)(2,1)}, bf16[256,512]{1,0:T(8,128)(2,1)S(1)}, u32[]{:S(2)}) copy-start(bf16[256,512]{1,0:T(8,128)(2,1)S(1)} %collective-permute-done.11.refs_5_) | copy-start | bytes 786436
  123.1 11.7 %collective-permute-start.13 = (bf16[256,512]{1,0:T(8,128)(2,1)}, bf16[256,512]{1,0:T(8,128)(2,1)S(1)}, u32[]{:S(2)}, u32[]{:S(2)}) collective-permute-start(bf16[256,512]{1,0:T(8,128)(2,1)} %shard_map.56.refs_4_), channel_id=1, source_target_pairs={{0,5},{1,4},{2,7},{3,6},{4,1},{5,0},{6,3},{7,2},{8,13},{9,12},{10,... | collective-permute-start | bytes 786440 | tf_op jit(solution)/shard_map/ppermute | solution.py:348
  134.4 5.2 %copy-start.9 = (bf16[256,512]{1,0:T(8,128)(2,1)}, bf16[256,512]{1,0:T(8,128)(2,1)S(1)}, u32[]{:S(2)}) copy-start(bf16[256,512]{1,0:T(8,128)(2,1)S(1)} %collective-permute-done.12.refs_6_) | copy-start | bytes 786436
  134.4 9.5 %collective-permute-start.16 = (bf16[256,512]{1,0:T(8,128)(2,1)}, bf16[256,512]{1,0:T(8,128)(2,1)S(1)}, u32[]{:S(2)}, u32[]{:S(2)}) collective-permute-start(bf16[256,512]{1,0:T(8,128)(2,1)} %shard_map.57.refs_8_), channel_id=1, source_target_pairs={{0,4},{2,6},{4,0},{6,2},{8,12},{10,14},{12,8},{14,10},{16,20},{18,... | collective-permute-start | bytes 786440 | tf_op jit(solution)/shard_map/ppermute | solution.py:295
  134.8 5.3 %copy-start.10 = (bf16[256,512]{1,0:T(8,128)(2,1)}, bf16[256,512]{1,0:T(8,128)(2,1)S(1)}, u32[]{:S(2)}) copy-start(bf16[256,512]{1,0:T(8,128)(2,1)S(1)} %collective-permute-done.13.refs_7_) | copy-start | bytes 786436
  134.8 12.5 %collective-permute-start.17 = (bf16[256,512]{1,0:T(8,128)(2,1)}, bf16[256,512]{1,0:T(8,128)(2,1)}, u32[]{:S(2)}, u32[]{:S(2)}) collective-permute-start(bf16[256,512]{1,0:T(8,128)(2,1)} %shard_map.57.refs_8_), channel_id=1, source_target_pairs={{0,1},{1,0},{2,3},{3,2},{4,5},{5,4},{6,7},{7,6},{8,9},{9,8},{10,11... | collective-permute-start | bytes 786440 | tf_op jit(solution)/shard_map/ppermute | solution.py:347
  135.3 12.0 %collective-permute-start.18 = (bf16[256,512]{1,0:T(8,128)(2,1)}, bf16[256,512]{1,0:T(8,128)(2,1)}, u32[]{:S(2)}, u32[]{:S(2)}) collective-permute-start(bf16[256,512]{1,0:T(8,128)(2,1)} %shard_map.57.refs_8_), channel_id=1, source_target_pairs={{0,5},{1,4},{2,7},{3,6},{4,1},{5,0},{6,3},{7,2},{8,13},{9,12},{10,... | collective-permute-start | bytes 786440 | tf_op jit(solution)/shard_map/ppermute | solution.py:348
  139.6 11.6 %collective-permute-start.22 = (bf16[384,1536]{1,0:T(8,128)(2,1)S(1)}, bf16[384,1536]{1,0:T(8,128)(2,1)}, u32[]{:S(2)}, u32[]{:S(2)}) collective-permute-start(bf16[384,1536]{1,0:T(8,128)(2,1)S(1)} %collective-permute-done.19.refs_2_), channel_id=1, source_target_pairs={{0,2},{2,0},{4,6},{6,4},{8,10},{10,8},{12,14},{14,12},{16,18},{18,... | collective-permute-start | bytes 3538952 | tf_op jit(solution)/shard_map/ppermute | solution.py:295
  139.6 11.6 %collective-permute-start.23 = (bf16[384,1536]{1,0:T(8,128)(2,1)S(1)}, bf16[384,1536]{1,0:T(8,128)(2,1)}, u32[]{:S(2)}, u32[]{:S(2)}) collective-permute-start(bf16[384,1536]{1,0:T(8,128)(2,1)S(1)} %collective-permute-done.20.refs_4_), channel_id=1, source_target_pairs={{0,2},{2,0},{4,6},{6,4},{8,10},{10,8},{12,14},{14,12},{16,18},{18,... | collective-permute-start | bytes 3538952 | tf_op jit(solution)/shard_map/ppermute | solution.py:295
  143.9 0.7 copy-start.11
  144.6 6.6 %collective-permute-start.25 = (bf16[384,1536]{1,0:T(8,128)(2,1)}, bf16[384,1536]{1,0:T(8,128)(2,1)}, u32[]{:S(2)}, u32[]{:S(2)}) collective-permute-start(bf16[384,1536]{1,0:T(8,128)(2,1)} %collective-permute-done.24.refs_6_), channel_id=1, source_target_pairs={{0,2},{2,0},{4,6},{6,4},{8,10},{10,8},{12,14},{14,12},{16,18},{18,... | collective-permute-start | bytes 3538952 | tf_op jit(solution)/shard_map/ppermute | solution.py:295
  147.4 3.9 %collective-permute-start.27 = (bf16[384,1536]{1,0:T(8,128)(2,1)}, bf16[384,1536]{1,0:T(8,128)(2,1)}, u32[]{:S(2)}, u32[]{:S(2)}) collective-permute-start(bf16[384,1536]{1,0:T(8,128)(2,1)} %collective-permute-done.26.refs_8_), channel_id=1, source_target_pairs={{0,2},{2,0},{4,6},{6,4},{8,10},{10,8},{12,14},{14,12},{16,18},{18,... | collective-permute-start | bytes 3538952 | tf_op jit(solution)/shard_map/ppermute | solution.py:295
  147.4 4.9 %collective-permute-start.29 = (bf16[384,1536]{1,0:T(8,128)(2,1)}, bf16[384,1536]{1,0:T(8,128)(2,1)}, u32[]{:S(2)}, u32[]{:S(2)}) collective-permute-start(bf16[384,1536]{1,0:T(8,128)(2,1)} %collective-permute-done.28.refs_10_), channel_id=1, source_target_pairs={{0,2},{2,0},{4,6},{6,4},{8,10},{10,8},{12,14},{14,12},{16,18},{18,... | collective-permute-start | bytes 3538952 | tf_op jit(solution)/shard_map/ppermute | solution.py:295
  148.5 3.8 %copy-start = (s32[4]{0:T(128)S(1)}, s32[4]{0:T(128)}, u32[]{:S(2)}) copy-start(s32[4]{0:T(128)} %pad_add_fusion.spot) | copy-start | bytes 52
  156.6 12.5 %collective-permute-start.30 = (bf16[256,512]{1,0:T(8,128)(2,1)S(1)}, bf16[256,512]{1,0:T(8,128)(2,1)S(1)}, u32[]{:S(2)}, u32[]{:S(2)}) collective-permute-start(bf16[256,512]{1,0:T(8,128)(2,1)S(1)} %get-tuple-element.38), channel_id=1, source_target_pairs={{0,4},{2,6},{4,0},{6,2},{8,12},{10,14},{12,8},{14,10},{16,20},{18,... | collective-permute-start | bytes 786440 | tf_op jit(solution)/shard_map/ppermute | solution.py:295
  162.6 9.3 %collective-permute-start.31 = (bf16[256,512]{1,0:T(8,128)(2,1)S(1)}, bf16[256,512]{1,0:T(8,128)(2,1)S(1)}, u32[]{:S(2)}, u32[]{:S(2)}) collective-permute-start(bf16[256,512]{1,0:T(8,128)(2,1)S(1)} %get-tuple-element.39), channel_id=1, source_target_pairs={{0,4},{2,6},{4,0},{6,2},{8,12},{10,14},{12,8},{14,10},{16,20},{18,... | collective-permute-start | bytes 786440 | tf_op jit(solution)/shard_map/ppermute | solution.py:295
  167.4 9.0 %collective-permute-start.32 = (bf16[256,512]{1,0:T(8,128)(2,1)S(1)}, bf16[256,512]{1,0:T(8,128)(2,1)S(1)}, u32[]{:S(2)}, u32[]{:S(2)}) collective-permute-start(bf16[256,512]{1,0:T(8,128)(2,1)S(1)} %get-tuple-element.40), channel_id=1, source_target_pairs={{0,4},{2,6},{4,0},{6,2},{8,12},{10,14},{12,8},{14,10},{16,20},{18,... | collective-permute-start | bytes 786440 | tf_op jit(solution)/shard_map/ppermute | solution.py:295

commit v6 on v5

--- a/solution.py
+++ b/solution.py
@@ -113,7 +113,8 @@
 
 def attend_kernel(listed, q_ref, *refs):
     o_ref = refs[-1]
-    keys, values = refs[:9], refs[9:18]
+    tiles = refs[:9]
+    tile = q_ref.shape[0]
     coef = HEAD_DIM**-0.5 * LOG2E
     toward = 1 - 2 * (listed[27] & 1)
     for head in range(q_ref.shape[1] // HEAD_DIM):
@@ -125,7 +126,7 @@
             new = top
             for k, step in enumerate((0, toward, -toward)):
                 s = lax.dot_general(
-                    keys[3 * r + k][:, at], q, (((1,), (1,)), ((), ())), preferred_element_type=jnp.float32
+                    tiles[3 * r + k][:tile, at], q, (((1,), (1,)), ((), ())), preferred_element_type=jnp.float32
                 )
                 live = listed[10 + 3 * r + step] >= 0
                 scores.append(s)
@@ -138,7 +139,7 @@
                 w_sum = jnp.sum(w, axis=0, keepdims=True)
                 part = w_sum if part is None else part + w_sum
                 weights.append(w.astype(jnp.bfloat16))
-            sides = jnp.concatenate([values[3 * r + k][:, at].T for k in range(3)], axis=1)
+            sides = jnp.concatenate([tiles[3 * r + k][tile:, at].T for k in range(3)], axis=1)
             pv = jnp.dot(sides, jnp.concatenate(weights, axis=0), preferred_element_type=jnp.float32)
             if top is None:
                 total, acc = part, pv
@@ -156,8 +157,8 @@
 def attend_tile(listed, q, head, count, first, own, rows, before):
     tile = q.shape[0]
 
-    def spec(block, at=first):
-        return pl.BlockSpec((tile, AT_ONCE * HEAD_DIM), lambda h, listed: (block, at // AT_ONCE + h))
+    def spec(block, at=first, rows=2 * tile):
+        return pl.BlockSpec((rows, AT_ONCE * HEAD_DIM), lambda h, listed: (block, at // AT_ONCE + h))
 
     return pl.pallas_call(
         attend_kernel,
@@ -165,19 +166,16 @@
         grid_spec=pltpu.PrefetchScalarGridSpec(
             num_scalar_prefetch=1,
             grid=(count // AT_ONCE,),
-            in_specs=[spec(0, head)]
+            in_specs=[spec(0, head, tile)]
             + [spec(0)] * 3
             + [spec(0, head)] * 3
-            + [spec(2)] * 3
             + [spec(1)] * 3
-            + [spec(1, head)] * 3
-            + [spec(3)] * 3
             + [pl.BlockSpec(memory_space=pl.ANY)] * len(before),
             out_specs=pl.BlockSpec((tile, AT_ONCE * HEAD_DIM), lambda h, listed: (0, h)),
         ),
         compiler_params=pltpu.CompilerParams(vmem_limit_bytes=VMEM_LIMIT),
         cost_estimate=pl.CostEstimate(flops=1, bytes_accessed=1, transcendentals=0),
-    )(listed, q, *rows, *own, *rows, *rows, *own, *rows, *before)
+    )(listed, q, *rows, *own, *rows, *before)
 
 
 def gather_kernel(spot, *refs):

time: 179 us -> 178 us (level)
  no operation moved by 1% of the time
where the time goes in v6:
time: 178 us
  waiting for transfers between devices  71.1 us (40%)
  starting transfers between devices  46.6 us (26%)
  Pallas kernels  41.1 us (23%)
  local copies, waits for them, and re-layouts  9.28 us (5%)
  other arithmetic  9.13 us (5%)
    ppermute x26, waiting for transfers between devices, move(): return lax.ppermute(array, 'seq', pairs)  50.8 us
    ppermute x26, starting transfers between devices, move(): return lax.ppermute(array, 'seq', pairs)  35.7 us
    pallas_call x3, Pallas kernels, attend_tile(): pl.pallas_call(attend_kernel, out_shape=jax.ShapeDtypeStruct((tile, count...  25.4 us
    pallas_call x3, Pallas kernels, project(): pl.pallas_call(functools.partial(project_kernel, planes, at), out_shape=[...  13 us
    ppermute x1, waiting for transfers between devices, local_plane(): q = in_order(side, q_own, lax.ppermute(q_else, 'head', [(0, 1), (1, 0)]), 0)  9.4 us
    ppermute x3, waiting for transfers between devices, local_plane(): lax.ppermute(mine, ('seq', 'head'), [(2 * i + y, 2 * (i ^ 2) + 1 - y) for...  8.18 us
    ppermute x3, starting transfers between devices, local_plane(): lax.ppermute(mine, ('seq', 'head'), [(2 * i + y, 2 * (i ^ 2) + 1 - y) for...  6.56 us
    select_n x3, other arithmetic, in_order(): jnp.where(flag == 0, jnp.concatenate([own, other], axis=axis), jnp.concat...  5.21 us
  transfers between devices with their start and end apart: 33, of which 14 were waited for; matrix products, arithmetic and copies ran while one was open for 8% of the time, Pallas kernels for 21%

profile of v6, /device:TPU:0, one launch (start us, length us, event | category | flops | bytes accessed | tf_op | source)
XLA Modules:
  0.0 177.6 jit_solution(9462649347314458927)
XLA Ops:
  0.0 2.3 %constant_dynamic-slice_fusion.3 = (bf16[192,1536]{1,0:T(8,128)(2,1)S(1)}, bf16[192,1536]{1,0:T(8,128)(2,1)}) fusion(bf16[192,3072]{1,0:T(8,128)(2,1)} %param.9, s32[]{:T(128)S(6)} %select_n.66, s32[]{:T(128)S(6)} %select_n.67), kind=kLoop, calls=%fused_computation.23 | loop fusion | bytes 2359304 | tf_op jit(solution)/shard_map/dynamic_slice | solution.py:310
  2.3 2.9 %collective-permute-start.2 = (bf16[192,1536]{1,0:T(8,128)(2,1)}, bf16[192,1536]{1,0:T(8,128)(2,1)}, u32[]{:S(2)}, u32[]{:S(2)}) collective-permute-start(bf16[192,1536]{1,0:T(8,128)(2,1)} %get-tuple-element.42), channel_id=1, source_target_pairs={{0,4},{2,6},{4,0},{6,2},{8,12},{10,14},{12,8},{14,10},{16,20},{18,... | collective-permute-start | bytes 1769480 | tf_op jit(solution)/shard_map/ppermute | solution.py:293
  5.3 4.6 %collective-permute-start = (bf16[512,1536]{1,0:T(8,128)(2,1)S(1)}, bf16[512,1536]{1,0:T(8,128)(2,1)}, u32[]{:S(2)}, u32[]{:S(2)}) collective-permute-start(bf16[512,1536]{1,0:T(8,128)(2,1)S(1)} %constant_dynamic-update-slice_fusion.refs_3_), channel_id=1, source_target_pairs={{0,8},{2,10},{4,12},{6,14},{8,16},{10,18},{12,20},{14,22},{16,24},... | collective-permute-start | bytes 4718600 | tf_op jit(solution)/shard_map/ppermute | solution.py:293
  10.0 1.3 collective-permute-start.1
  11.3 7.6 %collective-permute-done.2 = bf16[192,1536]{1,0:T(8,128)(2,1)} collective-permute-done((bf16[192,1536]{1,0:T(8,128)(2,1)}, bf16[192,1536]{1,0:T(8,128)(2,1)}, u32[]{:S(2)}, u32[]{:S(2)}) %collective-permute-start.2) | collective-permute-done | bytes 589856 | tf_op jit(solution)/shard_map/ppermute | solution.py:293
  18.8 1.7 maximum_select_fusion.refs_0_
  20.5 0.1 collective-permute-start.3
  20.6 1.9 %collective-permute-start.4 = (bf16[512,1536]{1,0:T(8,128)(2,1)S(1)}, bf16[512,1536]{1,0:T(8,128)(2,1)}, u32[]{:S(2)}, u32[]{:S(2)}) collective-permute-start(bf16[512,1536]{1,0:T(8,128)(2,1)S(1)} %constant_dynamic-update-slice_fusion.refs_3_), channel_id=1, source_target_pairs={{2,4},{4,2},{10,12},{12,10},{18,20},{20,18},{26,28},{28,26},{3,5},... | collective-permute-start | bytes 4718600 | tf_op jit(solution)/shard_map/ppermute | solution.py:293
  22.5 1.2 constant_dynamic-slice_fusion.1
  23.7 1.8 %collective-permute-start.5 = (bf16[128,1536]{1,0:T(8,128)(2,1)S(1)}, bf16[128,1536]{1,0:T(8,128)(2,1)}, u32[]{:S(2)}, u32[]{:S(2)}) collective-permute-start(bf16[128,1536]{1,0:T(8,128)(2,1)S(1)} %get-tuple-element.44), channel_id=1, source_target_pairs={{0,1},{1,0},{2,3},{3,2},{4,5},{5,4},{6,7},{7,6},{8,9},{9,8},{10,11... | collective-permute-start | bytes 1179656 | tf_op jit(solution)/shard_map/ppermute | solution.py:307
  25.5 9.4 %collective-permute-done.5 = bf16[128,1536]{1,0:T(8,128)(2,1)} collective-permute-done((bf16[128,1536]{1,0:T(8,128)(2,1)S(1)}, bf16[128,1536]{1,0:T(8,128)(2,1)}, u32[]{:S(2)}, u32[]{:S(2)}) %collective-permute-start.5) | collective-permute-done | bytes 393248 | tf_op jit(solution)/shard_map/ppermute | solution.py:307
  34.9 2.2 %maximum_select_fusion.1.q_ref = bf16[256,1536]{1,0:T(8,128)(2,1)} fusion(bf16[128,1536]{1,0:T(8,128)(2,1)} %collective-permute-done.5, bf16[128,1536]{1,0:T(8,128)(2,1)S(1)} %get-tuple-element.43, pred[]{:T(512)S(6)} %eq.14), kind=kLoop, calls=%fused_computation.5 | loop fusion | flops 3538944 | bytes 1572865 | tf_op jit(solution)/shard_map/jit(_where)/select_n | solution.py:296
  37.1 5.1 %collective-permute-done = bf16[512,1536]{1,0:T(8,128)(2,1)} collective-permute-done((bf16[512,1536]{1,0:T(8,128)(2,1)S(1)}, bf16[512,1536]{1,0:T(8,128)(2,1)}, u32[]{:S(2)}, u32[]{:S(2)}) %collective-permute-start) | collective-permute-done | bytes 1572896 | tf_op jit(solution)/shard_map/ppermute | solution.py:293
  42.2 5.4 %collective-permute-done.1 = bf16[512,1536]{1,0:T(8,128)(2,1)} collective-permute-done((bf16[512,1536]{1,0:T(8,128)(2,1)S(1)}, bf16[512,1536]{1,0:T(8,128)(2,1)}, u32[]{:S(2)}, u32[]{:S(2)}) %collective-permute-start.1) | collective-permute-done | bytes 1572896 | tf_op jit(solution)/shard_map/ppermute | solution.py:293
  47.5 2.4 %collective-permute-start.19 = (bf16[384,1536]{1,0:T(8,128)(2,1)S(1)}, bf16[384,1536]{1,0:T(8,128)(2,1)S(1)}, u32[]{:S(2)}, u32[]{:S(2)}) collective-permute-start(bf16[384,1536]{1,0:T(8,128)(2,1)S(1)} %maximum_select_fusion.refs_0_), channel_id=1, source_target_pairs={{0,8},{2,10},{4,12},{6,14},{8,16},{10,18},{12,20},{14,22},{16,24},... | collective-permute-start | bytes 3538952 | tf_op jit(solution)/shard_map/ppermute | solution.py:293
  50.0 1.3 collective-permute-start.20
  51.3 1.3 slice.13
  52.6 1.3 slice.12
  53.9 1.5 pad_maximum_fusion.refs_0_.refs_6_
  55.4 2.0 %collective-permute-start.7 = (bf16[1024,1024]{1,0:T(8,128)(2,1)}, bf16[1024,1024]{1,0:T(8,128)(2,1)}, u32[]{:S(2)}, u32[]{:S(2)}) collective-permute-start(bf16[1024,1024]{1,0:T(8,128)(2,1)} %pad_maximum_fusion.refs_0_.refs_6_), channel_id=1, source_target_pairs={{2,4},{4,2},{10,12},{12,10},{18,20},{20,18},{26,28},{28,26},{3,5},... | collective-permute-start | bytes 6291464 | tf_op jit(solution)/shard_map/ppermute | solution.py:293
  57.4 1.1 slice.15
  58.5 1.1 slice.14
  59.6 1.1 pad_maximum_fusion.1.refs_0_.refs_6_
  60.6 0.5 collective-permute-start.14
  61.2 12.5 %collective-permute-done.19.refs_2_ = bf16[384,1536]{1,0:T(8,128)(2,1)S(1)} collective-permute-done((bf16[384,1536]{1,0:T(8,128)(2,1)S(1)}, bf16[384,1536]{1,0:T(8,128)(2,1)S(1)}, u32[]{:S(2)}, u32[]{:S(2)}) %collective-permute-start.19) | collective-permute-done | bytes 1179680 | tf_op jit(solution)/shard_map/ppermute | solution.py:293
  73.6 4.2 %collective-permute-done.20.refs_4_ = bf16[384,1536]{1,0:T(8,128)(2,1)S(1)} collective-permute-done((bf16[384,1536]{1,0:T(8,128)(2,1)S(1)}, bf16[384,1536]{1,0:T(8,128)(2,1)S(1)}, u32[]{:S(2)}, u32[]{:S(2)}) %collective-permute-start.20) | collective-permute-done | bytes 1179680 | tf_op jit(solution)/shard_map/ppermute | solution.py:293
  77.8 1.6 collective-permute-start.15
  79.5 4.3 %collective-permute-start.24 = (bf16[384,1536]{1,0:T(8,128)(2,1)S(1)}, bf16[384,1536]{1,0:T(8,128)(2,1)}, u32[]{:S(2)}, u32[]{:S(2)}) collective-permute-start(bf16[384,1536]{1,0:T(8,128)(2,1)S(1)} %maximum_select_fusion.refs_0_), channel_id=1, source_target_pairs={{0,16},{2,18},{4,20},{6,22},{24,8},{26,10},{28,12},{30,14},{1,17},... | collective-permute-start | bytes 3538952 | tf_op jit(solution)/shard_map/ppermute | solution.py:293
  83.8 0.1 broadcast_select_fusion.1
  83.9 1.3 collective-permute-start.26
  85.2 4.5 %collective-permute-start.28 = (bf16[384,1536]{1,0:T(8,128)(2,1)S(1)}, bf16[384,1536]{1,0:T(8,128)(2,1)}, u32[]{:S(2)}, u32[]{:S(2)}) collective-permute-start(bf16[384,1536]{1,0:T(8,128)(2,1)S(1)} %maximum_select_fusion.refs_0_), channel_id=1, source_target_pairs={{0,24},{2,26},{4,28},{6,30},{24,0},{26,2},{28,4},{30,6},{1,25},{3,... | collective-permute-start | bytes 3538952 | tf_op jit(solution)/shard_map/ppermute | solution.py:293
  89.8 0.6 pad_add_fusion.1.listed
  90.4 8.5 %shard_map.55.refs_0_ = bf16[256,512]{1,0:T(8,128)(2,1)} custom-call(s32[28]{0:T(128)} %pad_add_fusion.1.listed, bf16[256,1536]{1,0:T(8,128)(2,1)} %maximum_select_fusion.1.q_ref, bf16[1024,1024]{1,0:T(8,128)(2,1)} %pad_maximum_fusion.refs_0_.refs_6_, bf16[1024,1024]{1,0:T(8,128)(2,1)} %collective-permute-done.6.refs_1_.refs_7_, ...), custom_call_target="tpu_custom_call" | custom-call | flops 1 | bytes 1 | tf_op jit(solution)/shard_map/pallas_call | solution.py:163
  98.9 0.8 collective-permute-start.8
  99.7 1.5 collective-permute-start.9
  101.2 8.5 %shard_map.56.refs_4_ = bf16[256,512]{1,0:T(8,128)(2,1)} custom-call(s32[28]{0:T(128)} %pad_add_fusion.1.listed, bf16[256,1536]{1,0:T(8,128)(2,1)} %maximum_select_fusion.1.q_ref, bf16[1024,1024]{1,0:T(8,128)(2,1)} %pad_maximum_fusion.refs_0_.refs_6_, bf16[1024,1024]{1,0:T(8,128)(2,1)} %collective-permute-done.6.refs_1_.refs_7_, ...), custom_call_target="tpu_custom_call" | custom-call | flops 1 | bytes 1 | tf_op jit(solution)/shard_map/pallas_call | solution.py:163
  109.7 1.3 collective-permute-start.10
  111.0 0.7 collective-permute-start.11
  111.7 8.2 %collective-permute-done.10.refs_3_ = bf16[256,512]{1,0:T(8,128)(2,1)S(1)} collective-permute-done((bf16[256,512]{1,0:T(8,128)(2,1)S(1)}, bf16[256,512]{1,0:T(8,128)(2,1)S(1)}, u32[]{:S(2)}, u32[]{:S(2)}) %collective-permute-start.10) | collective-permute-done | bytes 262176 | tf_op jit(solution)/shard_map/ppermute | solution.py:346
  119.9 0.5 collective-permute-start.12
  120.4 2.5 %collective-permute-done.11.refs_5_ = bf16[256,512]{1,0:T(8,128)(2,1)S(1)} collective-permute-done((bf16[256,512]{1,0:T(8,128)(2,1)}, bf16[256,512]{1,0:T(8,128)(2,1)S(1)}, u32[]{:S(2)}, u32[]{:S(2)}) %collective-permute-start.11) | collective-permute-done | bytes 262176 | tf_op jit(solution)/shard_map/ppermute | solution.py:293
  122.9 2.6 %collective-permute-start.13 = (bf16[256,512]{1,0:T(8,128)(2,1)}, bf16[256,512]{1,0:T(8,128)(2,1)S(1)}, u32[]{:S(2)}, u32[]{:S(2)}) collective-permute-start(bf16[256,512]{1,0:T(8,128)(2,1)} %shard_map.56.refs_4_), channel_id=1, source_target_pairs={{0,5},{1,4},{2,7},{3,6},{4,1},{5,0},{6,3},{7,2},{8,13},{9,12},{10,... | collective-permute-start | bytes 786440 | tf_op jit(solution)/shard_map/ppermute | solution.py:346
  125.5 8.5 %shard_map.57.refs_8_ = bf16[256,512]{1,0:T(8,128)(2,1)} custom-call(s32[28]{0:T(128)} %pad_add_fusion.1.listed, bf16[256,1536]{1,0:T(8,128)(2,1)} %maximum_select_fusion.1.q_ref, bf16[1024,512]{1,0:T(8,128)(2,1)} %pad_maximum_fusion.1.refs_0_.refs_6_, bf16[1024,512]{1,0:T(8,128)(2,1)} %collective-permute-done.14.refs_1_.refs_7_, ...), custom_call_target="tpu_custom_call" | custom-call | flops 1 | bytes 1 | tf_op jit(solution)/shard_map/pallas_call | solution.py:163
  134.0 0.4 collective-permute-start.16
  134.5 0.5 collective-permute-start.17
  135.0 2.6 %collective-permute-start.18 = (bf16[256,512]{1,0:T(8,128)(2,1)}, bf16[256,512]{1,0:T(8,128)(2,1)}, u32[]{:S(2)}, u32[]{:S(2)}) collective-permute-start(bf16[256,512]{1,0:T(8,128)(2,1)} %shard_map.57.refs_8_), channel_id=1, source_target_pairs={{0,5},{1,4},{2,7},{3,6},{4,1},{5,0},{6,3},{7,2},{8,13},{9,12},{10,... | collective-permute-start | bytes 786440 | tf_op jit(solution)/shard_map/ppermute | solution.py:346
  137.6 2.0 %collective-permute-done.26.refs_8_ = bf16[384,1536]{1,0:T(8,128)(2,1)} collective-permute-done((bf16[384,1536]{1,0:T(8,128)(2,1)S(1)}, bf16[384,1536]{1,0:T(8,128)(2,1)}, u32[]{:S(2)}, u32[]{:S(2)}) %collective-permute-start.26) | collective-permute-done | bytes 1179680 | tf_op jit(solution)/shard_map/ppermute | solution.py:293
  139.6 0.5 collective-permute-start.23
  140.1 3.5 %collective-permute-done.16.refs_9_ = bf16[256,512]{1,0:T(8,128)(2,1)S(1)} collective-permute-done((bf16[256,512]{1,0:T(8,128)(2,1)}, bf16[256,512]{1,0:T(8,128)(2,1)S(1)}, u32[]{:S(2)}, u32[]{:S(2)}) %collective-permute-start.16) | collective-permute-done | bytes 262176 | tf_op jit(solution)/shard_map/ppermute | solution.py:293
  143.6 0.7 copy-done.11
  144.3 2.7 %collective-permute-done.17.refs_10_ = bf16[256,512]{1,0:T(8,128)(2,1)} collective-permute-done((bf16[256,512]{1,0:T(8,128)(2,1)}, bf16[256,512]{1,0:T(8,128)(2,1)}, u32[]{:S(2)}, u32[]{:S(2)}) %collective-permute-start.17) | collective-permute-done | bytes 262176 | tf_op jit(solution)/shard_map/ppermute | solution.py:345
  147.0 0.5 collective-permute-start.29
  147.5 0.6 pad_add_fusion.spot
  148.1 2.7 %shard_map.58.a_ref = bf16[512,3072]{1,0:T(8,128)(2,1)S(1)} custom-call(s32[4]{0:T(128)} %pad_add_fusion.spot, bf16[256,512]{1,0:T(8,128)(2,1)} %shard_map.55.refs_0_, bf16[256,512]{1,0:T(8,128)(2,1)} %copy-done.3, bf16[256,512]{1,0:T(8,128)(2,1)} %copy-done.6, bf16[256,512]{1,0:T(8,128)(2,1)} %copy-done.7, bf16[256,512]{1,0:T(8,128)(2,1)} %shard_map.56.refs_4_, ...), custom_call_target="tpu_custom_call" | custom-call | bytes 6291456 | tf_op jit(solution)/shard_map/pallas_call | solution.py:200
  150.9 1.0 collective-permute-done.29.refs_11_
  151.9 4.3 %shard_map.59 = (bf16[256,512]{1,0:T(8,128)(2,1)S(1)}, bf16[256,512]{1,0:T(8,128)(2,1)S(1)}) custom-call(s32[4]{0:T(128)S(1)} %copy-done, bf16[512,3072]{1,0:T(8,128)(2,1)S(1)} %shard_map.58.a_ref, bf16[384,1536]{1,0:T(8,128)(2,1)S(1)} %maximum_select_fusion.refs_0_, bf16[384,1536]{1,0:T(8,128)(2,1)} %collective-permute-done.21.refs_1_, ...), custom_call_target="tpu_custom_call" | custom-call | flops 1610612736 | bytes 6815744 | tf_op jit(solution)/shard_map/pallas_call | solution.py:260
  156.2 1.7 collective-permute-start.30
  157.9 4.3 %shard_map.60 = (bf16[256,512]{1,0:T(8,128)(2,1)S(1)}, bf16[256,512]{1,0:T(8,128)(2,1)S(1)}) custom-call(s32[4]{0:T(128)S(1)} %copy-done, bf16[512,3072]{1,0:T(8,128)(2,1)S(1)} %shard_map.58.a_ref, bf16[384,1536]{1,0:T(8,128)(2,1)S(1)} %maximum_select_fusion.refs_0_, bf16[384,1536]{1,0:T(8,128)(2,1)} %collective-permute-done.21.refs_1_, ...), custom_call_target="tpu_custom_call" | custom-call | flops 1610612736 | bytes 6815744 | tf_op jit(solution)/shard_map/pallas_call | solution.py:260
  162.3 0.4 collective-permute-start.31
  162.7 4.3 %shard_map.61 = (bf16[256,512]{1,0:T(8,128)(2,1)S(1)}, bf16[256,512]{1,0:T(8,128)(2,1)S(1)}) custom-call(s32[4]{0:T(128)S(1)} %copy-done, bf16[512,3072]{1,0:T(8,128)(2,1)S(1)} %shard_map.58.a_ref, bf16[384,1536]{1,0:T(8,128)(2,1)S(1)} %maximum_select_fusion.refs_0_, bf16[384,1536]{1,0:T(8,128)(2,1)} %collective-permute-done.21.refs_1_, ...), custom_call_target="tpu_custom_call" | custom-call | flops 1610612736 | bytes 6815744 | tf_op jit(solution)/shard_map/pallas_call | solution.py:260
  167.0 1.7 collective-permute-start.32
  168.8 2.8 %collective-permute-done.31 = bf16[256,512]{1,0:T(8,128)(2,1)S(1)} collective-permute-done((bf16[256,512]{1,0:T(8,128)(2,1)S(1)}, bf16[256,512]{1,0:T(8,128)(2,1)S(1)}, u32[]{:S(2)}, u32[]{:S(2)}) %collective-permute-start.31) | collective-permute-done | bytes 262176 | tf_op jit(solution)/shard_map/ppermute | solution.py:293
  171.5 4.5 %collective-permute-done.32 = bf16[256,512]{1,0:T(8,128)(2,1)S(1)} collective-permute-done((bf16[256,512]{1,0:T(8,128)(2,1)S(1)}, bf16[256,512]{1,0:T(8,128)(2,1)S(1)}, u32[]{:S(2)}, u32[]{:S(2)}) %collective-permute-start.32) | collective-permute-done | bytes 262176 | tf_op jit(solution)/shard_map/ppermute | solution.py:293
  176.3 1.3 broadcast_select_fusion
  (60 shorter events, 0.5 us)
Async XLA Ops:
  0.0 5.2 %copy-start.4 = (bf16[256,1536]{1,0:T(8,128)(2,1)S(1)}, bf16[256,1536]{1,0:T(8,128)(2,1)}, u32[]{:S(2)}) copy-start(bf16[256,1536]{1,0:T(8,128)(2,1)} %param.6) | copy-start | bytes 2359300
  0.0 5.3 %copy-start.5 = (bf16[256,1536]{1,0:T(8,128)(2,1)S(1)}, bf16[256,1536]{1,0:T(8,128)(2,1)}, u32[]{:S(2)}) copy-start(bf16[256,1536]{1,0:T(8,128)(2,1)} %param.7) | copy-start | bytes 2359300
  2.3 16.6 %collective-permute-start.2 = (bf16[192,1536]{1,0:T(8,128)(2,1)}, bf16[192,1536]{1,0:T(8,128)(2,1)}, u32[]{:S(2)}, u32[]{:S(2)}) collective-permute-start(bf16[192,1536]{1,0:T(8,128)(2,1)} %get-tuple-element.42), channel_id=1, source_target_pairs={{0,4},{2,6},{4,0},{6,2},{8,12},{10,14},{12,8},{14,10},{16,20},{18,... | collective-permute-start | bytes 1769480 | tf_op jit(solution)/shard_map/ppermute | solution.py:293
  5.3 18.3 %copy-start.1 = (bf16[512,1536]{1,0:T(8,128)(2,1)}, bf16[512,1536]{1,0:T(8,128)(2,1)S(1)}, u32[]{:S(2)}) copy-start(bf16[512,1536]{1,0:T(8,128)(2,1)S(1)} %constant_dynamic-update-slice_fusion.refs_3_) | copy-start | bytes 4718596
  5.3 36.8 %collective-permute-start = (bf16[512,1536]{1,0:T(8,128)(2,1)S(1)}, bf16[512,1536]{1,0:T(8,128)(2,1)}, u32[]{:S(2)}, u32[]{:S(2)}) collective-permute-start(bf16[512,1536]{1,0:T(8,128)(2,1)S(1)} %constant_dynamic-update-slice_fusion.refs_3_), channel_id=1, source_target_pairs={{0,8},{2,10},{4,12},{6,14},{8,16},{10,18},{12,20},{14,22},{16,24},... | collective-permute-start | bytes 4718600 | tf_op jit(solution)/shard_map/ppermute | solution.py:293
  10.0 37.6 %collective-permute-start.1 = (bf16[512,1536]{1,0:T(8,128)(2,1)S(1)}, bf16[512,1536]{1,0:T(8,128)(2,1)}, u32[]{:S(2)}, u32[]{:S(2)}) collective-permute-start(bf16[512,1536]{1,0:T(8,128)(2,1)S(1)} %constant_dynamic-update-slice_fusion.refs_3_), channel_id=1, source_target_pairs={{8,0},{10,2},{12,4},{14,6},{16,8},{18,10},{20,12},{22,14},{24,16},... | collective-permute-start | bytes 4718600 | tf_op jit(solution)/shard_map/ppermute | solution.py:293
  20.5 27.0 %collective-permute-start.3 = (bf16[512,1536]{1,0:T(8,128)(2,1)S(1)}, bf16[512,1536]{1,0:T(8,128)(2,1)}, u32[]{:S(2)}, u32[]{:S(2)}) collective-permute-start(bf16[512,1536]{1,0:T(8,128)(2,1)S(1)} %constant_dynamic-update-slice_fusion.refs_3_), channel_id=1, source_target_pairs={{0,2},{2,0},{4,6},{6,4},{8,10},{10,8},{12,14},{14,12},{16,18},{18,... | collective-permute-start | bytes 4718600 | tf_op jit(solution)/shard_map/ppermute | solution.py:293
  20.6 26.9 %collective-permute-start.4 = (bf16[512,1536]{1,0:T(8,128)(2,1)S(1)}, bf16[512,1536]{1,0:T(8,128)(2,1)}, u32[]{:S(2)}, u32[]{:S(2)}) collective-permute-start(bf16[512,1536]{1,0:T(8,128)(2,1)S(1)} %constant_dynamic-update-slice_fusion.refs_3_), channel_id=1, source_target_pairs={{2,4},{4,2},{10,12},{12,10},{18,20},{20,18},{26,28},{28,26},{3,5},... | collective-permute-start | bytes 4718600 | tf_op jit(solution)/shard_map/ppermute | solution.py:293
  23.7 11.2 %collective-permute-start.5 = (bf16[128,1536]{1,0:T(8,128)(2,1)S(1)}, bf16[128,1536]{1,0:T(8,128)(2,1)}, u32[]{:S(2)}, u32[]{:S(2)}) collective-permute-start(bf16[128,1536]{1,0:T(8,128)(2,1)S(1)} %get-tuple-element.44), channel_id=1, source_target_pairs={{0,1},{1,0},{2,3},{3,2},{4,5},{5,4},{6,7},{7,6},{8,9},{9,8},{10,11... | collective-permute-start | bytes 1179656 | tf_op jit(solution)/shard_map/ppermute | solution.py:307
  47.5 26.1 %collective-permute-start.19 = (bf16[384,1536]{1,0:T(8,128)(2,1)S(1)}, bf16[384,1536]{1,0:T(8,128)(2,1)S(1)}, u32[]{:S(2)}, u32[]{:S(2)}) collective-permute-start(bf16[384,1536]{1,0:T(8,128)(2,1)S(1)} %maximum_select_fusion.refs_0_), channel_id=1, source_target_pairs={{0,8},{2,10},{4,12},{6,14},{8,16},{10,18},{12,20},{14,22},{16,24},... | collective-permute-start | bytes 3538952 | tf_op jit(solution)/shard_map/ppermute | solution.py:293
  50.0 27.8 %collective-permute-start.20 = (bf16[384,1536]{1,0:T(8,128)(2,1)S(1)}, bf16[384,1536]{1,0:T(8,128)(2,1)S(1)}, u32[]{:S(2)}, u32[]{:S(2)}) collective-permute-start(bf16[384,1536]{1,0:T(8,128)(2,1)S(1)} %maximum_select_fusion.refs_0_), channel_id=1, source_target_pairs={{8,0},{10,2},{12,4},{14,6},{16,8},{18,10},{20,12},{22,14},{24,16},... | collective-permute-start | bytes 3538952 | tf_op jit(solution)/shard_map/ppermute | solution.py:293
  55.4 28.5 %collective-permute-start.6 = (bf16[1024,1024]{1,0:T(8,128)(2,1)}, bf16[1024,1024]{1,0:T(8,128)(2,1)}, u32[]{:S(2)}, u32[]{:S(2)}) collective-permute-start(bf16[1024,1024]{1,0:T(8,128)(2,1)} %pad_maximum_fusion.refs_0_.refs_6_), channel_id=1, source_target_pairs={{0,2},{2,0},{4,6},{6,4},{8,10},{10,8},{12,14},{14,12},{16,18},{18,... | collective-permute-start | bytes 6291464 | tf_op jit(solution)/shard_map/ppermute | solution.py:293
  55.4 29.8 %collective-permute-start.7 = (bf16[1024,1024]{1,0:T(8,128)(2,1)}, bf16[1024,1024]{1,0:T(8,128)(2,1)}, u32[]{:S(2)}, u32[]{:S(2)}) collective-permute-start(bf16[1024,1024]{1,0:T(8,128)(2,1)} %pad_maximum_fusion.refs_0_.refs_6_), channel_id=1, source_target_pairs={{2,4},{4,2},{10,12},{12,10},{18,20},{20,18},{26,28},{28,26},{3,5},... | collective-permute-start | bytes 6291464 | tf_op jit(solution)/shard_map/ppermute | solution.py:293
  60.6 18.8 %collective-permute-start.14 = (bf16[1024,512]{1,0:T(8,128)(2,1)}, bf16[1024,512]{1,0:T(8,128)(2,1)}, u32[]{:S(2)}, u32[]{:S(2)}) collective-permute-start(bf16[1024,512]{1,0:T(8,128)(2,1)} %pad_maximum_fusion.1.refs_0_.refs_6_), channel_id=1, source_target_pairs={{0,2},{2,0},{4,6},{6,4},{8,10},{10,8},{12,14},{14,12},{16,18},{18,... | collective-permute-start | bytes 3145736 | tf_op jit(solution)/shard_map/ppermute | solution.py:293
  73.6 26.1 %collective-permute-start.21 = (bf16[384,1536]{1,0:T(8,128)(2,1)S(1)}, bf16[384,1536]{1,0:T(8,128)(2,1)}, u32[]{:S(2)}, u32[]{:S(2)}) collective-permute-start(bf16[384,1536]{1,0:T(8,128)(2,1)S(1)} %maximum_select_fusion.refs_0_), channel_id=1, source_target_pairs={{0,2},{2,0},{4,6},{6,4},{8,10},{10,8},{12,14},{14,12},{16,18},{18,... | collective-permute-start | bytes 3538952 | tf_op jit(solution)/shard_map/ppermute | solution.py:293
  77.8 21.1 %collective-permute-start.15 = (bf16[1024,512]{1,0:T(8,128)(2,1)}, bf16[1024,512]{1,0:T(8,128)(2,1)}, u32[]{:S(2)}, u32[]{:S(2)}) collective-permute-start(bf16[1024,512]{1,0:T(8,128)(2,1)} %pad_maximum_fusion.1.refs_0_.refs_6_), channel_id=1, source_target_pairs={{2,4},{4,2},{10,12},{12,10},{18,20},{20,18},{26,28},{28,26},{3,5},... | collective-permute-start | bytes 3145736 | tf_op jit(solution)/shard_map/ppermute | solution.py:293
  79.5 10.3 %copy-start.12 = (s32[1,27]{1,0:T(1,128)S(1)}, s32[1,27]{1,0:T(1,128)}, u32[]{:S(2)}) copy-start(s32[1,27]{1,0:T(1,128)} %param.8) | copy-start | bytes 328
  79.5 55.5 %collective-permute-start.24 = (bf16[384,1536]{1,0:T(8,128)(2,1)S(1)}, bf16[384,1536]{1,0:T(8,128)(2,1)}, u32[]{:S(2)}, u32[]{:S(2)}) collective-permute-start(bf16[384,1536]{1,0:T(8,128)(2,1)S(1)} %maximum_select_fusion.refs_0_), channel_id=1, source_target_pairs={{0,16},{2,18},{4,20},{6,22},{24,8},{26,10},{28,12},{30,14},{1,17},... | collective-permute-start | bytes 3538952 | tf_op jit(solution)/shard_map/ppermute | solution.py:293
  83.9 55.7 %collective-permute-start.26 = (bf16[384,1536]{1,0:T(8,128)(2,1)S(1)}, bf16[384,1536]{1,0:T(8,128)(2,1)}, u32[]{:S(2)}, u32[]{:S(2)}) collective-permute-start(bf16[384,1536]{1,0:T(8,128)(2,1)S(1)} %broadcast_select_fusion.1), channel_id=1, source_target_pairs={{16,24},{18,26},{20,28},{22,30},{8,0},{10,2},{12,4},{14,6},{17,25}... | collective-permute-start | bytes 3538952 | tf_op jit(solution)/shard_map/ppermute | solution.py:293
  85.2 54.4 %collective-permute-start.28 = (bf16[384,1536]{1,0:T(8,128)(2,1)S(1)}, bf16[384,1536]{1,0:T(8,128)(2,1)}, u32[]{:S(2)}, u32[]{:S(2)}) collective-permute-start(bf16[384,1536]{1,0:T(8,128)(2,1)S(1)} %maximum_select_fusion.refs_0_), channel_id=1, source_target_pairs={{0,24},{2,26},{4,28},{6,30},{24,0},{26,2},{28,4},{30,6},{1,25},{3,... | collective-permute-start | bytes 3538952 | tf_op jit(solution)/shard_map/ppermute | solution.py:293
  98.9 10.8 %copy-start.2 = (bf16[256,512]{1,0:T(8,128)(2,1)S(1)}, bf16[256,512]{1,0:T(8,128)(2,1)}, u32[]{:S(2)}) copy-start(bf16[256,512]{1,0:T(8,128)(2,1)} %shard_map.55.refs_0_) | copy-start | bytes 786436
  98.9 10.8 %collective-permute-start.8 = (bf16[256,512]{1,0:T(8,128)(2,1)}, bf16[256,512]{1,0:T(8,128)(2,1)S(1)}, u32[]{:S(2)}, u32[]{:S(2)}) collective-permute-start(bf16[256,512]{1,0:T(8,128)(2,1)} %shard_map.55.refs_0_), channel_id=1, source_target_pairs={{0,4},{2,6},{4,0},{6,2},{8,12},{10,14},{12,8},{14,10},{16,20},{18,... | collective-permute-start | bytes 786440 | tf_op jit(solution)/shard_map/ppermute | solution.py:293
  99.7 11.4 %collective-permute-start.9 = (bf16[256,512]{1,0:T(8,128)(2,1)}, bf16[256,512]{1,0:T(8,128)(2,1)S(1)}, u32[]{:S(2)}, u32[]{:S(2)}) collective-permute-start(bf16[256,512]{1,0:T(8,128)(2,1)} %shard_map.55.refs_0_), channel_id=1, source_target_pairs={{0,1},{1,0},{2,3},{3,2},{4,5},{5,4},{6,7},{7,6},{8,9},{9,8},{10,11... | collective-permute-start | bytes 786440 | tf_op jit(solution)/shard_map/ppermute | solution.py:345
  109.7 15.8 %copy-start.3 = (bf16[256,512]{1,0:T(8,128)(2,1)}, bf16[256,512]{1,0:T(8,128)(2,1)S(1)}, u32[]{:S(2)}) copy-start(bf16[256,512]{1,0:T(8,128)(2,1)S(1)} %collective-permute-done.8.refs_9_.refs_1_) | copy-start | bytes 786436
  109.7 10.2 %collective-permute-start.10 = (bf16[256,512]{1,0:T(8,128)(2,1)S(1)}, bf16[256,512]{1,0:T(8,128)(2,1)S(1)}, u32[]{:S(2)}, u32[]{:S(2)}) collective-permute-start(bf16[256,512]{1,0:T(8,128)(2,1)S(1)} %copy-done.2), channel_id=1, source_target_pairs={{0,5},{1,4},{2,7},{3,6},{4,1},{5,0},{6,3},{7,2},{8,13},{9,12},{10,... | collective-permute-start | bytes 786440 | tf_op jit(solution)/shard_map/ppermute | solution.py:346
  111.0 23.0 %copy-start.6 = (bf16[256,512]{1,0:T(8,128)(2,1)}, bf16[256,512]{1,0:T(8,128)(2,1)S(1)}, u32[]{:S(2)}) copy-start(bf16[256,512]{1,0:T(8,128)(2,1)S(1)} %collective-permute-done.9.refs_2_) | copy-start | bytes 786436
  111.0 11.9 %collective-permute-start.11 = (bf16[256,512]{1,0:T(8,128)(2,1)}, bf16[256,512]{1,0:T(8,128)(2,1)S(1)}, u32[]{:S(2)}, u32[]{:S(2)}) collective-permute-start(bf16[256,512]{1,0:T(8,128)(2,1)} %shard_map.56.refs_4_), channel_id=1, source_target_pairs={{0,4},{2,6},{4,0},{6,2},{8,12},{10,14},{12,8},{14,10},{16,20},{18,... | collective-permute-start | bytes 786440 | tf_op jit(solution)/shard_map/ppermute | solution.py:293
  119.9 14.1 %copy-start.7 = (bf16[256,512]{1,0:T(8,128)(2,1)}, bf16[256,512]{1,0:T(8,128)(2,1)S(1)}, u32[]{:S(2)}) copy-start(bf16[256,512]{1,0:T(8,128)(2,1)S(1)} %collective-permute-done.10.refs_3_) | copy-start | bytes 786436
  119.9 14.1 %collective-permute-start.12 = (bf16[256,512]{1,0:T(8,128)(2,1)}, bf16[256,512]{1,0:T(8,128)(2,1)S(1)}, u32[]{:S(2)}, u32[]{:S(2)}) collective-permute-start(bf16[256,512]{1,0:T(8,128)(2,1)} %shard_map.56.refs_4_), channel_id=1, source_target_pairs={{0,1},{1,0},{2,3},{3,2},{4,5},{5,4},{6,7},{7,6},{8,9},{9,8},{10,11... | collective-permute-start | bytes 786440 | tf_op jit(solution)/shard_map/ppermute | solution.py:345
  122.9 11.1 %copy-start.8 = (bf16[256,512]{1,0:T(8,128)(2,1)}, bf16[256,512]{1,0:T(8,128)(2,1)S(1)}, u32[]{:S(2)}) copy-start(bf16[256,512]{1,0:T(8,128)(2,1)S(1)} %collective-permute-done.11.refs_5_) | copy-start | bytes 786436
  122.9 11.6 %collective-permute-start.13 = (bf16[256,512]{1,0:T(8,128)(2,1)}, bf16[256,512]{1,0:T(8,128)(2,1)S(1)}, u32[]{:S(2)}, u32[]{:S(2)}) collective-permute-start(bf16[256,512]{1,0:T(8,128)(2,1)} %shard_map.56.refs_4_), channel_id=1, source_target_pairs={{0,5},{1,4},{2,7},{3,6},{4,1},{5,0},{6,3},{7,2},{8,13},{9,12},{10,... | collective-permute-start | bytes 786440 | tf_op jit(solution)/shard_map/ppermute | solution.py:346
  134.0 5.6 %copy-start.9 = (bf16[256,512]{1,0:T(8,128)(2,1)}, bf16[256,512]{1,0:T(8,128)(2,1)S(1)}, u32[]{:S(2)}) copy-start(bf16[256,512]{1,0:T(8,128)(2,1)S(1)} %collective-permute-done.12.refs_6_) | copy-start | bytes 786436
  134.0 9.5 %collective-permute-start.16 = (bf16[256,512]{1,0:T(8,128)(2,1)}, bf16[256,512]{1,0:T(8,128)(2,1)S(1)}, u32[]{:S(2)}, u32[]{:S(2)}) collective-permute-start(bf16[256,512]{1,0:T(8,128)(2,1)} %shard_map.57.refs_8_), channel_id=1, source_target_pairs={{0,4},{2,6},{4,0},{6,2},{8,12},{10,14},{12,8},{14,10},{16,20},{18,... | collective-permute-start | bytes 786440 | tf_op jit(solution)/shard_map/ppermute | solution.py:293
  134.5 5.6 %copy-start.10 = (bf16[256,512]{1,0:T(8,128)(2,1)}, bf16[256,512]{1,0:T(8,128)(2,1)S(1)}, u32[]{:S(2)}) copy-start(bf16[256,512]{1,0:T(8,128)(2,1)S(1)} %collective-permute-done.13.refs_7_) | copy-start | bytes 786436
  134.5 12.5 %collective-permute-start.17 = (bf16[256,512]{1,0:T(8,128)(2,1)}, bf16[256,512]{1,0:T(8,128)(2,1)}, u32[]{:S(2)}, u32[]{:S(2)}) collective-permute-start(bf16[256,512]{1,0:T(8,128)(2,1)} %shard_map.57.refs_8_), channel_id=1, source_target_pairs={{0,1},{1,0},{2,3},{3,2},{4,5},{5,4},{6,7},{7,6},{8,9},{9,8},{10,11... | collective-permute-start | bytes 786440 | tf_op jit(solution)/shard_map/ppermute | solution.py:345
  135.0 12.0 %collective-permute-start.18 = (bf16[256,512]{1,0:T(8,128)(2,1)}, bf16[256,512]{1,0:T(8,128)(2,1)}, u32[]{:S(2)}, u32[]{:S(2)}) collective-permute-start(bf16[256,512]{1,0:T(8,128)(2,1)} %shard_map.57.refs_8_), channel_id=1, source_target_pairs={{0,5},{1,4},{2,7},{3,6},{4,1},{5,0},{6,3},{7,2},{8,13},{9,12},{10,... | collective-permute-start | bytes 786440 | tf_op jit(solution)/shard_map/ppermute | solution.py:346
  139.6 11.2 %collective-permute-start.22 = (bf16[384,1536]{1,0:T(8,128)(2,1)S(1)}, bf16[384,1536]{1,0:T(8,128)(2,1)}, u32[]{:S(2)}, u32[]{:S(2)}) collective-permute-start(bf16[384,1536]{1,0:T(8,128)(2,1)S(1)} %collective-permute-done.19.refs_2_), channel_id=1, source_target_pairs={{0,2},{2,0},{4,6},{6,4},{8,10},{10,8},{12,14},{14,12},{16,18},{18,... | collective-permute-start | bytes 3538952 | tf_op jit(solution)/shard_map/ppermute | solution.py:293
  139.6 11.2 %collective-permute-start.23 = (bf16[384,1536]{1,0:T(8,128)(2,1)S(1)}, bf16[384,1536]{1,0:T(8,128)(2,1)}, u32[]{:S(2)}, u32[]{:S(2)}) collective-permute-start(bf16[384,1536]{1,0:T(8,128)(2,1)S(1)} %collective-permute-done.20.refs_4_), channel_id=1, source_target_pairs={{0,2},{2,0},{4,6},{6,4},{8,10},{10,8},{12,14},{14,12},{16,18},{18,... | collective-permute-start | bytes 3538952 | tf_op jit(solution)/shard_map/ppermute | solution.py:293
  143.6 0.7 copy-start.11
  144.3 6.6 %collective-permute-start.25 = (bf16[384,1536]{1,0:T(8,128)(2,1)}, bf16[384,1536]{1,0:T(8,128)(2,1)}, u32[]{:S(2)}, u32[]{:S(2)}) collective-permute-start(bf16[384,1536]{1,0:T(8,128)(2,1)} %collective-permute-done.24.refs_6_), channel_id=1, source_target_pairs={{0,2},{2,0},{4,6},{6,4},{8,10},{10,8},{12,14},{14,12},{16,18},{18,... | collective-permute-start | bytes 3538952 | tf_op jit(solution)/shard_map/ppermute | solution.py:293
  147.0 3.9 %collective-permute-start.27 = (bf16[384,1536]{1,0:T(8,128)(2,1)}, bf16[384,1536]{1,0:T(8,128)(2,1)}, u32[]{:S(2)}, u32[]{:S(2)}) collective-permute-start(bf16[384,1536]{1,0:T(8,128)(2,1)} %collective-permute-done.26.refs_8_), channel_id=1, source_target_pairs={{0,2},{2,0},{4,6},{6,4},{8,10},{10,8},{12,14},{14,12},{16,18},{18,... | collective-permute-start | bytes 3538952 | tf_op jit(solution)/shard_map/ppermute | solution.py:293
  147.0 4.9 %collective-permute-start.29 = (bf16[384,1536]{1,0:T(8,128)(2,1)}, bf16[384,1536]{1,0:T(8,128)(2,1)}, u32[]{:S(2)}, u32[]{:S(2)}) collective-permute-start(bf16[384,1536]{1,0:T(8,128)(2,1)} %collective-permute-done.28.refs_10_), channel_id=1, source_target_pairs={{0,2},{2,0},{4,6},{6,4},{8,10},{10,8},{12,14},{14,12},{16,18},{18,... | collective-permute-start | bytes 3538952 | tf_op jit(solution)/shard_map/ppermute | solution.py:293
  148.1 3.8 %copy-start = (s32[4]{0:T(128)S(1)}, s32[4]{0:T(128)}, u32[]{:S(2)}) copy-start(s32[4]{0:T(128)} %pad_add_fusion.spot) | copy-start | bytes 52
  156.2 12.5 %collective-permute-start.30 = (bf16[256,512]{1,0:T(8,128)(2,1)S(1)}, bf16[256,512]{1,0:T(8,128)(2,1)S(1)}, u32[]{:S(2)}, u32[]{:S(2)}) collective-permute-start(bf16[256,512]{1,0:T(8,128)(2,1)S(1)} %get-tuple-element.38), channel_id=1, source_target_pairs={{0,4},{2,6},{4,0},{6,2},{8,12},{10,14},{12,8},{14,10},{16,20},{18,... | collective-permute-start | bytes 786440 | tf_op jit(solution)/shard_map/ppermute | solution.py:293
  162.3 9.3 %collective-permute-start.31 = (bf16[256,512]{1,0:T(8,128)(2,1)S(1)}, bf16[256,512]{1,0:T(8,128)(2,1)S(1)}, u32[]{:S(2)}, u32[]{:S(2)}) collective-permute-start(bf16[256,512]{1,0:T(8,128)(2,1)S(1)} %get-tuple-element.39), channel_id=1, source_target_pairs={{0,4},{2,6},{4,0},{6,2},{8,12},{10,14},{12,8},{14,10},{16,20},{18,... | collective-permute-start | bytes 786440 | tf_op jit(solution)/shard_map/ppermute | solution.py:293
  167.0 9.0 %collective-permute-start.32 = (bf16[256,512]{1,0:T(8,128)(2,1)S(1)}, bf16[256,512]{1,0:T(8,128)(2,1)S(1)}, u32[]{:S(2)}, u32[]{:S(2)}) collective-permute-start(bf16[256,512]{1,0:T(8,128)(2,1)S(1)} %get-tuple-element.40), channel_id=1, source_target_pairs={{0,4},{2,6},{4,0},{6,2},{8,12},{10,14},{12,8},{14,10},{16,20},{18,... | collective-permute-start | bytes 786440 | tf_op jit(solution)/shard_map/ppermute | solution.py:293
